TPU v7x, 128 devices: a whole 4x4x4 slice. The times are simulated.
128 devices in a mesh: rows: 128 (over y, x, z, core).
Axes of the slice: x: 4, y: 4, z: 4, core: 2. Of those that a mesh axis runs over, the one named last changes fastest.
Arguments:
- vectors: float32 [262144, 128], P('rows'), may hold values from -6.05 to 6.05
- hblocks: float32 [2048, 20, 128, 128], P('rows'), may hold values from -1 to 1
- local_cols: int32 [2048, 20], P('rows'), may hold values from 0 to 47, as said below
- ghost_lists: int32 [128, 4, 8], replicated, may hold values from 0 to 15, as said below
Outputs:
- basis: float32 [262144, 128], P('rows')
- factor: float32 [128, 128], replicated
Inputs may be any that keep to these rules, and one draw needn't show every extreme that they name: `ghost_lists`: each list names 8 different blocks of the sending device. `local_cols`: each block row names 20 different slots.
All inputs are finite; a program needn't handle non-finite values.
Results may differ from a plain program's by a relative error of at most 0.0003.
Values sent between devices are 32-bit elements; how exact they have to be, the bound alone decides.
No kernel may reach another device: no remote copies, remote signals or barrier semaphores. Data moves between devices by JAX's collectives and lax.ppermute only.
A program may use at most 128 MiB of HBM per device.

v0:
```python
import jax
import jax.numpy as jnp
from jax import lax
from jax.sharding import PartitionSpec as P

BS = 128
REACH = 2


def from_behind(shard, axis, by):
    count = lax.axis_size(axis)
    return lax.ppermute(shard, axis, [(i, (i + by) % count) for i in range(count)])


def fetch_whole(payload, by):
    return from_behind(payload, "rows", by)


def lower_cholesky(gram):
    size = gram.shape[0]
    index_all = jnp.arange(size, dtype=jnp.int32)

    def column_step(j, lower):
        row_j = lax.dynamic_index_in_dim(lower, j, 0, keepdims=False)
        col_a = lax.dynamic_index_in_dim(gram, j, 1, keepdims=False)
        rest = col_a - jnp.dot(lower, row_j, precision=lax.Precision.HIGHEST)
        pivot = jnp.sqrt(lax.dynamic_index_in_dim(rest, j, 0, keepdims=False))
        column = jnp.where(index_all > j, rest / pivot, jnp.where(index_all == j, pivot, 0.0))
        return lower + column[:, None] * (index_all[None, :] == j).astype(gram.dtype)

    return lax.fori_loop(0, size, column_step, jnp.zeros_like(gram))


def upper_inverse(upper):
    size = upper.shape[0]
    eye = jnp.eye(size, dtype=upper.dtype)

    def row_step(t, inverse):
        i = size - 1 - t
        row_u = lax.dynamic_index_in_dim(upper, i, 0, keepdims=False)
        diag = lax.dynamic_index_in_dim(row_u, i, 0, keepdims=False)
        row_e = lax.dynamic_index_in_dim(eye, i, 0, keepdims=False)
        new_row = (row_e - jnp.dot(row_u, inverse, precision=lax.Precision.HIGHEST)) / diag
        return lax.dynamic_update_index_in_dim(inverse, new_row, i, 0)

    return lax.fori_loop(0, size, row_step, jnp.zeros_like(upper))


def shards(vectors, hblocks, local_cols, ghost_lists):
    count = lax.axis_size("rows")
    me = lax.axis_index("rows")
    rows_dev = vectors.shape[0]
    width = vectors.shape[1]
    nblk = rows_dev // BS
    total = rows_dev * count
    offsets = [o for o in range(-REACH, REACH + 1) if o != 0]
    highest = lax.Precision.HIGHEST

    def extend(blocks):
        parts = [blocks]
        for k, off in enumerate(offsets):
            source = (me + off) % count
            theirs = lax.dynamic_index_in_dim(ghost_lists, source, 0, keepdims=False)[k]
            parts.append(fetch_whole(blocks, -off)[theirs])
        return jnp.concatenate(parts, axis=0)

    def apply_ham(field):
        blocks = field.reshape(nblk, BS, width)
        extended = extend(blocks)
        picked = extended[local_cols]
        result = jnp.einsum("rnij,rnjk->rik", hblocks, picked, precision=highest)
        return result.reshape(rows_dev, width)

    def upper_factor(mat):
        local_gram = jnp.dot(mat.T, mat, precision=highest)
        gram = lax.psum(local_gram, "rows") / total
        return lower_cholesky(gram).T

    first = apply_ham(vectors) - 0.5 * vectors
    second = 2.0 * (apply_ham(first) - 0.5 * first) - vectors
    upper_one = upper_factor(second)
    middle = jnp.dot(second, upper_inverse(upper_one), precision=highest)
    upper_two = upper_factor(middle)
    basis = jnp.dot(middle, upper_inverse(upper_two), precision=highest)
    factor = jnp.dot(upper_two, upper_one, precision=highest)
    return (basis, factor)


def solution(mesh):
    in_specs = (P("rows", None), P("rows", None, None, None), P("rows", None), P())
    out_specs = (P("rows", None), P())
    return jax.shard_map(shards, mesh=mesh, in_specs=in_specs, out_specs=out_specs, check_vma=False)
```

profile of v0, /device:TPU:0, one launch (start us, length us, event | category | flops | bytes accessed | tf_op | source)
XLA Modules:
  0.0 1252.6 jit_solution(7589000532860210193)
XLA Ops:
  9.3 7.2 collective-permute-start.2
  21.0 19.3 %collective-permute-done = f32[16,128,128]{2,1,0:T(8,128)} collective-permute-done((f32[16,128,128]{2,1,0:T(8,128)}, f32[16,128,128]{2,1,0:T(8,128)}, u32[]{:S(2)}, u32[]{:S(2)}) %collective-permute-start) | collective-permute-done | bytes 1048608 | tf_op jit(solution)/shard_map/ppermute | solution.py:12
  40.3 2.6 gather_fusion
  42.9 7.8 collective-permute-done.1
  50.8 2.6 gather_fusion.1
  53.4 2.6 gather_fusion.2
  59.2 2.6 gather_fusion.3
  62.9 8.6 gather_fusion.4
  71.5 26.8 %fusion.31 = f32[16,128,128,1]{1,2,3,0:T(8,128)S(1)} fusion(f32[16,20,128,128]{3,2,1,0:T(8,128)} %bitcast.161, f32[16,20,128,128]{3,2,1,0:T(8,128)} %param.13), kind=kOutput, calls=%fused_computation.82 | convolution fusion | flops 8053063680 | bytes 42991616 | tf_op jit(solution)/shard_map/rnij,rnjk->rik/dot_general | solution.py:71
  99.5 7.2 collective-permute-start.6
  110.1 21.3 %collective-permute-done.4 = f32[16,128,128]{2,1,0:T(8,128)} collective-permute-done((f32[16,128,128]{2,1,0:T(8,128)}, f32[16,128,128]{2,1,0:T(8,128)}, u32[]{:S(2)}, u32[]{:S(2)}) %collective-permute-start.4) | collective-permute-done | bytes 1048608 | tf_op jit(solution)/shard_map/ppermute | solution.py:12
  131.4 2.6 gather_fusion.5
  134.2 2.6 gather_fusion.6
  136.8 2.6 gather_fusion.7
  142.7 2.6 gather_fusion.8
  146.3 8.6 gather_fusion.9
  155.0 26.9 %fusion.32 = f32[16,128,128,1]{1,2,3,0:T(8,128)S(1)} fusion(f32[16,20,128,128]{3,2,1,0:T(8,128)} %bitcast.160, f32[16,20,128,128]{3,2,1,0:T(8,128)} %param.13), kind=kOutput, calls=%fused_computation.83 | convolution fusion | flops 8053063680 | bytes 42991616 | tf_op jit(solution)/shard_map/rnij,rnjk->rik/dot_general | solution.py:71
  184.9 135.3 %all-reduce.3.cloned.1.call-done = f32[128,128]{1,0:T(8,128)} async-done(((f32[128,128]{1,0:T(8,128)}), f32[128,128]{1,0:T(8,128)}) %all-reduce.3.cloned.1.call-update) | async-done | bytes 65552 | tf_op jit(solution)/shard_map/psum | solution.py:76
  321.1 211.9 %while.64 = (s32[]{:T(128)}, f32[128,128]{1,0:T(8,128)S(1)}, f32[128,128]{0,1:T(8,128)S(1)}, s32[]{:T(128)}, s32[]{:T(128)}) while((s32[]{:T(128)}, f32[128,128]{1,0:T(8,128)S(1)}, f32[128,128]{0,1:T(8,128)S(1)}, s32[]{:T(128)}, s32[]{:T(128)}) %tuple.144), condition=%wide.region_2.3_spmd.clone.clone, body=%wide.region_1.2_spmd.clone.clone.sunk | while | flops 263171 | bytes 332904 | solution.py:31
  533.2 185.2 %while.62 = (s32[]{:T(128)}, f32[128,128]{1,0:T(8,128)S(1)}, f32[128,128]{1,0:T(8,128)S(1)}, f32[128,128]{1,0:T(8,128)S(1)}, s32[]{:T(128)}, /*index=5*/s32[]{:T(128)}, s32[]{:T(128)}, s32[]{:T(128)}) while((s32[]{:T(128)}, f32[128,128]{1,0:T(8,128)S(1)}, f32[128,128]{1,0:T(8,128)S(1)}, f32[128,128]{1,0:T(8,128)S(1)}, s32[]{:T(128)}, ...), condition=%wide.region_4.5_spmd, body=%wide.region_3.4_spmd.sunk | while | flops 196871 | bytes 69287 | solution.py:46
  719.4 2.5 fusion.35
  721.8 134.8 %all-reduce.5.cloned.1.call-done = f32[128,128]{1,0:T(8,128)} async-done(((f32[128,128]{1,0:T(8,128)}), f32[128,128]{1,0:T(8,128)}) %all-reduce.5.cloned.1.call-update) | async-done | bytes 65552 | tf_op jit(solution)/shard_map/psum | solution.py:76
  857.6 211.9 %while.65 = (s32[]{:T(128)}, f32[128,128]{1,0:T(8,128)S(1)}, f32[128,128]{0,1:T(8,128)S(1)}, s32[]{:T(128)}, s32[]{:T(128)}) while((s32[]{:T(128)}, f32[128,128]{1,0:T(8,128)S(1)}, f32[128,128]{0,1:T(8,128)S(1)}, s32[]{:T(128)}, s32[]{:T(128)}) %tuple.150), condition=%wide.region_7.8_spmd.clone.clone, body=%wide.region_6.7_spmd.clone.clone.sunk | while | flops 263171 | bytes 332904 | solution.py:31
  1070.6 173.2 %while.63 = (s32[]{:T(128)}, f32[128,128]{1,0:T(8,128)S(1)}, f32[128,128]{1,0:T(8,128)S(1)}, f32[128,128]{1,0:T(8,128)S(1)}, s32[]{:T(128)}, /*index=5*/s32[]{:T(128)}, s32[]{:T(128)}, s32[]{:T(128)}) while((s32[]{:T(128)}, f32[128,128]{1,0:T(8,128)S(1)}, f32[128,128]{1,0:T(8,128)S(1)}, f32[128,128]{1,0:T(8,128)S(1)}, s32[]{:T(128)}, ...), condition=%wide.region_9.10_spmd, body=%wide.region_8.9_spmd.sunk | while | flops 196871 | bytes 69287 | solution.py:46
  (2366 shorter events, 613.4 us)
Async XLA Ops:
  7.2 313.0 %all-reduce.3.cloned.1.call-start = ((), (), s32[]{:S(2)}) async-start(), calls=%async_computation | async-start | bytes 131072 | tf_op jit(solution)/shard_map/psum | solution.py:76
  7.2 33.1 %collective-permute-start = (f32[16,128,128]{2,1,0:T(8,128)}, f32[16,128,128]{2,1,0:T(8,128)}, u32[]{:S(2)}, u32[]{:S(2)}) collective-permute-start(f32[16,128,128]{2,1,0:T(8,128)} %bitcast.164), channel_id=1, source_target_pairs={{0,2},{1,3},{2,4},{3,5},{4,6},{5,7},{6,8},{7,9},{8,10},{9,11},{10,... | collective-permute-start | bytes 3145736 | tf_op jit(solution)/shard_map/ppermute | solution.py:12
  9.3 41.5 %collective-permute-start.1 = (f32[16,128,128]{2,1,0:T(8,128)}, f32[16,128,128]{2,1,0:T(8,128)}, u32[]{:S(2)}, u32[]{:S(2)}) collective-permute-start(f32[16,128,128]{2,1,0:T(8,128)} %bitcast.165), channel_id=1, source_target_pairs={{0,1},{1,2},{2,3},{3,4},{4,5},{5,6},{6,7},{7,8},{8,9},{9,10},{10,1... | collective-permute-start | bytes 3145736 | tf_op jit(solution)/shard_map/ppermute | solution.py:12
  9.3 44.1 %collective-permute-start.2 = (f32[16,128,128]{2,1,0:T(8,128)}, f32[16,128,128]{2,1,0:T(8,128)}, u32[]{:S(2)}, u32[]{:S(2)}) collective-permute-start(f32[16,128,128]{2,1,0:T(8,128)} %bitcast.166), channel_id=1, source_target_pairs={{0,127},{1,0},{2,1},{3,2},{4,3},{5,4},{6,5},{7,6},{8,7},{9,8},{10,... | collective-permute-start | bytes 3145736 | tf_op jit(solution)/shard_map/ppermute | solution.py:12
  16.5 42.7 %collective-permute-start.3 = (f32[16,128,128]{2,1,0:T(8,128)}, f32[16,128,128]{2,1,0:T(8,128)}, u32[]{:S(2)}, u32[]{:S(2)}) collective-permute-start(f32[16,128,128]{2,1,0:T(8,128)} %bitcast.167), channel_id=1, source_target_pairs={{0,126},{1,127},{2,0},{3,1},{4,2},{5,3},{6,4},{7,5},{8,6},{9,7},{1... | collective-permute-start | bytes 3145736 | tf_op jit(solution)/shard_map/ppermute | solution.py:12
  71.5 26.8 %copy-start.2 = (f32[2048,128]{1,0:T(8,128)S(1)}, f32[2048,128]{1,0:T(8,128)}, u32[]{:S(2)}) copy-start(f32[2048,128]{1,0:T(8,128)} %param.12) | copy-start | bytes 3145732
  98.3 8.4 copy-start
  99.5 31.8 %collective-permute-start.4 = (f32[16,128,128]{2,1,0:T(8,128)}, f32[16,128,128]{2,1,0:T(8,128)}, u32[]{:S(2)}, u32[]{:S(2)}) collective-permute-start(f32[16,128,128]{2,1,0:T(8,128)} %bitcast.22), channel_id=1, source_target_pairs={{0,2},{1,3},{2,4},{3,5},{4,6},{5,7},{6,8},{7,9},{8,10},{9,11},{10,... | collective-permute-start | bytes 3145736 | tf_op jit(solution)/shard_map/ppermute | solution.py:12
  99.5 34.6 %collective-permute-start.5 = (f32[16,128,128]{2,1,0:T(8,128)}, f32[16,128,128]{2,1,0:T(8,128)}, u32[]{:S(2)}, u32[]{:S(2)}) collective-permute-start(f32[16,128,128]{2,1,0:T(8,128)} %bitcast.22), channel_id=1, source_target_pairs={{0,1},{1,2},{2,3},{3,4},{4,5},{5,6},{6,7},{7,8},{8,9},{9,10},{10,1... | collective-permute-start | bytes 3145736 | tf_op jit(solution)/shard_map/ppermute | solution.py:12
  99.5 37.2 %collective-permute-start.6 = (f32[16,128,128]{2,1,0:T(8,128)}, f32[16,128,128]{2,1,0:T(8,128)}, u32[]{:S(2)}, u32[]{:S(2)}) collective-permute-start(f32[16,128,128]{2,1,0:T(8,128)} %bitcast.22), channel_id=1, source_target_pairs={{0,127},{1,0},{2,1},{3,2},{4,3},{5,4},{6,5},{7,6},{8,7},{9,8},{10,... | collective-permute-start | bytes 3145736 | tf_op jit(solution)/shard_map/ppermute | solution.py:12
  106.8 35.9 %collective-permute-start.7 = (f32[16,128,128]{2,1,0:T(8,128)}, f32[16,128,128]{2,1,0:T(8,128)}, u32[]{:S(2)}, u32[]{:S(2)}) collective-permute-start(f32[16,128,128]{2,1,0:T(8,128)} %bitcast.22), channel_id=1, source_target_pairs={{0,126},{1,127},{2,0},{3,1},{4,2},{5,3},{6,4},{7,5},{8,6},{9,7},{1... | collective-permute-start | bytes 3145736 | tf_op jit(solution)/shard_map/ppermute | solution.py:12
  155.0 26.9 %copy-start.1 = (f32[16,128,128,1]{1,2,3,0:T(8,128)S(1)}, f32[16,128,128,1]{1,2,3,0:T(8,128)}, u32[]{:S(2)}) copy-start(f32[16,128,128,1]{1,2,3,0:T(8,128)} %copy-done) | copy-start | bytes 3145732
  155.0 26.9 %copy-start.3 = (f32[2048,128]{1,0:T(8,128)S(1)}, f32[2048,128]{1,0:T(8,128)}, u32[]{:S(2)}) copy-start(f32[2048,128]{1,0:T(8,128)} %param.12) | copy-start | bytes 3145732
  184.6 672.1 %all-reduce.5.cloned.1.call-start = ((), (), s32[]{:S(2)}) async-start(), calls=%async_computation.1 | async-start | bytes 131072 | tf_op jit(solution)/shard_map/psum | solution.py:76
Sparse Core Ops, SparseCore 0:
  184.7 135.4 all-reduce.2
  722.0 134.6 all-reduce.4
where the time goes:
time: 1260 us; the launch traced here: 1250 us
  local copies, waits for them, and re-layouts  371 us (29%)
  waiting for transfers between devices  319 us (25%)
  matrix products  300 us (24%)
  loops' own time  198 us (16%)
  other arithmetic  30.3 us (2%)
  starting transfers between devices  20.2 us (2%)
  between operations  14.4 us (1%)
    psum x2, waiting for transfers between devices, upper_factor(): gram = lax.psum(local_gram, 'rows') / total  270 us
    dot_general x256, matrix products, row_step(): jnp.dot(row_u, inverse, precision=lax.Precision.HIGHEST)  193 us
    another operation x2, loops' own time, lower_cholesky(): return lax.fori_loop(0, size, column_step, jnp.zeros_like(gram))  190 us
    dynamic_slice x256, local copies, waits for them, and re-layouts, column_step(): pivot = jnp.sqrt(lax.dynamic_index_in_dim(rest, j, 0, keepdims=False))  163 us
    dynamic_slice x256, local copies, waits for them, and re-layouts, row_step(): diag = lax.dynamic_index_in_dim(row_u, i, 0, keepdims=False)  150 us
    dot_general x2, matrix products, apply_ham(): result = jnp.einsum('rnij,rnjk->rik', hblocks, picked, precision=highest)  53.7 us
    ppermute x8, waiting for transfers between devices, from_behind(): lax.ppermute(shard, axis, [(i, (i + by) % count) for i in range(count)])  48.6 us
    dot_general x256, matrix products, column_step(): rest = col_a - jnp.dot(lower, row_j, precision=lax.Precision.HIGHEST)  44.7 us
  transfers between devices with their start and end apart: 10, of which 6 were waited for; matrix products, arithmetic and copies ran while one was open for 2% of the time, Pallas kernels for 0%

commit v1 on v0

v1 whole, which is shorter than its diff:
```python
import functools

import jax
import jax.numpy as jnp
from jax import lax
from jax.experimental import pallas as pl
from jax.experimental.pallas import tpu as pltpu
from jax.sharding import PartitionSpec as P

BS = 128
W = 128
RB = 16
GHOST = 8
NNZB = 20
NE = RB * NNZB
SPLIT = 3
VZERO = 48
MAXE = NE + 48
FIRST_VSLOT = (0, 24, 40)
GROUP = 8
VMEM_LIMIT = 28 * 1024 * 1024
F32 = jnp.float32
BF16 = jnp.bfloat16
HIGHEST = lax.Precision.HIGHEST

ANY = pl.BlockSpec(memory_space=pl.ANY)
VM = pl.BlockSpec(memory_space=pltpu.VMEM)
SM = pl.BlockSpec(memory_space=pltpu.SMEM)


def on_chip(x):
    return pltpu.with_memory_space_constraint(x, pltpu.VMEM)


def pieces(x):
    out = []
    for _ in range(SPLIT - 1):
        part = x.astype(BF16)
        out.append(part)
        x = x - part.astype(F32)
    out.append(x.astype(BF16))
    return out


def convert_kernel(cols_ref, base_ref, h_ref, hs_ref, list_ref, cnt_ref):
    r = pl.program_id(0)

    @pl.when(r == 0)
    def _():
        for p in range(3):
            cnt_ref[p] = 0

    for n in range(NNZB):
        hi, mid, lo = pieces(h_ref[0, n])
        e = r * NNZB + n
        hs_ref[e, 0:BS, :] = hi
        hs_ref[e, BS : 2 * BS, :] = mid
        hs_ref[e, 2 * BS : 3 * BS, :] = lo
        slot = cols_ref[r, n]
        kind = jnp.where(slot < RB, 0, 1 + lax.shift_right_logical(slot - RB, 3))
        v = slot + base_ref[kind]
        phase = (v >= FIRST_VSLOT[1]).astype(jnp.int32) + (v >= FIRST_VSLOT[2]).astype(jnp.int32)
        at = cnt_ref[phase]
        list_ref[phase, at] = r * 65536 + e * 64 + v
        cnt_ref[phase] = at + 1
    for p in range(3):
        at = cnt_ref[p]
        list_ref[p, at] = r * 65536 + VZERO
        cnt_ref[p] = at + (at & 1)

    @pl.when(r == RB - 1)
    def _():
        for p in range(3):
            at = cnt_ref[p]
            for i in range(2 * GROUP):
                list_ref[p, at + i] = VZERO


def convert(hblocks, local_cols, base):
    return pl.pallas_call(
        convert_kernel,
        grid=(RB,),
        in_specs=[SM, SM, pl.BlockSpec((1, NNZB, BS, BS), lambda r: (r, 0, 0, 0))],
        out_specs=[VM, SM, SM],
        out_shape=[
            pltpu.VMEM((NE, SPLIT * BS, BS), BF16),
            jax.ShapeDtypeStruct((3, MAXE), jnp.int32),
            jax.ShapeDtypeStruct((3,), jnp.int32),
        ],
        compiler_params=pltpu.CompilerParams(vmem_limit_bytes=VMEM_LIMIT),
        cost_estimate=pl.CostEstimate(flops=NE * BS * BS * 8, bytes_accessed=NE * BS * BS * 4, transcendentals=0),
        name="convert",
    )(local_cols, base, hblocks)


def pack_kernel(sel_ref, blocks_ref, *outs):
    for t in range(4):
        for g in range(GHOST):
            outs[t][g] = blocks_ref[sel_ref[t, g]]


def pack(sel, blocks):
    return pl.pallas_call(
        pack_kernel,
        in_specs=[SM, VM],
        out_specs=[VM] * 4,
        out_shape=[jax.ShapeDtypeStruct((GHOST, BS, W), F32)] * 4,
        name="pack",
    )(sel, blocks)


def load_table(v12_ref, v3_ref, at, block):
    hi, mid, lo = pieces(block)
    v12_ref[at, :, 0:W] = hi
    v12_ref[at, :, W : 2 * W] = mid
    v3_ref[at] = lo


def products(phase, list_ref, cnt_ref, hs_ref, v12_ref, v3_ref, acc_ref):
    def step(g, carry):
        for i in range(GROUP):
            one = list_ref[phase, g * (2 * GROUP) + 2 * i]
            two = list_ref[phase, g * (2 * GROUP) + 2 * i + 1]
            row = lax.shift_right_logical(one, 16)
            e1 = lax.shift_right_logical(one, 6) & 1023
            e2 = lax.shift_right_logical(two, 6) & 1023
            s1 = one & 63
            s2 = two & 63
            lhs = jnp.concatenate([hs_ref[e1], hs_ref[e2]], axis=1)
            rhs = jnp.concatenate([v12_ref[s1], v12_ref[s2]], axis=0)
            low = jnp.concatenate([v3_ref[s1], v3_ref[s2]], axis=0)
            big = jnp.dot(lhs, rhs, preferred_element_type=F32)
            small = jnp.dot(lhs[0:BS], low, preferred_element_type=F32)
            total = big[0:BS, 0:W] + (
                (big[0:BS, W:] + big[BS : 2 * BS, 0:W]) + (big[BS : 2 * BS, W:] + big[2 * BS :, 0:W] + small)
            )
            acc_ref[row] = acc_ref[row] + total
        return carry

    count = cnt_ref[phase]
    steps = lax.shift_right_logical(count + (2 * GROUP - 1), 4)
    lax.fori_loop(0, steps, step, 0)


def phase_kernel(phase, nbufs, list_ref, cnt_ref, *refs):
    hs_ref = refs[0]
    bufs = refs[1 : 1 + nbufs]
    rest = refs[1 + nbufs :]
    if phase == 0:
        acc_in = None
        acc_ref, v12_ref, v3_ref = rest
        acc_ref[...] = jnp.zeros_like(acc_ref)
    else:
        acc_in, acc_ref, v12_ref, v3_ref = rest
        acc_ref[...] = acc_in[...]
    v12_ref[VZERO] = jnp.zeros((BS, 2 * W), BF16)
    v3_ref[VZERO] = jnp.zeros((BS, W), BF16)
    at = FIRST_VSLOT[phase]
    for buf in bufs:
        for i in range(buf.shape[0]):
            load_table(v12_ref, v3_ref, at, buf[i])
            at += 1
    products(phase, list_ref, cnt_ref, hs_ref, v12_ref, v3_ref, acc_ref)


TABLE = [pltpu.VMEM((VZERO + 1, BS, 2 * W), BF16), pltpu.VMEM((VZERO + 1, BS, W), BF16)]


def run_phase(phase, lists, cnt, hs, bufs, acc):
    args = [lists, cnt, on_chip(hs), *bufs] + ([] if acc is None else [acc])
    share = (24, 16, 8)[phase] / 48
    return pl.pallas_call(
        functools.partial(phase_kernel, phase, len(bufs)),
        in_specs=[SM, SM] + [VM] * (len(args) - 2),
        out_specs=VM,
        out_shape=jax.ShapeDtypeStruct((RB, BS, W), F32),
        scratch_shapes=TABLE,
        compiler_params=pltpu.CompilerParams(vmem_limit_bytes=VMEM_LIMIT),
        cost_estimate=pl.CostEstimate(
            flops=int(NE * share * 2 * 6 * BS**3), bytes_accessed=4 * 2**20, transcendentals=0
        ),
        name=f"phase{phase}",
    )(*args)


def finish_one_kernel(list_ref, cnt_ref, sel_ref, hs_ref, buf_ref, acc_in, v_ref, first_ref, *rest):
    outs, (v12_ref, v3_ref) = rest[:4], rest[4:]
    first_ref[...] = acc_in[...] - 0.5 * v_ref[...]
    v12_ref[VZERO] = jnp.zeros((BS, 2 * W), BF16)
    v3_ref[VZERO] = jnp.zeros((BS, W), BF16)
    for i in range(GHOST):
        load_table(v12_ref, v3_ref, FIRST_VSLOT[2] + i, buf_ref[i])
    products(2, list_ref, cnt_ref, hs_ref, v12_ref, v3_ref, first_ref)
    for t in range(4):
        for g in range(GHOST):
            outs[t][g] = first_ref[sel_ref[t, g]]


def finish_one(lists, cnt, sel, hs, buf, acc, v):
    return pl.pallas_call(
        finish_one_kernel,
        in_specs=[SM, SM, SM] + [VM] * 4,
        out_specs=[VM] * 5,
        out_shape=[jax.ShapeDtypeStruct((RB, BS, W), F32)] + [jax.ShapeDtypeStruct((GHOST, BS, W), F32)] * 4,
        scratch_shapes=TABLE,
        compiler_params=pltpu.CompilerParams(vmem_limit_bytes=VMEM_LIMIT),
        cost_estimate=pl.CostEstimate(flops=NE * 2 * BS**3, bytes_accessed=8 * 2**20, transcendentals=0),
        name="finish_one",
    )(lists, cnt, sel, on_chip(hs), buf, acc, v)


def two_sum(a, b):
    s = a + b
    t = s - a
    return s, (a - (s - t)) + (b - t)


def pair_add(ah, al, bh, bl):
    s, e = two_sum(ah, bh)
    e = e + (al + bl)
    h = s + e
    return h, e - (h - s)


def power_scale(biggest):
    q = jnp.full_like(biggest, 2.0**-100)
    qi = jnp.full_like(biggest, 2.0**100)
    for e in (64, 64, 32, 16, 8, 4, 2, 1):
        t = q * (2.0**e)
        up = t <= biggest
        q = jnp.where(up, t, q)
        qi = jnp.where(up, qi * (2.0**-e), qi)
    return q * 2.0, qi * 0.5


def digits(x, bits, count):
    out = []
    x = x * (2.0 ** (bits - 1))
    for i in range(count):
        d = jnp.round(x)
        out.append(d.astype(BF16))
        x = (x - d) * (2.0**bits)
    return out


def gram_of_digits(cols, bits):
    count = len(cols)
    stacked = jnp.concatenate(cols, axis=1)
    full = lax.dot_general(stacked, stacked, (((0,), (0,)), ((), ())), preferred_element_type=F32)
    terms = []
    for w in range(2, 2 * count + 1):
        for i in range(1, count + 1):
            j = w - i
            if 1 <= j <= count:
                block = full[(i - 1) * W : i * W, (j - 1) * W : j * W]
                terms.append(block * (2.0 ** (2 - bits * w)))
    return terms


def finish_two_kernel(list_ref, cnt_ref, hs_ref, buf_ref, acc_in, first_ref, v_ref, out_ref, gram_ref, v12_ref, v3_ref, acc_ref):
    acc_ref[...] = acc_in[...]
    v12_ref[VZERO] = jnp.zeros((BS, 2 * W), BF16)
    v3_ref[VZERO] = jnp.zeros((BS, W), BF16)
    for i in range(GHOST):
        load_table(v12_ref, v3_ref, FIRST_VSLOT[2] + i, buf_ref[i])
    products(2, list_ref, cnt_ref, hs_ref, v12_ref, v3_ref, acc_ref)
    biggest = jnp.zeros((BS, W), F32)
    for r in range(RB):
        second = 2.0 * (acc_ref[r] - 0.5 * first_ref[r]) - v_ref[r]
        out_ref[r] = second
        biggest = jnp.maximum(biggest, jnp.abs(second))
    biggest = jnp.max(biggest, axis=0, keepdims=True)
    scale, inverse = power_scale(jnp.broadcast_to(biggest, (8, W)))
    scaled = out_ref[...].reshape(RB * BS, W) * inverse[0:1]
    terms = gram_of_digits(digits(scaled, 7, 4), 7)
    hi = terms[0]
    lo = jnp.zeros_like(hi)
    for t in terms[1:]:
        hi, e = two_sum(hi, t)
        lo = lo + e
    wide = jnp.broadcast_to(scale[0:1], (W, W))
    both = wide.T
    gram_ref[0] = (hi * wide) * both
    gram_ref[1] = (lo * wide) * both


def finish_two(lists, cnt, hs, buf, acc, first, v):
    return pl.pallas_call(
        finish_two_kernel,
        in_specs=[SM, SM] + [VM] * 5,
        out_specs=[VM] * 2,
        out_shape=[jax.ShapeDtypeStruct((RB, BS, W), F32), jax.ShapeDtypeStruct((2, W, W), F32)],
        scratch_shapes=TABLE + [pltpu.VMEM((RB, BS, W), F32)],
        compiler_params=pltpu.CompilerParams(vmem_limit_bytes=VMEM_LIMIT),
        cost_estimate=pl.CostEstimate(flops=NE * 2 * BS**3, bytes_accessed=8 * 2**20, transcendentals=0),
        name="finish_two",
    )(lists, cnt, on_chip(hs), buf, acc, first, v)


def eliminate(A):
    ri = lax.broadcasted_iota(jnp.int32, (8, W), 0)
    ci = lax.broadcasted_iota(jnp.int32, (8, W), 1)
    nb = W // 8
    A = [A[8 * b : 8 * b + 8, :] for b in range(nb)]
    B = [(ci == ri + 8 * b).astype(F32) for b in range(nb)]
    for j in range(W):
        bj, r = divmod(j, 8)
        row = jnp.broadcast_to(A[bj][r : r + 1, :], (8, W))
        brow = jnp.broadcast_to(B[bj][r : r + 1, :], (8, W))
        inv = 1.0 / jnp.broadcast_to(row[:, j : j + 1], (8, W))
        srow = row * inv
        sbrow = brow * inv
        for b in range(bj, nb):
            if b == bj and r == 7:
                continue
            col = jnp.broadcast_to(A[b][:, j : j + 1], (8, W))
            if b == bj:
                col = jnp.where(ri > r, col, 0.0)
            A[b] = A[b] - col * srow
            B[b] = B[b] - col * sbrow
    upper, lower_inv = [], []
    for b in range(nb):
        diag = jnp.sum(jnp.where(ci == ri + 8 * b, A[b], 0.0), axis=1, keepdims=True)
        s = 1.0 / jnp.sqrt(diag)
        upper.append(jnp.where(ci >= ri + 8 * b, A[b] * s, 0.0))
        lower_inv.append(jnp.where(ci <= ri + 8 * b, B[b] * s, 0.0))
    return jnp.concatenate(upper, axis=0), jnp.concatenate(lower_inv, axis=0)


def mm(a, b):
    return jnp.dot(a, b, precision=HIGHEST, preferred_element_type=F32)


def factor_kernel(total, gram_ref, inv_ref, factor_ref, u_ref, x_ref, y_ref):
    ri = lax.broadcasted_iota(jnp.int32, (W, W), 0)
    ci = lax.broadcasted_iota(jnp.int32, (W, W), 1)
    eye = (ri == ci).astype(F32)
    hi = gram_ref[0] * (1.0 / total)
    lo = gram_ref[1] * (1.0 / total)
    upper, linv = eliminate(hi)

    biggest = jnp.max(jnp.abs(upper), axis=0, keepdims=True)
    scale, inverse = power_scale(jnp.broadcast_to(biggest, (8, W)))
    wide, wide_inv = jnp.broadcast_to(scale[0:1], (W, W)), jnp.broadcast_to(inverse[0:1], (W, W))
    tall, tall_inv = wide.T, wide_inv.T
    rest = (hi * wide_inv) * tall_inv
    small = (lo * wide_inv) * tall_inv
    for t in gram_of_digits(digits(upper * wide_inv, 8, 4), 8):
        rest, e = two_sum(rest, -t)
        small = small + e
    rest = ((rest + small) * wide) * tall

    off = mm(mm(linv, rest), linv.T)
    off = 0.5 * (off + off.T)
    norm = jnp.sum(off * off)

    def half_lower(x):
        return jnp.where(ri > ci, x, jnp.where(ri == ci, 0.5 * x, 0.0))

    close = norm < 1e-5

    @pl.when(close)
    def _():
        x = half_lower(off)
        for _ in range(2):
            x = half_lower(off - mm(x, x.T))
        x_ref[...] = eye + x
        y_ref[...] = mm(eye - x, eye + mm(x, x))

    @pl.when(jnp.logical_not(close))
    def _():
        u2, l2 = eliminate(eye + off)
        x_ref[...] = u2.T
        y_ref[...] = l2

    upper_two = x_ref[...].T
    factor = mm(upper_two, upper)
    inv = mm(y_ref[...], linv).T
    inv = inv + mm(inv, eye - mm(factor, inv))
    inv_ref[...] = jnp.where(ri <= ci, inv, 0.0)
    factor_ref[...] = factor


def factors(gram, total):
    return pl.pallas_call(
        functools.partial(factor_kernel, float(total)),
        in_specs=[VM],
        out_specs=[VM, VM],
        out_shape=[jax.ShapeDtypeStruct((W, W), F32)] * 2,
        scratch_shapes=[pltpu.VMEM((W, W), F32)] * 3,
        compiler_params=pltpu.CompilerParams(vmem_limit_bytes=VMEM_LIMIT),
        name="factors",
    )(gram)


def basis_kernel(s_ref, t_ref, out_ref):
    out_ref[...] = mm(s_ref[...], t_ref[...])


def basis_of(second, inv):
    rows = second.shape[0]
    part = rows // 4
    return pl.pallas_call(
        basis_kernel,
        grid=(4,),
        in_specs=[pl.BlockSpec((part, W), lambda i: (i, 0)), pl.BlockSpec((W, W), lambda i: (0, 0))],
        out_specs=pl.BlockSpec((part, W), lambda i: (i, 0)),
        out_shape=jax.ShapeDtypeStruct((rows, W), F32),
        name="basis",
    )(second, inv)


def shards(vectors, hblocks, local_cols, ghost_lists):
    count = lax.axis_size("rows")
    me = lax.axis_index("rows")
    chips = count // 2
    core = me % 2
    odd = (me // 2) % 2

    def to_chip(i, by):
        return ((i // 2 + by) % chips) * 2 + i % 2

    pair_c = [(i, i ^ 1) for i in range(count)]
    pair_a = [(i, to_chip(i, 1 if (i // 2) % 2 == 0 else -1)) for i in range(count)]
    pair_b = [(i, to_chip(i, -1 if (i // 2) % 2 == 0 else 1)) for i in range(count)]
    pair_d = [(i, (i + (1 if i % 2 else -1)) % count) for i in range(count)]

    mine = lax.dynamic_index_in_dim(ghost_lists, me, 0, keepdims=False)
    which = jnp.stack([1 + core, 3 * odd, 3 - 3 * odd, 2 - core])
    sel = mine[which]
    at_c, at_a, at_b, at_d = 16, 24, 32, 40
    base = jnp.stack(
        [
            jnp.zeros_like(me),
            jnp.where(odd == 1, at_a, at_b) - 16,
            jnp.where(core == 1, at_c, at_d) - 24,
            jnp.where(core == 1, at_d, at_c) - 32,
            jnp.where(odd == 1, at_b, at_a) - 40,
        ]
    ).astype(jnp.int32)

    v = vectors.reshape(RB, BS, W)
    move = functools.partial(lax.ppermute, axis_name="rows")

    def gather(packs, hold):
        c = move(packs[0], perm=pair_c)
        a = move(packs[1], perm=pair_a)
        b = move(packs[2], perm=pair_b)
        return c, a, b

    packs = pack(sel, v)
    c, a, b = gather(packs, None)
    hs, lists, cnt = convert(hblocks, local_cols, base)
    d = move(packs[3], perm=pair_d)
    acc = run_phase(0, lists, cnt, hs, [v, c], None)
    acc = run_phase(1, lists, cnt, hs, [a, b], acc)
    first, *packs = finish_one(lists, cnt, sel, hs, d, acc, v)

    c, a, b = gather(packs, None)
    d = move(packs[3], perm=pair_d)
    acc = run_phase(0, lists, cnt, hs, [first, c], None)
    acc = run_phase(1, lists, cnt, hs, [a, b], acc)
    second, gram = finish_two(lists, cnt, hs, d, acc, first, v)

    perms = [[(i, i ^ 1) for i in range(count)]]
    for shift in (1, 3, 5):
        def flip(i, by):
            return i ^ (by << shift)

        perms.append([(i, flip(i, 1)) for i in range(count)])
        perms.append([(i, flip(i, 3)) for i in range(count)])
    hi, lo = gram[0], gram[1]
    for perm in perms:
        theirs = move(jnp.stack([hi, lo]), perm=perm)
        hi, lo = pair_add(hi, lo, theirs[0], theirs[1])
    inv, factor = factors(jnp.stack([hi, lo]), RB * BS * count)
    return basis_of(second.reshape(RB * BS, W), inv), factor


def solution(mesh):
    in_specs = (P("rows", None), P("rows", None, None, None), P("rows", None), P())
    out_specs = (P("rows", None), P())
    return jax.shard_map(shards, mesh=mesh, in_specs=in_specs, out_specs=out_specs, check_vma=False)
```

time: 1260 us -> 178 us (0.14)
  local copies, waits for them, and re-layouts: 371 us -> 8.78 us
  matrix products: 300 us -> 0 us
  waiting for transfers between devices: 319 us -> 37.5 us
  loops' own time: 198 us -> 0 us
  Pallas kernels: 0 us -> 110 us
  other arithmetic: 30.3 us -> 1.26 us
  between operations: 14.4 us -> 0.85 us
    dynamic_slice x512 -> x1, local copies, waits for them, and re-layouts: 313 us -> 0.21 us  [shards(): mine = lax.dynamic_index_in_dim(ghost_lists, me, 0, keepdims=False)]
    dot_general x519 -> x0, matrix products: 300 us -> none  [the longest x256 193 us: row_step(): jnp.dot(row_u, inverse, precision=lax.Precision.HIGHEST)]
    psum x2 -> x0, waiting for transfers between devices: 270 us -> none  [upper_factor(): gram = lax.psum(local_gram, 'rows') / total]
    another operation x4 -> x0, loops' own time: 198 us -> none  [the longest x2 190 us: lower_cholesky(): return lax.fori_loop(0, size, column_step, jnp.zeros_like(gram))]
    pallas_call x0 -> x10, Pallas kernels: none -> 110 us  [the longest x4 38.3 us: run_phase(): pl.pallas_call(functools.partial(phase_kernel, phase, len(bufs)), in_spec...]
    gather x10 -> x1, local copies, waits for them, and re-layouts: 38.1 us -> 1.14 us  [shards(): sel = mine[which]]
    add x256 -> x0, other arithmetic: 21.7 us -> none  [column_step(): lower + column[:, None] * (index_all[None, :] == j).astype(gram.dtype)]
    ppermute x8 -> x15, waiting for transfers between devices: 48.6 us -> 37.5 us  [the longest x7 35.5 us: shards(): theirs = move(jnp.stack([hi, lo]), perm=perm)]
  transfers between devices with their start and end apart: 10 -> 15, of which waited for: 6 -> 8; matrix products, arithmetic and copies ran while one was open for 2% -> 0% of each run, Pallas kernels for 0% -> 30%
where the time goes in v1:
time: 178 us
  Pallas kernels  110 us (62%)
  waiting for transfers between devices  37.5 us (21%)
  starting transfers between devices  19.2 us (11%)
  local copies, waits for them, and re-layouts  8.78 us (5%)
    pallas_call x4, Pallas kernels, run_phase(): pl.pallas_call(functools.partial(phase_kernel, phase, len(bufs)), in_spec...  38.3 us
    pallas_call x1, Pallas kernels, factors(): pl.pallas_call(functools.partial(factor_kernel, float(total)), in_specs=[...  36.6 us
    ppermute x7, waiting for transfers between devices, shards(): theirs = move(jnp.stack([hi, lo]), perm=perm)  35.5 us
    pallas_call x1, Pallas kernels, convert(): pl.pallas_call(convert_kernel, grid=(RB,), in_specs=[SM, SM, pl.BlockSpec...  14.5 us
    ppermute x2, starting transfers between devices, gather(): b = move(packs[2], perm=pair_b)  11.7 us
    pallas_call x1, Pallas kernels, finish_two(): pl.pallas_call(finish_two_kernel, in_specs=[SM, SM] + [VM] * 5, out_specs...  7.48 us
    unnamed x22, local copies, waits for them, and re-layouts  6.78 us
    pallas_call x1, Pallas kernels, finish_one(): pl.pallas_call(finish_one_kernel, in_specs=[SM, SM, SM] + [VM] * 4, out_s...  6.58 us
  transfers between devices with their start and end apart: 15, of which 8 were waited for; matrix products, arithmetic and copies ran while one was open for 0% of the time, Pallas kernels for 30%

profile of v1, /device:TPU:0, one launch (start us, length us, event | category | flops | bytes accessed | tf_op | source)
XLA Modules:
  0.0 177.7 jit_solution(972008444910557873)
XLA Ops:
  1.6 1.1 gather_fusion
  2.7 2.7 %pack.1 = (f32[8,128,128]{2,1,0:T(8,128)}, f32[8,128,128]{2,1,0:T(8,128)}, f32[8,128,128]{2,1,0:T(8,128)}, f32[8,128,128]{2,1,0:T(8,128)}) custom-call(s32[4,8]{1,0:T(4,128)} %gather_fusion, f32[16,128,128]{2,1,0:T(8,128)} %bitcast.12), custom_call_target="tpu_custom_call" | custom-call | tf_op jit(solution)/shard_map/pack/pallas_call | solution.py:103
  5.4 2.0 %collective-permute-start.1 = (f32[8,128,128]{2,1,0:T(8,128)}, f32[8,128,128]{2,1,0:T(8,128)S(1)}, u32[]{:S(2)}, u32[]{:S(2)}) collective-permute-start(f32[8,128,128]{2,1,0:T(8,128)} %get-tuple-element.22), channel_id=1, source_target_pairs={{0,2},{1,3},{2,0},{3,1},{4,6},{5,7},{6,4},{7,5},{8,10},{9,11},{10,... | collective-permute-start | bytes 1572872 | tf_op jit(solution)/shard_map/ppermute | solution.py:447
  7.4 7.2 %collective-permute-start.2 = (f32[8,128,128]{2,1,0:T(8,128)}, f32[8,128,128]{2,1,0:T(8,128)S(1)}, u32[]{:S(2)}, u32[]{:S(2)}) collective-permute-start(f32[8,128,128]{2,1,0:T(8,128)} %get-tuple-element.23), channel_id=1, source_target_pairs={{0,126},{1,127},{2,4},{3,5},{4,2},{5,3},{6,8},{7,9},{8,6},{9,7},{1... | collective-permute-start | bytes 1572872 | tf_op jit(solution)/shard_map/ppermute | solution.py:448
  15.2 14.5 %convert.2 = (bf16[320,384,128]{2,1,0:T(8,128)(2,1)S(1)}, s32[3,368]{1,0:T(4,128)}, s32[3]{0:T(128)}) custom-call(s32[16,20]{1,0:T(8,128)} %cols_ref.1, s32[5]{0:T(128)} %stack.70.base_ref, f32[16,20,128,128]{3,2,1,0:T(8,128)} %h_ref.1), custom_call_target="tpu_custom_call" | custom-call | flops 41943040 | bytes 20971520 | tf_op jit(solution)/shard_map/convert/pallas_call | solution.py:80
  30.5 10.6 %phase0.2.refs_3_ = f32[16,128,128]{2,1,0:T(8,128)} custom-call(s32[3,368]{1,0:T(4,128)} %get-tuple-element.18.list_ref, s32[3]{0:T(128)} %get-tuple-element.19.cnt_ref, bf16[320,384,128]{2,1,0:T(8,128)(2,1)S(1)} %get-tuple-element.20.refs_0_.hs_ref, f32[16,128,128]{2,1,0:T(8,128)} %bitcast.13, f32[8,128,128]{2,1,0:T(8,128)} %copy-done.6), custom_call_target="tpu_custom_call" | custom-call | flops 4026531840 | bytes 4194304 | tf_op jit(solution)/shard_map/phase0/pallas_call | solution.py:172
  42.7 8.5 %phase1.2.acc_in = f32[16,128,128]{2,1,0:T(8,128)} custom-call(s32[3,368]{1,0:T(4,128)} %get-tuple-element.18.list_ref, s32[3]{0:T(128)} %get-tuple-element.19.cnt_ref, bf16[320,384,128]{2,1,0:T(8,128)(2,1)S(1)} %get-tuple-element.20.refs_0_.hs_ref, f32[8,128,128]{2,1,0:T(8,128)} %copy-done.4, f32[8,128,128]{2,1,0:T(8,128)} %copy-done.5, ...), custom_call_target="tpu_custom_call" | custom-call | flops 2684354560 | bytes 4194304 | tf_op jit(solution)/shard_map/phase1/pallas_call | solution.py:172
  52.0 6.6 %finish_one.1 = (f32[16,128,128]{2,1,0:T(8,128)}, f32[8,128,128]{2,1,0:T(8,128)}, f32[8,128,128]{2,1,0:T(8,128)}, f32[8,128,128]{2,1,0:T(8,128)}, f32[8,128,128]{2,1,0:T(8,128)}) custom-call(s32[3,368]{1,0:T(4,128)} %get-tuple-element.18.list_ref, s32[3]{0:T(128)} %get-tuple-element.19.cnt_ref, s32[4,8]{1,0:T(4,128)} %gather_fusion, ...), custom_call_target="tpu_custom_call" | custom-call | flops 1342177280 | bytes 8388608 | tf_op jit(solution)/shard_map/finish_one/pallas_call | solution.py:200
  58.6 2.3 %collective-permute-start.5 = (f32[8,128,128]{2,1,0:T(8,128)}, f32[8,128,128]{2,1,0:T(8,128)S(1)}, u32[]{:S(2)}, u32[]{:S(2)}) collective-permute-start(f32[8,128,128]{2,1,0:T(8,128)} %get-tuple-element.26), channel_id=1, source_target_pairs={{0,2},{1,3},{2,0},{3,1},{4,6},{5,7},{6,4},{7,5},{8,10},{9,11},{10,... | collective-permute-start | bytes 1572872 | tf_op jit(solution)/shard_map/ppermute | solution.py:447
  60.9 4.6 %collective-permute-start.6 = (f32[8,128,128]{2,1,0:T(8,128)}, f32[8,128,128]{2,1,0:T(8,128)S(1)}, u32[]{:S(2)}, u32[]{:S(2)}) collective-permute-start(f32[8,128,128]{2,1,0:T(8,128)} %get-tuple-element.27), channel_id=1, source_target_pairs={{0,126},{1,127},{2,4},{3,5},{4,2},{5,3},{6,8},{7,9},{8,6},{9,7},{1... | collective-permute-start | bytes 1572872 | tf_op jit(solution)/shard_map/ppermute | solution.py:448
  65.5 2.4 %collective-permute-start.4 = (f32[8,128,128]{2,1,0:T(8,128)}, f32[8,128,128]{2,1,0:T(8,128)S(1)}, u32[]{:S(2)}, u32[]{:S(2)}) collective-permute-start(f32[8,128,128]{2,1,0:T(8,128)} %get-tuple-element.25), channel_id=1, source_target_pairs={{0,127},{1,2},{2,1},{3,4},{4,3},{5,6},{6,5},{7,8},{8,7},{9,10},{10... | collective-permute-start | bytes 1572872 | tf_op jit(solution)/shard_map/ppermute | solution.py:460
  68.7 10.6 %phase0.3.refs_3_ = f32[16,128,128]{2,1,0:T(8,128)} custom-call(s32[3,368]{1,0:T(4,128)} %get-tuple-element.18.list_ref, s32[3]{0:T(128)} %get-tuple-element.19.cnt_ref, bf16[320,384,128]{2,1,0:T(8,128)(2,1)S(1)} %get-tuple-element.20.refs_0_.hs_ref, f32[16,128,128]{2,1,0:T(8,128)} %get-tuple-element.28.refs_1_.first_ref, f32[8,128,128]{2,1,0:T(8,128)} %copy-done.10), custom_call_target="tpu_custom_call" | custom-call | flops 4026531840 | bytes 4194304 | tf_op jit(solution)/shard_map/phase0/pallas_call | solution.py:172
  79.3 2.0 %collective-permute-done.6.refs_2_ = f32[8,128,128]{2,1,0:T(8,128)S(1)} collective-permute-done((f32[8,128,128]{2,1,0:T(8,128)}, f32[8,128,128]{2,1,0:T(8,128)S(1)}, u32[]{:S(2)}, u32[]{:S(2)}) %collective-permute-start.6) | collective-permute-done | bytes 524320 | tf_op jit(solution)/shard_map/ppermute | solution.py:448
  82.1 8.5 %phase1.3.acc_in = f32[16,128,128]{2,1,0:T(8,128)} custom-call(s32[3,368]{1,0:T(4,128)} %get-tuple-element.18.list_ref, s32[3]{0:T(128)} %get-tuple-element.19.cnt_ref, bf16[320,384,128]{2,1,0:T(8,128)(2,1)S(1)} %get-tuple-element.20.refs_0_.hs_ref, f32[8,128,128]{2,1,0:T(8,128)} %copy-done.8, f32[8,128,128]{2,1,0:T(8,128)} %copy-done.9, ...), custom_call_target="tpu_custom_call" | custom-call | flops 2684354560 | bytes 4194304 | tf_op jit(solution)/shard_map/phase1/pallas_call | solution.py:172
  91.5 7.5 %finish_two.1 = (f32[16,128,128]{2,1,0:T(8,128)}, f32[2,128,128]{2,1,0:T(8,128)}) custom-call(s32[3,368]{1,0:T(4,128)} %get-tuple-element.18.list_ref, s32[3]{0:T(128)} %get-tuple-element.19.cnt_ref, bf16[320,384,128]{2,1,0:T(8,128)(2,1)S(1)} %get-tuple-element.20.refs_0_.hs_ref, f32[8,128,128]{2,1,0:T(8,128)} %copy-done.7, f32[16,128,128]{2,1,0:T(8,128)} %phase1.3.acc_in, ...), custom_call_target="tpu_custom_call" | custom-call | flops 1342177280 | bytes 8388608 | tf_op jit(solution)/shard_map/finish_two/pallas_call | solution.py:288
  98.9 1.6 collective-permute-done.8
  101.7 5.5 %collective-permute-done.9 = f32[2,128,128]{2,1,0:T(8,128)S(1)} collective-permute-done((f32[2,128,128]{2,1,0:T(8,128)S(1)}, f32[2,128,128]{2,1,0:T(8,128)S(1)}, u32[]{:S(2)}, u32[]{:S(2)}) %collective-permute-start.9) | collective-permute-done | bytes 131104 | tf_op jit(solution)/shard_map/ppermute | solution.py:474
  107.4 6.2 %collective-permute-done.10 = f32[2,128,128]{2,1,0:T(8,128)S(1)} collective-permute-done((f32[2,128,128]{2,1,0:T(8,128)S(1)}, f32[2,128,128]{2,1,0:T(8,128)S(1)}, u32[]{:S(2)}, u32[]{:S(2)}) %collective-permute-start.10) | collective-permute-done | bytes 131104 | tf_op jit(solution)/shard_map/ppermute | solution.py:474
  113.7 5.0 %collective-permute-done.11 = f32[2,128,128]{2,1,0:T(8,128)S(1)} collective-permute-done((f32[2,128,128]{2,1,0:T(8,128)S(1)}, f32[2,128,128]{2,1,0:T(8,128)S(1)}, u32[]{:S(2)}, u32[]{:S(2)}) %collective-permute-start.11) | collective-permute-done | bytes 131104 | tf_op jit(solution)/shard_map/ppermute | solution.py:474
  118.8 6.2 %collective-permute-done.12 = f32[2,128,128]{2,1,0:T(8,128)S(1)} collective-permute-done((f32[2,128,128]{2,1,0:T(8,128)S(1)}, f32[2,128,128]{2,1,0:T(8,128)S(1)}, u32[]{:S(2)}, u32[]{:S(2)}) %collective-permute-start.12) | collective-permute-done | bytes 131104 | tf_op jit(solution)/shard_map/ppermute | solution.py:474
  125.1 5.0 %collective-permute-done.13 = f32[2,128,128]{2,1,0:T(8,128)S(1)} collective-permute-done((f32[2,128,128]{2,1,0:T(8,128)S(1)}, f32[2,128,128]{2,1,0:T(8,128)S(1)}, u32[]{:S(2)}, u32[]{:S(2)}) %collective-permute-start.13) | collective-permute-done | bytes 131104 | tf_op jit(solution)/shard_map/ppermute | solution.py:474
  130.2 6.2 %collective-permute-done.14 = f32[2,128,128]{2,1,0:T(8,128)S(1)} collective-permute-done((f32[2,128,128]{2,1,0:T(8,128)S(1)}, f32[2,128,128]{2,1,0:T(8,128)S(1)}, u32[]{:S(2)}, u32[]{:S(2)}) %collective-permute-start.14) | collective-permute-done | bytes 131104 | tf_op jit(solution)/shard_map/ppermute | solution.py:474
  136.4 36.6 %factors.1 = (f32[128,128]{1,0:T(8,128)S(1)}, f32[128,128]{1,0:T(8,128)}) custom-call(f32[2,128,128]{2,1,0:T(8,128)S(1)} %pad_maximum_fusion.6.gram_ref), custom_call_target="tpu_custom_call" | custom-call | tf_op jit(solution)/shard_map/factors/pallas_call | solution.py:385
  173.6 4.1 %basis.1 = f32[2048,128]{1,0:T(8,128)} custom-call(f32[2048,128]{1,0:T(8,128)} %bitcast.16, f32[128,128]{1,0:T(8,128)} %copy-done.2), custom_call_target="tpu_custom_call" | custom-call | tf_op jit(solution)/shard_map/basis/pallas_call | solution.py:403
  (57 shorter events, 9.6 us)
Async XLA Ops:
  5.4 24.3 %collective-permute-start.3 = (f32[8,128,128]{2,1,0:T(8,128)}, f32[8,128,128]{2,1,0:T(8,128)S(1)}, u32[]{:S(2)}, u32[]{:S(2)}) collective-permute-start(f32[8,128,128]{2,1,0:T(8,128)} %get-tuple-element.24), channel_id=1, source_target_pairs={{0,1},{1,0},{2,3},{3,2},{4,5},{5,4},{6,7},{7,6},{8,9},{9,8},{10,11... | collective-permute-start | bytes 1572872 | tf_op jit(solution)/shard_map/ppermute | solution.py:446
  5.4 35.7 %collective-permute-start.1 = (f32[8,128,128]{2,1,0:T(8,128)}, f32[8,128,128]{2,1,0:T(8,128)S(1)}, u32[]{:S(2)}, u32[]{:S(2)}) collective-permute-start(f32[8,128,128]{2,1,0:T(8,128)} %get-tuple-element.22), channel_id=1, source_target_pairs={{0,2},{1,3},{2,0},{3,1},{4,6},{5,7},{6,4},{7,5},{8,10},{9,11},{10,... | collective-permute-start | bytes 1572872 | tf_op jit(solution)/shard_map/ppermute | solution.py:447
  7.4 33.7 %collective-permute-start.2 = (f32[8,128,128]{2,1,0:T(8,128)}, f32[8,128,128]{2,1,0:T(8,128)S(1)}, u32[]{:S(2)}, u32[]{:S(2)}) collective-permute-start(f32[8,128,128]{2,1,0:T(8,128)} %get-tuple-element.23), channel_id=1, source_target_pairs={{0,126},{1,127},{2,4},{3,5},{4,2},{5,3},{6,8},{7,9},{8,6},{9,7},{1... | collective-permute-start | bytes 1572872 | tf_op jit(solution)/shard_map/ppermute | solution.py:448
  14.6 36.7 %collective-permute-start = (f32[8,128,128]{2,1,0:T(8,128)}, f32[8,128,128]{2,1,0:T(8,128)S(1)}, u32[]{:S(2)}, u32[]{:S(2)}) collective-permute-start(f32[8,128,128]{2,1,0:T(8,128)} %get-tuple-element.21), channel_id=1, source_target_pairs={{0,127},{1,2},{2,1},{3,4},{4,3},{5,6},{6,5},{7,8},{8,7},{9,10},{10... | collective-permute-start | bytes 1572872 | tf_op jit(solution)/shard_map/ppermute | solution.py:454
  29.7 0.8 copy-start.6
  41.1 0.8 copy-start.4
  41.9 0.8 copy-start.5
  51.3 0.8 copy-start.3
  58.6 9.3 %collective-permute-start.7 = (f32[8,128,128]{2,1,0:T(8,128)}, f32[8,128,128]{2,1,0:T(8,128)S(1)}, u32[]{:S(2)}, u32[]{:S(2)}) collective-permute-start(f32[8,128,128]{2,1,0:T(8,128)} %get-tuple-element.29), channel_id=1, source_target_pairs={{0,1},{1,0},{2,3},{3,2},{4,5},{5,4},{6,7},{7,6},{8,9},{9,8},{10,11... | collective-permute-start | bytes 1572872 | tf_op jit(solution)/shard_map/ppermute | solution.py:446
  58.6 20.7 %collective-permute-start.5 = (f32[8,128,128]{2,1,0:T(8,128)}, f32[8,128,128]{2,1,0:T(8,128)S(1)}, u32[]{:S(2)}, u32[]{:S(2)}) collective-permute-start(f32[8,128,128]{2,1,0:T(8,128)} %get-tuple-element.26), channel_id=1, source_target_pairs={{0,2},{1,3},{2,0},{3,1},{4,6},{5,7},{6,4},{7,5},{8,10},{9,11},{10,... | collective-permute-start | bytes 1572872 | tf_op jit(solution)/shard_map/ppermute | solution.py:447
  60.9 20.4 %collective-permute-start.6 = (f32[8,128,128]{2,1,0:T(8,128)}, f32[8,128,128]{2,1,0:T(8,128)S(1)}, u32[]{:S(2)}, u32[]{:S(2)}) collective-permute-start(f32[8,128,128]{2,1,0:T(8,128)} %get-tuple-element.27), channel_id=1, source_target_pairs={{0,126},{1,127},{2,4},{3,5},{4,2},{5,3},{6,8},{7,9},{8,6},{9,7},{1... | collective-permute-start | bytes 1572872 | tf_op jit(solution)/shard_map/ppermute | solution.py:448
  65.5 25.2 %collective-permute-start.4 = (f32[8,128,128]{2,1,0:T(8,128)}, f32[8,128,128]{2,1,0:T(8,128)S(1)}, u32[]{:S(2)}, u32[]{:S(2)}) collective-permute-start(f32[8,128,128]{2,1,0:T(8,128)} %get-tuple-element.25), channel_id=1, source_target_pairs={{0,127},{1,2},{2,1},{3,4},{4,3},{5,6},{6,5},{7,8},{8,7},{9,10},{10... | collective-permute-start | bytes 1572872 | tf_op jit(solution)/shard_map/ppermute | solution.py:460
  67.9 0.8 copy-start.10
  68.7 109.0 %copy-start.1 = (s32[128,4,8]{0,2,1:T(8,128)S(1)}, s32[128,4,8]{0,2,1:T(8,128)}, u32[]{:S(2)}) copy-start(s32[128,4,8]{0,2,1:T(8,128)} %param.7) | copy-start | bytes 49156
  79.3 2.0 %copy-start.8 = (f32[8,128,128]{2,1,0:T(8,128)}, f32[8,128,128]{2,1,0:T(8,128)S(1)}, u32[]{:S(2)}) copy-start(f32[8,128,128]{2,1,0:T(8,128)S(1)} %collective-permute-done.5.refs_1_) | copy-start | bytes 1572868
  81.3 0.8 copy-start.9
  90.6 0.8 copy-start.7
  98.9 1.6 collective-permute-start.8
  101.4 5.8 %collective-permute-start.9 = (f32[2,128,128]{2,1,0:T(8,128)S(1)}, f32[2,128,128]{2,1,0:T(8,128)S(1)}, u32[]{:S(2)}, u32[]{:S(2)}) collective-permute-start(f32[2,128,128]{2,1,0:T(8,128)S(1)} %pad_maximum_fusion), channel_id=1, source_target_pairs={{0,2},{1,3},{2,0},{3,1},{4,6},{5,7},{6,4},{7,5},{8,10},{9,11},{10,... | collective-permute-start | bytes 393224 | tf_op jit(solution)/shard_map/ppermute | solution.py:474
  107.3 6.3 %collective-permute-start.10 = (f32[2,128,128]{2,1,0:T(8,128)S(1)}, f32[2,128,128]{2,1,0:T(8,128)S(1)}, u32[]{:S(2)}, u32[]{:S(2)}) collective-permute-start(f32[2,128,128]{2,1,0:T(8,128)S(1)} %pad_maximum_fusion.1), channel_id=1, source_target_pairs={{0,6},{1,7},{2,4},{3,5},{4,2},{5,3},{6,0},{7,1},{8,14},{9,15},{10,... | collective-permute-start | bytes 393224 | tf_op jit(solution)/shard_map/ppermute | solution.py:474
  113.6 5.0 %collective-permute-start.11 = (f32[2,128,128]{2,1,0:T(8,128)S(1)}, f32[2,128,128]{2,1,0:T(8,128)S(1)}, u32[]{:S(2)}, u32[]{:S(2)}) collective-permute-start(f32[2,128,128]{2,1,0:T(8,128)S(1)} %pad_maximum_fusion.2), channel_id=1, source_target_pairs={{0,8},{1,9},{2,10},{3,11},{4,12},{5,13},{6,14},{7,15},{8,0},{9,1},... | collective-permute-start | bytes 393224 | tf_op jit(solution)/shard_map/ppermute | solution.py:474
  118.7 6.3 %collective-permute-start.12 = (f32[2,128,128]{2,1,0:T(8,128)S(1)}, f32[2,128,128]{2,1,0:T(8,128)S(1)}, u32[]{:S(2)}, u32[]{:S(2)}) collective-permute-start(f32[2,128,128]{2,1,0:T(8,128)S(1)} %pad_maximum_fusion.3), channel_id=1, source_target_pairs={{0,24},{1,25},{2,26},{3,27},{4,28},{5,29},{6,30},{7,31},{8,16},{9,... | collective-permute-start | bytes 393224 | tf_op jit(solution)/shard_map/ppermute | solution.py:474
  125.0 5.0 %collective-permute-start.13 = (f32[2,128,128]{2,1,0:T(8,128)S(1)}, f32[2,128,128]{2,1,0:T(8,128)S(1)}, u32[]{:S(2)}, u32[]{:S(2)}) collective-permute-start(f32[2,128,128]{2,1,0:T(8,128)S(1)} %pad_maximum_fusion.4), channel_id=1, source_target_pairs={{0,32},{1,33},{2,34},{3,35},{4,36},{5,37},{6,38},{7,39},{8,40},{9,... | collective-permute-start | bytes 393224 | tf_op jit(solution)/shard_map/ppermute | solution.py:474
  130.1 6.3 %collective-permute-start.14 = (f32[2,128,128]{2,1,0:T(8,128)S(1)}, f32[2,128,128]{2,1,0:T(8,128)S(1)}, u32[]{:S(2)}, u32[]{:S(2)}) collective-permute-start(f32[2,128,128]{2,1,0:T(8,128)S(1)} %pad_maximum_fusion.5), channel_id=1, source_target_pairs={{0,96},{1,97},{2,98},{3,99},{4,100},{5,101},{6,102},{7,103},{8,104... | collective-permute-start | bytes 393224 | tf_op jit(solution)/shard_map/ppermute | solution.py:474
  (2 other events, 1.3 us)

commit v2 on v0

v2 whole, which is shorter than its diff:
```python
import functools

import jax
import jax.numpy as jnp
from jax import lax
from jax.experimental import pallas as pl
from jax.experimental.pallas import tpu as pltpu
from jax.sharding import PartitionSpec as P

BS = 128
W = 128
RB = 16
GHOST = 8
NNZB = 20
NE = RB * NNZB
SPLIT = 3
BAND = W // 4
PACKED = BAND + 8
A_B_D = 4
VZERO = 48
MAXE = NE + 48
OWN, AT_C, AT_A, AT_B, AT_D = 0, 16, 24, 32, 40
LISTS = 5
GROUP = 8
FETCH, FETCHES = 10, 8
VMEM_LIMIT = 26 * 1024 * 1024
F32 = jnp.float32
BF16 = jnp.bfloat16
HIGHEST = lax.Precision.HIGHEST

ANY = pl.BlockSpec(memory_space=pl.ANY)
VM = pl.BlockSpec(memory_space=pltpu.VMEM)
SM = pl.BlockSpec(memory_space=pltpu.SMEM)


def on_chip(x):
    return pltpu.with_memory_space_constraint(x, pltpu.VMEM)


def pieces(x, count=SPLIT):
    out = []
    for _ in range(count - 1):
        part = x.astype(BF16)
        out.append(part)
        x = x - part.astype(F32)
    out.append(x.astype(BF16))
    return out


def load_table(v12_ref, v3_ref, at, block):
    hi, mid, lo = pieces(block)
    v12_ref[at, :, 0:W] = hi
    v12_ref[at, :, W : 2 * W] = mid
    v3_ref[at] = lo


def load_zero(v12_ref, v3_ref):
    v12_ref[VZERO] = jnp.zeros((BS, 2 * W), BF16)
    v3_ref[VZERO] = jnp.zeros((BS, W), BF16)


def group_of_products(which, first, count, list_ref, hs_ref, v12_ref, v3_ref, acc_ref):
    for i in range(count):
        one = list_ref[which, first + 2 * i]
        two = list_ref[which, first + 2 * i + 1]
        row = lax.shift_right_logical(one, 16)
        e1 = lax.shift_right_logical(one, 6) & 1023
        e2 = lax.shift_right_logical(two, 6) & 1023
        s1 = one & 63
        s2 = two & 63
        lhs = jnp.concatenate([hs_ref[e1], hs_ref[e2]], axis=1)
        rhs = jnp.concatenate([v12_ref[s1], v12_ref[s2]], axis=0)
        low = jnp.concatenate([v3_ref[s1], v3_ref[s2]], axis=0)
        big = jnp.dot(lhs, rhs, preferred_element_type=F32)
        small = jnp.dot(lhs[0:BS], low, preferred_element_type=F32)
        total = big[0:BS, 0:W] + (
            (big[0:BS, W:] + big[BS : 2 * BS, 0:W]) + (big[BS : 2 * BS, W:] + big[2 * BS :, 0:W] + small)
        )
        acc_ref[row] = acc_ref[row] + total


def products(which, group, list_ref, cnt_ref, *refs):
    def large(g, carry):
        group_of_products(which, g * (2 * group), group, list_ref, *refs)
        return carry

    def small(g, carry):
        group_of_products(which, begin + g * (2 * GROUP), GROUP, list_ref, *refs)
        return carry

    count = cnt_ref[which]
    begin = 0
    if group > GROUP:
        steps = lax.div(count, 2 * group)
        lax.fori_loop(0, steps, large, 0)
        begin = steps * (2 * group)
    lax.fori_loop(0, lax.div(count - begin + (2 * GROUP - 1), 2 * GROUP), small, 0)


def convert_kernel(cols_ref, info_ref, h_ref, hs_ref, list_ref, cnt_ref, buf_ref, sem_ref):
    def fetch(i, slot):
        return pltpu.make_async_copy(h_ref.at[pl.ds(i * FETCH, FETCH)], buf_ref.at[slot], sem_ref.at[slot])

    for i in range(FETCHES):
        fetch(i, i).start()
    def list_row(r, counts):
        counts = list(counts)
        for n in range(NNZB):
            col = cols_ref[r, n]
            kind = jnp.where(col < RB, 0, 1 + lax.shift_right_logical(col - RB, 3))
            v = col + info_ref[4 + kind]
            code = r * 65536 + (r * NNZB + n) * 64 + v
            source = lax.shift_right_logical(v, 3)
            mine = [source < 3, source == 3, source == 4, source == 5]
            at = jnp.where(mine[0], counts[0], jnp.where(mine[1], counts[1], jnp.where(mine[2], counts[2], counts[3])))
            list_ref[jnp.maximum(source - 2, 0), at] = code
            list_ref[A_B_D, counts[4]] = code
            for p, yes in enumerate((*mine, source >= 3)):
                counts[p] = counts[p] + yes.astype(jnp.int32)
        for p in range(LISTS):
            list_ref[p, counts[p]] = r * 65536 + VZERO
            counts[p] = counts[p] + (counts[p] & 1)
        return tuple(counts)

    counts = lax.fori_loop(0, RB, list_row, (jnp.int32(0),) * LISTS)
    for p in range(LISTS):
        cnt_ref[p] = counts[p]
        for i in range(2 * GROUP):
            list_ref[p, counts[p] + i] = VZERO

    def part(i, carry):
        slot = lax.rem(i, FETCHES)
        fetch(i, slot).wait()
        for n in range(FETCH):
            e = i * FETCH + n
            hi, mid, lo = pieces(buf_ref[slot, n])
            hs_ref[e, 0:BS, :] = hi
            hs_ref[e, BS : 2 * BS, :] = mid
            hs_ref[e, 2 * BS : 3 * BS, :] = lo

        @pl.when(i + FETCHES < NE // FETCH)
        def _():
            fetch(i + FETCHES, slot).start()

        return carry

    lax.fori_loop(0, NE // FETCH, part, 0)


TABLE = [pltpu.VMEM((VZERO + 1, BS, 2 * W), BF16), pltpu.VMEM((VZERO + 1, BS, W), BF16)]


def convert(hblocks, local_cols, info):
    return pl.pallas_call(
        convert_kernel,
        in_specs=[SM, SM, ANY],
        out_specs=[VM, SM, SM],
        out_shape=[
            pltpu.VMEM((NE, SPLIT * BS, BS), BF16),
            jax.ShapeDtypeStruct((LISTS, MAXE), jnp.int32),
            jax.ShapeDtypeStruct((LISTS,), jnp.int32),
        ],
        scratch_shapes=[pltpu.VMEM((FETCHES, FETCH, BS, BS), F32), pltpu.SemaphoreType.DMA((FETCHES,))],
        compiler_params=pltpu.CompilerParams(vmem_limit_bytes=VMEM_LIMIT),
        cost_estimate=pl.CostEstimate(flops=NE * 4 * BS**3, bytes_accessed=NE * BS * BS * 4, transcendentals=0),
        name="convert",
    )(local_cols, info, hblocks.reshape(NE, BS, BS))


def fill_packs(info_ref, lists_ref, blocks_ref, outs):
    for t in range(4):
        for g in range(GHOST):
            outs[t][g] = blocks_ref[lists_ref[info_ref[t], g]]


PACKS = [pltpu.VMEM((GHOST, BS, W), F32)] * 4


def pack_kernel(info_ref, lists_ref, v_ref, held_ref, *rest):
    outs, sem_ref = rest[:4], rest[4]
    copies = []
    for i in range(RB // 2):
        part = pl.ds(2 * i, 2)
        copies.append(pltpu.make_async_copy(v_ref.at[part], held_ref.at[part], sem_ref.at[i]))
        copies[-1].start()
    for copy in copies:
        copy.wait()
    fill_packs(info_ref, lists_ref, held_ref, outs)


def pack(info, mine, v):
    return pl.pallas_call(
        pack_kernel,
        in_specs=[SM, SM, pl.BlockSpec(memory_space=pltpu.HBM)],
        out_specs=[VM] * 5,
        out_shape=[pltpu.VMEM((RB, BS, W), F32)] + PACKS,
        scratch_shapes=[pltpu.SemaphoreType.DMA((RB // 2,))],
        compiler_params=pltpu.CompilerParams(vmem_limit_bytes=VMEM_LIMIT),
        name="pack",
    )(info, mine, pltpu.with_memory_space_constraint(v, pltpu.HBM))


def add_list(which, group, places, bufs, list_ref, cnt_ref, hs_ref, v12_ref, v3_ref, acc_ref):
    load_zero(v12_ref, v3_ref)
    for place, buf in zip(places, bufs):
        for i in range(buf.shape[0]):
            load_table(v12_ref, v3_ref, place + i, buf[i])
    products(which, group, list_ref, cnt_ref, hs_ref, v12_ref, v3_ref, acc_ref)


def phase_kernel(which, group, places, fresh, list_ref, cnt_ref, hs_ref, *refs):
    bufs = refs[: len(places)]
    acc_ref, v12_ref, v3_ref = refs[-3:]
    if fresh:
        acc_ref[...] = jnp.zeros_like(acc_ref)
    add_list(which, group, places, bufs, list_ref, cnt_ref, hs_ref, v12_ref, v3_ref, acc_ref)


def run_phase(which, group, places, lists, cnt, hs, bufs, acc=None):
    args = [lists, cnt] + [on_chip(x) for x in (hs, *bufs)] + ([] if acc is None else [on_chip(acc)])
    return pl.pallas_call(
        functools.partial(phase_kernel, which, group, places, acc is None),
        in_specs=[SM, SM] + [VM] * (len(args) - 2),
        out_specs=VM,
        out_shape=pltpu.VMEM((RB, BS, W), F32),
        scratch_shapes=TABLE,
        input_output_aliases={} if acc is None else {len(args) - 1: 0},
        compiler_params=pltpu.CompilerParams(vmem_limit_bytes=VMEM_LIMIT),
        cost_estimate=pl.CostEstimate(
            flops=len(places) * NE * 2 * BS**3, bytes_accessed=4 * 2**20, transcendentals=0
        ),
        name=f"phase_{which}",
    )(*args)


def finish_one_kernel(
    list_ref, cnt_ref, info_ref, mine_ref, hs_ref, a_ref, b_ref, d_ref, v_ref, acc_in, first_ref, *rest
):
    outs, tables = rest[:4], rest[4:]
    for r in range(RB):
        first_ref[r] = first_ref[r] - 0.5 * v_ref[r]
    places, bufs = (AT_A, AT_B, AT_D), (a_ref, b_ref, d_ref)
    add_list(A_B_D, 2 * GROUP, places, bufs, list_ref, cnt_ref, hs_ref, *tables, first_ref)
    fill_packs(info_ref, mine_ref, first_ref, outs)


def finish_one(lists, cnt, info, mine, hs, bufs, v, acc):
    return pl.pallas_call(
        finish_one_kernel,
        in_specs=[SM] * 4 + [VM] * 6,
        out_specs=[VM] * 5,
        out_shape=[pltpu.VMEM((RB, BS, W), F32)] + PACKS,
        scratch_shapes=TABLE,
        input_output_aliases={9: 0},
        compiler_params=pltpu.CompilerParams(vmem_limit_bytes=VMEM_LIMIT),
        cost_estimate=pl.CostEstimate(flops=NE * 6 * BS**3, bytes_accessed=8 * 2**20, transcendentals=0),
        name="finish_one",
    )(lists, cnt, info, mine, on_chip(hs), *[on_chip(x) for x in bufs], on_chip(v), on_chip(acc))


def two_sum(a, b):
    s = a + b
    t = s - a
    return s, (a - (s - t)) + (b - t)


def pair_add(ah, al, bh, bl):
    s, e = two_sum(ah, bh)
    e = e + (al + bl)
    h = s + e
    return h, e - (h - s)


def power_scale(biggest):
    q = jnp.full_like(biggest, 2.0**-100)
    qi = jnp.full_like(biggest, 2.0**100)
    for e in (64, 64, 32, 16, 8, 4, 2, 1):
        t = q * (2.0**e)
        up = t <= biggest
        q = jnp.where(up, t, q)
        qi = jnp.where(up, qi * (2.0**-e), qi)
    return q * 2.0, qi * 0.5


def digits(x, bits, count):
    out = []
    x = x * (2.0 ** (bits - 1))
    for i in range(count):
        d = jnp.round(x)
        out.append(d.astype(BF16))
        x = (x - d) * (2.0**bits)
    return out


def gram_of_digits(cols, bits):
    count = len(cols)
    stacked = jnp.concatenate(cols, axis=1)
    full = lax.dot_general(stacked, stacked, (((0,), (0,)), ((), ())), preferred_element_type=F32)
    terms = []
    for w in range(2, 2 * count):
        total = None
        for i in range(1, count + 1):
            j = w - i
            if 1 <= j <= count:
                block = full[(i - 1) * W : i * W, (j - 1) * W : j * W]
                total = block if total is None else total + block
        terms.append(total * (2.0 ** (2 - bits * w)))
    return terms


def lanes_of(rows):
    return lax.broadcasted_iota(jnp.int32, (rows, W), 1)


def pack_symmetric(g):
    lane = lanes_of(BAND)
    small = lanes_of(8)

    def tail(at):
        out = jnp.zeros((8, W), F32)
        for q in range(4):
            moved = pltpu.roll(g[at + 8 * q : at + 8 * q + 8], (BAND * q - at) % W, 1)
            out = jnp.where(lax.shift_right_logical(small, 5) == q, moved, out)
        return out

    zero = jnp.where(lane < 3 * BAND, g[0:BAND], g[2 * BAND : 3 * BAND])
    one = jnp.where(lane >= BAND, g[BAND : 2 * BAND], g[3 * BAND :])
    return jnp.concatenate([zero, tail(2 * BAND)], axis=0), jnp.concatenate([one, tail(3 * BAND)], axis=0)


def unpack_symmetric(zero, one):
    lane = lanes_of(BAND)

    def tail(packed, at):
        return jnp.concatenate([pltpu.roll(packed[BAND:], (at - BAND * q) % W, 1) for q in range(4)], axis=0)

    two = jnp.where(lane >= 3 * BAND, zero[0:BAND], tail(zero, 2 * BAND))
    three = jnp.where(lane < BAND, one[0:BAND], tail(one, 3 * BAND))
    half = jnp.concatenate([zero[0:BAND], one[0:BAND], two, three], axis=0)
    i = lax.shift_right_logical(lax.broadcasted_iota(jnp.int32, (W, W), 0), 5)
    j = lax.shift_right_logical(lax.broadcasted_iota(jnp.int32, (W, W), 1), 5)
    ahead = (j - i) & 3
    return jnp.where((ahead < 2) | ((ahead == 2) & (i < 2)), half, half.T)


def finish_two_kernel(
    list_ref, cnt_ref, info_ref, hs_ref, buf_ref, first_ref, v_ref, acc_in,
    out_ref, keep_ref, send_ref, v12_ref, v3_ref,
):
    add_list(3, GROUP, (AT_D,), (buf_ref,), list_ref, cnt_ref, hs_ref, v12_ref, v3_ref, out_ref)
    biggest = jnp.zeros((BS, W), F32)
    for r in range(RB):
        second = 2.0 * (out_ref[r] - 0.5 * first_ref[r]) - v_ref[r]
        out_ref[r] = second
        biggest = jnp.maximum(biggest, jnp.abs(second))
    biggest = jnp.max(biggest, axis=0, keepdims=True)
    scale, inverse = power_scale(jnp.broadcast_to(biggest, (8, W)))
    scaled = out_ref[...].reshape(RB * BS, W) * inverse[0:1]
    terms = gram_of_digits(digits(scaled, 7, 4), 7)
    hi = terms[0]
    lo = jnp.zeros_like(hi)
    for t in terms[1:]:
        hi, e = two_sum(hi, t)
        lo = lo + e
    wide = jnp.broadcast_to(scale[0:1], (W, W))
    both = wide.T
    core = info_ref[9]
    for i, part in enumerate((hi, lo)):
        zero, one = pack_symmetric((part * wide) * both)
        keep_ref[i] = jnp.where(core == 0, zero, one)
        send_ref[i] = jnp.where(core == 0, one, zero)


def finish_two(lists, cnt, info, hs, buf, first, v, acc):
    return pl.pallas_call(
        finish_two_kernel,
        in_specs=[SM] * 3 + [VM] * 5,
        out_specs=[VM] * 3,
        out_shape=[pltpu.VMEM((RB, BS, W), F32)] + [pltpu.VMEM((2, PACKED, W), F32)] * 2,
        scratch_shapes=TABLE,
        input_output_aliases={7: 0},
        compiler_params=pltpu.CompilerParams(vmem_limit_bytes=VMEM_LIMIT),
        cost_estimate=pl.CostEstimate(flops=NE * 2 * BS**3, bytes_accessed=8 * 2**20, transcendentals=0),
        name="finish_two",
    )(lists, cnt, info, on_chip(hs), on_chip(buf), on_chip(first), on_chip(v), on_chip(acc))


def eliminate(G):
    ri = lax.broadcasted_iota(jnp.int32, (8, W), 0)
    ci = lax.broadcasted_iota(jnp.int32, (8, W), 1)
    nb = W // 8
    A = [G[8 * b : 8 * b + 8, :] for b in range(nb)]
    B = [(ci == ri + 8 * b).astype(F32) for b in range(nb)]
    upper, lower_inv = [], []
    for k in range(nb):
        lanes = [jnp.broadcast_to(A[k][:, 8 * k + c : 8 * k + c + 1], (8, W)) for c in range(8)]
        d = [[jnp.broadcast_to(lanes[c][m : m + 1, :], (8, W)) for c in range(m + 1)] for m in range(8)]
        ra = [jnp.broadcast_to(A[k][m : m + 1, :], (8, W)) for m in range(8)]
        rb = [jnp.broadcast_to(B[k][m : m + 1, :], (8, W)) for m in range(8)]
        cols = {b: [jnp.broadcast_to(A[b][:, 8 * k + c : 8 * k + c + 1], (8, W)) for c in range(8)] for b in range(k + 1, nb)}
        inv = [None] * 8
        l = [[None] * 8 for _ in range(8)]
        for i in range(8):
            inv[i] = 1.0 / d[i][i]
            for m in range(i + 1, 8):
                l[m][i] = d[m][i] * inv[i]
                for c in range(i + 1, m + 1):
                    d[m][c] = d[m][c] - l[m][i] * d[c][i]
            for m in range(i + 1, 8):
                ra[m] = ra[m] - l[m][i] * ra[i]
                rb[m] = rb[m] - l[m][i] * rb[i]
        sa = [ra[i] * inv[i] for i in range(8)]
        sb = [rb[i] * inv[i] for i in range(8)]
        for b in range(k + 1, nb):
            c = cols[b]
            for i in range(8):
                for j in range(i):
                    c[i] = c[i] - l[i][j] * c[j]
                A[b] = A[b] - c[i] * sa[i]
                B[b] = B[b] - c[i] * sb[i]
        pa, pb, pd = ra[0], rb[0], d[0][0]
        for m in range(1, 8):
            pa = jnp.where(ri == m, ra[m], pa)
            pb = jnp.where(ri == m, rb[m], pb)
            pd = jnp.where(ri == m, d[m][m], pd)
        s = 1.0 / jnp.sqrt(pd)
        upper.append(jnp.where(ci >= ri + 8 * k, pa * s, 0.0))
        lower_inv.append(jnp.where(ci <= ri + 8 * k, pb * s, 0.0))
    return jnp.concatenate(upper, axis=0), jnp.concatenate(lower_inv, axis=0)


def dot(a, b, ca, cb):
    return lax.dot_general(a, b, (((ca,), (cb,)), ((), ())), preferred_element_type=F32)


def mm1(a, b, ca=1, cb=0):
    return dot(a.astype(BF16), b.astype(BF16), ca, cb)


def mm3(a, b, ca=1, cb=0):
    ah, al = pieces(a, 2)
    bh, bl = pieces(b, 2)
    return dot(jnp.concatenate([al, ah, ah], axis=ca), jnp.concatenate([bh, bl, bh], axis=cb), ca, cb)


def mm6(a, b, ca=1, cb=0):
    ah, am, al = pieces(a)
    bh, bm, bl = pieces(b)
    return dot(
        jnp.concatenate([al, ah, am, am, ah, ah], axis=ca), jnp.concatenate([bh, bl, bm, bh, bm, bh], axis=cb), ca, cb
    )


def factor_kernel(total, info_ref, kept_ref, other_ref, inv_ref, factor_ref):
    ri = lax.broadcasted_iota(jnp.int32, (W, W), 0)
    ci = lax.broadcasted_iota(jnp.int32, (W, W), 1)
    eye = (ri == ci).astype(F32)

    def half_lower(x):
        return jnp.where(ri > ci, x, jnp.where(ri == ci, 0.5 * x, 0.0))

    core = info_ref[9]
    hi, lo = [
        unpack_symmetric(
            jnp.where(core == 0, kept_ref[i], other_ref[i]), jnp.where(core == 0, other_ref[i], kept_ref[i])
        )
        * (1.0 / total)
        for i in range(2)
    ]
    upper, linv = eliminate(hi)

    norm = jnp.sqrt(jnp.sum(hi * eye, axis=0, keepdims=True))
    scale, inverse = power_scale(jnp.broadcast_to(norm, (8, W)))
    wide, wide_inv = jnp.broadcast_to(scale[0:1], (W, W)), jnp.broadcast_to(inverse[0:1], (W, W))
    tall, tall_inv = wide.T, wide_inv.T
    rest = (hi * wide_inv) * tall_inv
    small = (lo * wide_inv) * tall_inv
    for t in gram_of_digits(digits(upper * wide_inv, 8, 4), 8):
        rest, e = two_sum(rest, -t)
        small = small + e
    rest = ((rest + small) * wide) * tall

    off = mm3(mm3(linv, rest), linv, 1, 1)
    defect = eye - mm6(linv, upper, 1, 1)
    close = jnp.sum(off * off) < 1e-5

    @pl.when(close)
    def _():
        x = half_lower(off)
        z = mm1(x, x - defect) + defect
        x = half_lower(off - mm1(x, x, 1, 1))
        inv_ref[...] = linv + mm3(z - x, linv)
        factor_ref[...] = upper + mm3(x, upper, 0, 0)

    @pl.when(jnp.logical_not(close))
    def _():
        u2, l2 = eliminate(eye + off)
        factor = mm6(u2, upper)
        inv = mm6(l2, linv)
        inv_ref[...] = inv + mm6(eye - mm6(inv, factor, 1, 1), inv)
        factor_ref[...] = factor


def factors(info, kept, other, total):
    return pl.pallas_call(
        functools.partial(factor_kernel, float(total)),
        in_specs=[SM, VM, VM],
        out_specs=[VM, VM],
        out_shape=[pltpu.VMEM((W, W), F32), jax.ShapeDtypeStruct((W, W), F32)],
        compiler_params=pltpu.CompilerParams(vmem_limit_bytes=VMEM_LIMIT),
        name="factors",
    )(info, kept, other)


def basis_kernel(s_ref, t_ref, out_ref):
    i = pl.program_id(0)
    out_ref[...] = mm6(s_ref[pl.ds(i * 4, 4)].reshape(4 * BS, W), t_ref[...], 1, 1)


def basis_of(second, inv):
    return pl.pallas_call(
        basis_kernel,
        grid=(RB // 4,),
        in_specs=[VM, VM],
        out_specs=pl.BlockSpec((4 * BS, W), lambda i: (i, 0)),
        out_shape=jax.ShapeDtypeStruct((RB * BS, W), F32),
        compiler_params=pltpu.CompilerParams(vmem_limit_bytes=VMEM_LIMIT),
        name="basis",
    )(on_chip(second), on_chip(inv))


def shards(vectors, hblocks, local_cols, ghost_lists):
    count = lax.axis_size("rows")
    me = lax.axis_index("rows")
    chips = count // 2
    core = me % 2
    odd = (me // 2) % 2

    def to_chip(i, by):
        return ((i // 2 + by) % chips) * 2 + i % 2

    pair_c = [(i, i ^ 1) for i in range(count)]
    pair_a = [(i, to_chip(i, 1 if (i // 2) % 2 == 0 else -1)) for i in range(count)]
    pair_b = [(i, to_chip(i, -1 if (i // 2) % 2 == 0 else 1)) for i in range(count)]
    pair_d = [(i, (i + (1 if i % 2 else -1)) % count) for i in range(count)]

    mine = lax.dynamic_index_in_dim(ghost_lists, me, 0, keepdims=False)
    info = jnp.stack(
        [
            1 + core,
            3 * odd,
            3 - 3 * odd,
            2 - core,
            jnp.zeros_like(me),
            jnp.where(odd == 1, AT_A, AT_B) - 16,
            jnp.where(core == 1, AT_C, AT_D) - 24,
            jnp.where(core == 1, AT_D, AT_C) - 32,
            jnp.where(odd == 1, AT_B, AT_A) - 40,
            core,
        ]
    ).astype(jnp.int32)

    v = vectors.reshape(RB, BS, W)
    move = functools.partial(lax.ppermute, axis_name="rows")

    def exchange(packs):
        return [move(x, perm=perm) for x, perm in zip(packs, (pair_c, pair_a, pair_b, pair_d))]

    v, *packs = pack(info, mine, v)
    c, a, b, d = exchange(packs)
    hs, lists, cnt = convert(hblocks, local_cols, info)
    acc = run_phase(0, 2 * GROUP, (OWN, AT_C), lists, cnt, hs, [v, c])
    first, *packs = finish_one(lists, cnt, info, mine, hs, [a, b, d], v, acc)

    c, a, b, d = exchange(packs)
    acc = run_phase(0, 2 * GROUP, (OWN, AT_C), lists, cnt, hs, [first, c])
    acc = run_phase(1, GROUP, (AT_A,), lists, cnt, hs, [a], acc)
    acc = run_phase(2, GROUP, (AT_B,), lists, cnt, hs, [b], acc)
    second, kept, sent = finish_two(lists, cnt, info, hs, d, first, v, acc)

    theirs = move(sent, perm=pair_c)
    pair = pair_add(kept[0], kept[1], theirs[0], theirs[1])
    for shift in (1, 3, 5):
        for by in (1, 3):
            theirs = move(jnp.stack(pair), perm=[(i, i ^ (by << shift)) for i in range(count)])
            pair = pair_add(*pair, theirs[0], theirs[1])
    kept = jnp.stack(pair)
    inv, factor = factors(info, kept, move(kept, perm=pair_c), RB * BS * count)
    return basis_of(second, inv), factor


def solution(mesh):
    in_specs = (P("rows", None), P("rows", None, None, None), P("rows", None), P())
    out_specs = (P("rows", None), P())
    return jax.shard_map(shards, mesh=mesh, in_specs=in_specs, out_specs=out_specs, check_vma=False)
```

time: 1260 us -> 125 us (0.10)
  local copies, waits for them, and re-layouts: 371 us -> 0.99 us
  matrix products: 300 us -> 0 us
  waiting for transfers between devices: 319 us -> 31.5 us
  loops' own time: 198 us -> 0 us
  Pallas kernels: 0 us -> 70.5 us
  other arithmetic: 30.3 us -> 0.14 us
  between operations: 14.4 us -> 0.96 us
    dynamic_slice x512 -> x1, local copies, waits for them, and re-layouts: 313 us -> 0.21 us  [shards(): mine = lax.dynamic_index_in_dim(ghost_lists, me, 0, keepdims=False)]
    dot_general x519 -> x0, matrix products: 300 us -> none  [the longest x256 193 us: row_step(): jnp.dot(row_u, inverse, precision=lax.Precision.HIGHEST)]
    psum x2 -> x0, waiting for transfers between devices: 270 us -> none  [upper_factor(): gram = lax.psum(local_gram, 'rows') / total]
    another operation x4 -> x0, loops' own time: 198 us -> none  [the longest x2 190 us: lower_cholesky(): return lax.fori_loop(0, size, column_step, jnp.zeros_like(gram))]
    pallas_call x0 -> x10, Pallas kernels: none -> 70.5 us  [the longest x4 24.6 us: run_phase(): pl.pallas_call(functools.partial(phase_kernel, which, group, places, acc...]
    gather x10 -> x0, local copies, waits for them, and re-layouts: 38.1 us -> none  [the longest x8 20.8 us: extend(): parts.append(fetch_whole(blocks, -off)[theirs])]
    add x256 -> x0, other arithmetic: 21.7 us -> none  [column_step(): lower + column[:, None] * (index_all[None, :] == j).astype(gram.dtype)]
    ppermute x8 -> x16, waiting for transfers between devices: 48.6 us -> 31.5 us  [the longest x6 27.3 us: shards(): move(jnp.stack(pair), perm=[(i, i ^ by << shift) for i in range(count)])]
  transfers between devices with their start and end apart: 10 -> 16, of which waited for: 6 -> 10; matrix products, arithmetic and copies ran while one was open for 2% -> 0% of each run, Pallas kernels for 0% -> 31%
where the time goes in v2:
time: 125 us; the launch traced here: 123 us
  Pallas kernels  70.5 us (56%)
  waiting for transfers between devices  31.5 us (25%)
  starting transfers between devices  18.8 us (15%)
    ppermute x6, waiting for transfers between devices, shards(): move(jnp.stack(pair), perm=[(i, i ^ by << shift) for i in range(count)])  27.3 us
    pallas_call x4, Pallas kernels, run_phase(): pl.pallas_call(functools.partial(phase_kernel, which, group, places, acc...  24.6 us
    ppermute x8, starting transfers between devices, exchange(): move(x, perm=perm)  17.8 us
    pallas_call x1, Pallas kernels, convert(): pl.pallas_call(convert_kernel, in_specs=[SM, SM, ANY], out_specs=[VM, SM,...  13.2 us
    pallas_call x1, Pallas kernels, factors(): pl.pallas_call(functools.partial(factor_kernel, float(total)), in_specs=[...  12.4 us
    pallas_call x1, Pallas kernels, finish_one(): pl.pallas_call(finish_one_kernel, in_specs=[SM] * 4 + [VM] * 6, out_specs...  9.35 us
    pallas_call x1, Pallas kernels, finish_two(): pl.pallas_call(finish_two_kernel, in_specs=[SM] * 3 + [VM] * 5, out_specs...  6.28 us
    pallas_call x1, Pallas kernels, basis_of(): pl.pallas_call(basis_kernel, grid=(RB // 4,), in_specs=[VM, VM], out_spec...  2.56 us
  transfers between devices with their start and end apart: 16, of which 10 were waited for; matrix products, arithmetic and copies ran while one was open for 0% of the time, Pallas kernels for 31%

profile of v2, /device:TPU:0, one launch (start us, length us, event | category | flops | bytes accessed | tf_op | source)
XLA Modules:
  0.0 122.8 jit_solution(2331176033247758949)
XLA Ops:
  1.7 2.1 %pack.1 = (f32[16,128,128]{2,1,0:T(8,128)S(1)}, f32[8,128,128]{2,1,0:T(8,128)S(1)}, f32[8,128,128]{2,1,0:T(8,128)S(1)}, f32[8,128,128]{2,1,0:T(8,128)S(1)}, f32[8,128,128]{2,1,0:T(8,128)S(1)}) custom-call(s32[10]{0:T(128)S(1)} %stack.74.info_ref, s32[4,8]{1,0:T(4,128)S(1)} %dynamic-slice_reduce_fusion.lists_ref.mine_ref, f32[16,128,128]{2,1,0:T(8,128)} %bitcast.12), custom_call_target="tpu_custom_call" | custom-call | tf_op jit(solution)/shard_map/pack/pallas_call | solution.py:192
  3.8 2.1 %collective-permute-start = (f32[8,128,128]{2,1,0:T(8,128)S(1)}, f32[8,128,128]{2,1,0:T(8,128)S(1)}, u32[]{:S(2)}, u32[]{:S(2)}) collective-permute-start(f32[8,128,128]{2,1,0:T(8,128)S(1)} %get-tuple-element.23), channel_id=1, source_target_pairs={{0,2},{1,3},{2,0},{3,1},{4,6},{5,7},{6,4},{7,5},{8,10},{9,11},{10,... | collective-permute-start | bytes 1572872 | tf_op jit(solution)/shard_map/ppermute | solution.py:567
  5.9 7.2 %collective-permute-start.1 = (f32[8,128,128]{2,1,0:T(8,128)S(1)}, f32[8,128,128]{2,1,0:T(8,128)S(1)}, u32[]{:S(2)}, u32[]{:S(2)}) collective-permute-start(f32[8,128,128]{2,1,0:T(8,128)S(1)} %get-tuple-element.24), channel_id=1, source_target_pairs={{0,126},{1,127},{2,4},{3,5},{4,2},{5,3},{6,8},{7,9},{8,6},{9,7},{1... | collective-permute-start | bytes 1572872 | tf_op jit(solution)/shard_map/ppermute | solution.py:567
  13.1 13.2 %convert.1 = (bf16[320,384,128]{2,1,0:T(8,128)(2,1)S(1)}, s32[5,368]{1,0:T(8,128)}, s32[5]{0:T(128)}) custom-call(s32[16,20]{1,0:T(8,128)} %cols_ref.1, s32[10]{0:T(128)} %copy-done.2, f32[320,128,128]{2,1,0:T(8,128)} %bitcast.11), custom_call_target="tpu_custom_call" | custom-call | flops 2684354560 | bytes 20971520 | tf_op jit(solution)/shard_map/convert/pallas_call | solution.py:154
  26.3 8.3 %phase_0.2.acc_in = f32[16,128,128]{2,1,0:T(8,128)S(1)} custom-call(s32[5,368]{1,0:T(8,128)} %get-tuple-element.20.list_ref, s32[5]{0:T(128)} %get-tuple-element.21.cnt_ref, bf16[320,384,128]{2,1,0:T(8,128)(2,1)S(1)} %get-tuple-element.22.hs_ref, f32[16,128,128]{2,1,0:T(8,128)S(1)} %get-tuple-element.26.refs_0_.v_ref, ...), custom_call_target="tpu_custom_call" | custom-call | flops 2684354560 | bytes 4194304 | tf_op jit(solution)/shard_map/phase_0/pallas_call | solution.py:221
  34.7 9.4 %finish_one.1 = (f32[16,128,128]{2,1,0:T(8,128)S(1)}, f32[8,128,128]{2,1,0:T(8,128)S(1)}, f32[8,128,128]{2,1,0:T(8,128)}, f32[8,128,128]{2,1,0:T(8,128)S(1)}, f32[8,128,128]{2,1,0:T(8,128)S(1)}) custom-call(s32[5,368]{1,0:T(8,128)} %get-tuple-element.20.list_ref, s32[5]{0:T(128)} %get-tuple-element.21.cnt_ref, ...), custom_call_target="tpu_custom_call", output_to_operand_aliasing={{0}: (9, {})} | custom-call | flops 4026531840 | bytes 8388608 | tf_op jit(solution)/shard_map/finish_one/pallas_call | solution.py:248
  44.1 1.5 %collective-permute-start.6 = (f32[8,128,128]{2,1,0:T(8,128)}, f32[8,128,128]{2,1,0:T(8,128)S(1)}, u32[]{:S(2)}, u32[]{:S(2)}) collective-permute-start(f32[8,128,128]{2,1,0:T(8,128)} %get-tuple-element.31), channel_id=1, source_target_pairs={{0,2},{1,3},{2,0},{3,1},{4,6},{5,7},{6,4},{7,5},{8,10},{9,11},{10,... | collective-permute-start | bytes 1572872 | tf_op jit(solution)/shard_map/ppermute | solution.py:567
  45.6 6.1 %collective-permute-start.5 = (f32[8,128,128]{2,1,0:T(8,128)S(1)}, f32[8,128,128]{2,1,0:T(8,128)S(1)}, u32[]{:S(2)}, u32[]{:S(2)}) collective-permute-start(f32[8,128,128]{2,1,0:T(8,128)S(1)} %get-tuple-element.30), channel_id=1, source_target_pairs={{0,126},{1,127},{2,4},{3,5},{4,2},{5,3},{6,8},{7,9},{8,6},{9,7},{1... | collective-permute-start | bytes 1572872 | tf_op jit(solution)/shard_map/ppermute | solution.py:567
  51.6 0.9 collective-permute-start.4
  52.6 8.3 %phase_0.3.refs_1_ = f32[16,128,128]{2,1,0:T(8,128)S(1)} custom-call(s32[5,368]{1,0:T(8,128)} %get-tuple-element.20.list_ref, s32[5]{0:T(128)} %get-tuple-element.21.cnt_ref, bf16[320,384,128]{2,1,0:T(8,128)(2,1)S(1)} %get-tuple-element.22.hs_ref, f32[16,128,128]{2,1,0:T(8,128)S(1)} %get-tuple-element.29.refs_0_.first_ref, ...), custom_call_target="tpu_custom_call" | custom-call | flops 2684354560 | bytes 4194304 | tf_op jit(solution)/shard_map/phase_0/pallas_call | solution.py:221
  60.9 4.0 %phase_1.1.refs_1_ = f32[16,128,128]{2,1,0:T(8,128)S(1)} custom-call(s32[5,368]{1,0:T(8,128)} %get-tuple-element.20.list_ref, s32[5]{0:T(128)} %get-tuple-element.21.cnt_ref, bf16[320,384,128]{2,1,0:T(8,128)(2,1)S(1)} %get-tuple-element.22.hs_ref, f32[8,128,128]{2,1,0:T(8,128)S(1)} %collective-permute-done.6.refs_0_, ...), custom_call_target="tpu_custom_call", output_to_operand_aliasing={{}: (4, {})} | custom-call | flops 1342177280 | bytes 4194304 | tf_op jit(solution)/shard_map/phase_1/pallas_call | solution.py:221
  65.8 4.0 %phase_2.1.acc_in = f32[16,128,128]{2,1,0:T(8,128)S(1)} custom-call(s32[5,368]{1,0:T(8,128)} %get-tuple-element.20.list_ref, s32[5]{0:T(128)} %get-tuple-element.21.cnt_ref, bf16[320,384,128]{2,1,0:T(8,128)(2,1)S(1)} %get-tuple-element.22.hs_ref, f32[8,128,128]{2,1,0:T(8,128)S(1)} %collective-permute-done.5.refs_0_, ...), custom_call_target="tpu_custom_call", output_to_operand_aliasing={{}: (4, {})} | custom-call | flops 1342177280 | bytes 4194304 | tf_op jit(solution)/shard_map/phase_2/pallas_call | solution.py:221
  69.8 0.9 collective-permute-done.4.buf_ref
  70.7 6.3 %finish_two.1 = (f32[16,128,128]{2,1,0:T(8,128)S(1)}, f32[2,40,128]{2,1,0:T(8,128)S(1)}, f32[2,40,128]{2,1,0:T(8,128)S(1)}) custom-call(s32[5,368]{1,0:T(8,128)} %get-tuple-element.20.list_ref, s32[5]{0:T(128)} %get-tuple-element.21.cnt_ref, s32[10]{0:T(128)} %copy-done.2, ...), custom_call_target="tpu_custom_call", output_to_operand_aliasing={{0}: (7, {})} | custom-call | flops 1342177280 | bytes 8388608 | tf_op jit(solution)/shard_map/finish_two/pallas_call | solution.py:375
  77.1 1.2 collective-permute-done.8
  78.4 4.0 %collective-permute-done.9 = f32[2,40,128]{2,1,0:T(8,128)S(1)} collective-permute-done((f32[2,40,128]{2,1,0:T(8,128)S(1)}, f32[2,40,128]{2,1,0:T(8,128)S(1)}, u32[]{:S(2)}, u32[]{:S(2)}) %collective-permute-start.9) | collective-permute-done | bytes 40992 | tf_op jit(solution)/shard_map/ppermute | solution.py:585
  82.5 5.2 %collective-permute-done.10 = f32[2,40,128]{2,1,0:T(8,128)S(1)} collective-permute-done((f32[2,40,128]{2,1,0:T(8,128)S(1)}, f32[2,40,128]{2,1,0:T(8,128)S(1)}, u32[]{:S(2)}, u32[]{:S(2)}) %collective-permute-start.10) | collective-permute-done | bytes 40992 | tf_op jit(solution)/shard_map/ppermute | solution.py:585
  87.8 4.0 %collective-permute-done.11 = f32[2,40,128]{2,1,0:T(8,128)S(1)} collective-permute-done((f32[2,40,128]{2,1,0:T(8,128)S(1)}, f32[2,40,128]{2,1,0:T(8,128)S(1)}, u32[]{:S(2)}, u32[]{:S(2)}) %collective-permute-start.11) | collective-permute-done | bytes 40992 | tf_op jit(solution)/shard_map/ppermute | solution.py:585
  91.9 5.2 %collective-permute-done.12 = f32[2,40,128]{2,1,0:T(8,128)S(1)} collective-permute-done((f32[2,40,128]{2,1,0:T(8,128)S(1)}, f32[2,40,128]{2,1,0:T(8,128)S(1)}, u32[]{:S(2)}, u32[]{:S(2)}) %collective-permute-start.12) | collective-permute-done | bytes 40992 | tf_op jit(solution)/shard_map/ppermute | solution.py:585
  97.3 4.0 %collective-permute-done.13 = f32[2,40,128]{2,1,0:T(8,128)S(1)} collective-permute-done((f32[2,40,128]{2,1,0:T(8,128)S(1)}, f32[2,40,128]{2,1,0:T(8,128)S(1)}, u32[]{:S(2)}, u32[]{:S(2)}) %collective-permute-start.13) | collective-permute-done | bytes 40992 | tf_op jit(solution)/shard_map/ppermute | solution.py:585
  101.6 5.0 %collective-permute-done.14 = f32[2,40,128]{2,1,0:T(8,128)S(1)} collective-permute-done((f32[2,40,128]{2,1,0:T(8,128)S(1)}, f32[2,40,128]{2,1,0:T(8,128)S(1)}, u32[]{:S(2)}, u32[]{:S(2)}) %collective-permute-start.14) | collective-permute-done | bytes 40992 | tf_op jit(solution)/shard_map/ppermute | solution.py:585
  106.7 1.2 collective-permute-done.15.other_ref
  107.9 12.4 %factors.1 = (f32[128,128]{1,0:T(8,128)S(1)}, f32[128,128]{1,0:T(8,128)}) custom-call(s32[10]{0:T(128)S(1)} %copy-done.3, f32[2,40,128]{2,1,0:T(8,128)S(1)} %pad_maximum_fusion.6.kept_ref, f32[2,40,128]{2,1,0:T(8,128)S(1)} %collective-permute-done.15.other_ref), custom_call_target="tpu_custom_call" | custom-call | tf_op jit(solution)/shard_map/factors/pallas_call | solution.py:505
  120.3 2.6 %basis.1 = f32[2048,128]{1,0:T(8,128)} custom-call(f32[16,128,128]{2,1,0:T(8,128)S(1)} %get-tuple-element.33.s_ref, f32[128,128]{1,0:T(8,128)S(1)} %get-tuple-element.36.t_ref), custom_call_target="tpu_custom_call" | custom-call | tf_op jit(solution)/shard_map/basis/pallas_call | solution.py:521
  (44 shorter events, 3.0 us)
Async XLA Ops:
  0.6 0.7 copy-start
  1.6 33.1 %copy-start.4 = (s32[4,8]{1,0:T(4,128)}, s32[4,8]{1,0:T(4,128)S(1)}, u32[]{:S(2)}) copy-start(s32[4,8]{1,0:T(4,128)S(1)} %dynamic-slice_reduce_fusion.lists_ref.mine_ref) | copy-start | bytes 388
  1.7 11.4 %copy-start.2 = (s32[10]{0:T(128)}, s32[10]{0:T(128)S(1)}, u32[]{:S(2)}) copy-start(s32[10]{0:T(128)S(1)} %stack.74.info_ref) | copy-start | bytes 124
  3.7 22.6 %collective-permute-start.3 = (f32[8,128,128]{2,1,0:T(8,128)S(1)}, f32[8,128,128]{2,1,0:T(8,128)S(1)}, u32[]{:S(2)}, u32[]{:S(2)}) collective-permute-start(f32[8,128,128]{2,1,0:T(8,128)S(1)} %get-tuple-element.27), channel_id=1, source_target_pairs={{0,1},{1,0},{2,3},{3,2},{4,5},{5,4},{6,7},{7,6},{8,9},{9,8},{10,11... | collective-permute-start | bytes 1572872 | tf_op jit(solution)/shard_map/ppermute | solution.py:567
  3.8 30.9 %collective-permute-start = (f32[8,128,128]{2,1,0:T(8,128)S(1)}, f32[8,128,128]{2,1,0:T(8,128)S(1)}, u32[]{:S(2)}, u32[]{:S(2)}) collective-permute-start(f32[8,128,128]{2,1,0:T(8,128)S(1)} %get-tuple-element.23), channel_id=1, source_target_pairs={{0,2},{1,3},{2,0},{3,1},{4,6},{5,7},{6,4},{7,5},{8,10},{9,11},{10,... | collective-permute-start | bytes 1572872 | tf_op jit(solution)/shard_map/ppermute | solution.py:567
  5.9 28.8 %collective-permute-start.1 = (f32[8,128,128]{2,1,0:T(8,128)S(1)}, f32[8,128,128]{2,1,0:T(8,128)S(1)}, u32[]{:S(2)}, u32[]{:S(2)}) collective-permute-start(f32[8,128,128]{2,1,0:T(8,128)S(1)} %get-tuple-element.24), channel_id=1, source_target_pairs={{0,126},{1,127},{2,4},{3,5},{4,2},{5,3},{6,8},{7,9},{8,6},{9,7},{1... | collective-permute-start | bytes 1572872 | tf_op jit(solution)/shard_map/ppermute | solution.py:567
  13.1 21.6 %collective-permute-start.2 = (f32[8,128,128]{2,1,0:T(8,128)S(1)}, f32[8,128,128]{2,1,0:T(8,128)S(1)}, u32[]{:S(2)}, u32[]{:S(2)}) collective-permute-start(f32[8,128,128]{2,1,0:T(8,128)S(1)} %get-tuple-element.25), channel_id=1, source_target_pairs={{0,127},{1,2},{2,1},{3,4},{4,3},{5,6},{6,5},{7,8},{8,7},{9,10},{10... | collective-permute-start | bytes 1572872 | tf_op jit(solution)/shard_map/ppermute | solution.py:567
  44.1 8.5 %collective-permute-start.7 = (f32[8,128,128]{2,1,0:T(8,128)S(1)}, f32[8,128,128]{2,1,0:T(8,128)S(1)}, u32[]{:S(2)}, u32[]{:S(2)}) collective-permute-start(f32[8,128,128]{2,1,0:T(8,128)S(1)} %get-tuple-element.32), channel_id=1, source_target_pairs={{0,1},{1,0},{2,3},{3,2},{4,5},{5,4},{6,7},{7,6},{8,9},{9,8},{10,11... | collective-permute-start | bytes 1572872 | tf_op jit(solution)/shard_map/ppermute | solution.py:567
  44.1 16.8 %collective-permute-start.6 = (f32[8,128,128]{2,1,0:T(8,128)}, f32[8,128,128]{2,1,0:T(8,128)S(1)}, u32[]{:S(2)}, u32[]{:S(2)}) collective-permute-start(f32[8,128,128]{2,1,0:T(8,128)} %get-tuple-element.31), channel_id=1, source_target_pairs={{0,2},{1,3},{2,0},{3,1},{4,6},{5,7},{6,4},{7,5},{8,10},{9,11},{10,... | collective-permute-start | bytes 1572872 | tf_op jit(solution)/shard_map/ppermute | solution.py:567
  45.6 20.2 %collective-permute-start.5 = (f32[8,128,128]{2,1,0:T(8,128)S(1)}, f32[8,128,128]{2,1,0:T(8,128)S(1)}, u32[]{:S(2)}, u32[]{:S(2)}) collective-permute-start(f32[8,128,128]{2,1,0:T(8,128)S(1)} %get-tuple-element.30), channel_id=1, source_target_pairs={{0,126},{1,127},{2,4},{3,5},{4,2},{5,3},{6,8},{7,9},{8,6},{9,7},{1... | collective-permute-start | bytes 1572872 | tf_op jit(solution)/shard_map/ppermute | solution.py:567
  51.6 19.0 %collective-permute-start.4 = (f32[8,128,128]{2,1,0:T(8,128)S(1)}, f32[8,128,128]{2,1,0:T(8,128)S(1)}, u32[]{:S(2)}, u32[]{:S(2)}) collective-permute-start(f32[8,128,128]{2,1,0:T(8,128)S(1)} %get-tuple-element.28), channel_id=1, source_target_pairs={{0,127},{1,2},{2,1},{3,4},{4,3},{5,6},{6,5},{7,8},{8,7},{9,10},{10... | collective-permute-start | bytes 1572872 | tf_op jit(solution)/shard_map/ppermute | solution.py:567
  60.9 61.9 %copy-start.1 = (s32[128,4,8]{0,2,1:T(8,128)S(1)}, s32[128,4,8]{0,2,1:T(8,128)}, u32[]{:S(2)}) copy-start(s32[128,4,8]{0,2,1:T(8,128)} %param.7) | copy-start | bytes 49156
  64.9 43.0 %copy-start.3 = (s32[10]{0:T(128)S(1)}, s32[10]{0:T(128)}, u32[]{:S(2)}) copy-start(s32[10]{0:T(128)} %copy-done.2) | copy-start | bytes 124
  77.0 1.3 %collective-permute-start.8 = (f32[2,40,128]{2,1,0:T(8,128)S(1)}, f32[2,40,128]{2,1,0:T(8,128)S(1)}, u32[]{:S(2)}, u32[]{:S(2)}) collective-permute-start(f32[2,40,128]{2,1,0:T(8,128)S(1)} %get-tuple-element.35), channel_id=1, source_target_pairs={{0,1},{1,0},{2,3},{3,2},{4,5},{5,4},{6,7},{7,6},{8,9},{9,8},{10,11... | collective-permute-start | bytes 122888 | tf_op jit(solution)/shard_map/ppermute | solution.py:581
  78.3 4.1 %collective-permute-start.9 = (f32[2,40,128]{2,1,0:T(8,128)S(1)}, f32[2,40,128]{2,1,0:T(8,128)S(1)}, u32[]{:S(2)}, u32[]{:S(2)}) collective-permute-start(f32[2,40,128]{2,1,0:T(8,128)S(1)} %pad_maximum_fusion), channel_id=1, source_target_pairs={{0,2},{1,3},{2,0},{3,1},{4,6},{5,7},{6,4},{7,5},{8,10},{9,11},{10,... | collective-permute-start | bytes 122888 | tf_op jit(solution)/shard_map/ppermute | solution.py:585
  82.4 5.3 %collective-permute-start.10 = (f32[2,40,128]{2,1,0:T(8,128)S(1)}, f32[2,40,128]{2,1,0:T(8,128)S(1)}, u32[]{:S(2)}, u32[]{:S(2)}) collective-permute-start(f32[2,40,128]{2,1,0:T(8,128)S(1)} %pad_maximum_fusion.1), channel_id=1, source_target_pairs={{0,6},{1,7},{2,4},{3,5},{4,2},{5,3},{6,0},{7,1},{8,14},{9,15},{10,... | collective-permute-start | bytes 122888 | tf_op jit(solution)/shard_map/ppermute | solution.py:585
  87.7 4.1 %collective-permute-start.11 = (f32[2,40,128]{2,1,0:T(8,128)S(1)}, f32[2,40,128]{2,1,0:T(8,128)S(1)}, u32[]{:S(2)}, u32[]{:S(2)}) collective-permute-start(f32[2,40,128]{2,1,0:T(8,128)S(1)} %pad_maximum_fusion.2), channel_id=1, source_target_pairs={{0,8},{1,9},{2,10},{3,11},{4,12},{5,13},{6,14},{7,15},{8,0},{9,1},... | collective-permute-start | bytes 122888 | tf_op jit(solution)/shard_map/ppermute | solution.py:585
  91.8 5.3 %collective-permute-start.12 = (f32[2,40,128]{2,1,0:T(8,128)S(1)}, f32[2,40,128]{2,1,0:T(8,128)S(1)}, u32[]{:S(2)}, u32[]{:S(2)}) collective-permute-start(f32[2,40,128]{2,1,0:T(8,128)S(1)} %pad_maximum_fusion.3), channel_id=1, source_target_pairs={{0,24},{1,25},{2,26},{3,27},{4,28},{5,29},{6,30},{7,31},{8,16},{9,... | collective-permute-start | bytes 122888 | tf_op jit(solution)/shard_map/ppermute | solution.py:585
  97.2 4.1 %collective-permute-start.13 = (f32[2,40,128]{2,1,0:T(8,128)S(1)}, f32[2,40,128]{2,1,0:T(8,128)S(1)}, u32[]{:S(2)}, u32[]{:S(2)}) collective-permute-start(f32[2,40,128]{2,1,0:T(8,128)S(1)} %pad_maximum_fusion.4), channel_id=1, source_target_pairs={{0,32},{1,33},{2,34},{3,35},{4,36},{5,37},{6,38},{7,39},{8,40},{9,... | collective-permute-start | bytes 122888 | tf_op jit(solution)/shard_map/ppermute | solution.py:585
  101.3 5.3 %collective-permute-start.14 = (f32[2,40,128]{2,1,0:T(8,128)S(1)}, f32[2,40,128]{2,1,0:T(8,128)S(1)}, u32[]{:S(2)}, u32[]{:S(2)}) collective-permute-start(f32[2,40,128]{2,1,0:T(8,128)S(1)} %pad_maximum_fusion.5), channel_id=1, source_target_pairs={{0,96},{1,97},{2,98},{3,99},{4,100},{5,101},{6,102},{7,103},{8,104... | collective-permute-start | bytes 122888 | tf_op jit(solution)/shard_map/ppermute | solution.py:585
  106.6 1.3 %collective-permute-start.15 = (f32[2,40,128]{2,1,0:T(8,128)S(1)}, f32[2,40,128]{2,1,0:T(8,128)S(1)}, u32[]{:S(2)}, u32[]{:S(2)}) collective-permute-start(f32[2,40,128]{2,1,0:T(8,128)S(1)} %pad_maximum_fusion.6.kept_ref), channel_id=1, source_target_pairs={{0,1},{1,0},{2,3},{3,2},{4,5},{5,4},{6,7},{7,6},{8,9},{9,8},{10,11... | collective-permute-start | bytes 122888 | tf_op jit(solution)/shard_map/ppermute | solution.py:588

commit v3 on v2

--- a/solution.py
+++ b/solution.py
@@ -103,13 +103,21 @@
 
     for i in range(FETCHES):
         fetch(i, i).start()
-    def list_row(r, counts):
+    def part(i, counts):
+        slot = lax.rem(i, FETCHES)
+        r = lax.div(i, NNZB // FETCH)
         counts = list(counts)
-        for n in range(NNZB):
-            col = cols_ref[r, n]
+        fetch(i, slot).wait()
+        for n in range(FETCH):
+            e = i * FETCH + n
+            hi, mid, lo = pieces(buf_ref[slot, n])
+            hs_ref[e, 0:BS, :] = hi
+            hs_ref[e, BS : 2 * BS, :] = mid
+            hs_ref[e, 2 * BS : 3 * BS, :] = lo
+            col = cols_ref[r, e - r * NNZB]
             kind = jnp.where(col < RB, 0, 1 + lax.shift_right_logical(col - RB, 3))
             v = col + info_ref[4 + kind]
-            code = r * 65536 + (r * NNZB + n) * 64 + v
+            code = r * 65536 + e * 64 + v
             source = lax.shift_right_logical(v, 3)
             mine = [source < 3, source == 3, source == 4, source == 5]
             at = jnp.where(mine[0], counts[0], jnp.where(mine[1], counts[1], jnp.where(mine[2], counts[2], counts[3])))
@@ -117,34 +125,22 @@
             list_ref[A_B_D, counts[4]] = code
             for p, yes in enumerate((*mine, source >= 3)):
                 counts[p] = counts[p] + yes.astype(jnp.int32)
+
+        @pl.when(i + FETCHES < NE // FETCH)
+        def _():
+            fetch(i + FETCHES, slot).start()
+
+        last = ((i + 1) * FETCH == (r + 1) * NNZB).astype(jnp.int32)
         for p in range(LISTS):
             list_ref[p, counts[p]] = r * 65536 + VZERO
-            counts[p] = counts[p] + (counts[p] & 1)
+            counts[p] = counts[p] + (counts[p] & last)
         return tuple(counts)
 
-    counts = lax.fori_loop(0, RB, list_row, (jnp.int32(0),) * LISTS)
+    counts = lax.fori_loop(0, NE // FETCH, part, (jnp.int32(0),) * LISTS)
     for p in range(LISTS):
         cnt_ref[p] = counts[p]
         for i in range(2 * GROUP):
             list_ref[p, counts[p] + i] = VZERO
-
-    def part(i, carry):
-        slot = lax.rem(i, FETCHES)
-        fetch(i, slot).wait()
-        for n in range(FETCH):
-            e = i * FETCH + n
-            hi, mid, lo = pieces(buf_ref[slot, n])
-            hs_ref[e, 0:BS, :] = hi
-            hs_ref[e, BS : 2 * BS, :] = mid
-            hs_ref[e, 2 * BS : 3 * BS, :] = lo
-
-        @pl.when(i + FETCHES < NE // FETCH)
-        def _():
-            fetch(i + FETCHES, slot).start()
-
-        return carry
-
-    lax.fori_loop(0, NE // FETCH, part, 0)
 
 
 TABLE = [pltpu.VMEM((VZERO + 1, BS, 2 * W), BF16), pltpu.VMEM((VZERO + 1, BS, W), BF16)]
@@ -451,7 +447,7 @@
     )
 
 
-def factor_kernel(total, info_ref, kept_ref, other_ref, inv_ref, factor_ref):
+def factor_kernel(total, zero_ref, one_ref, inv_ref, factor_ref):
     ri = lax.broadcasted_iota(jnp.int32, (W, W), 0)
     ci = lax.broadcasted_iota(jnp.int32, (W, W), 1)
     eye = (ri == ci).astype(F32)
@@ -459,14 +455,7 @@
     def half_lower(x):
         return jnp.where(ri > ci, x, jnp.where(ri == ci, 0.5 * x, 0.0))
 
-    core = info_ref[9]
-    hi, lo = [
-        unpack_symmetric(
-            jnp.where(core == 0, kept_ref[i], other_ref[i]), jnp.where(core == 0, other_ref[i], kept_ref[i])
-        )
-        * (1.0 / total)
-        for i in range(2)
-    ]
+    hi, lo = [unpack_symmetric(zero_ref[i], one_ref[i]) * (1.0 / total) for i in range(2)]
     upper, linv = eliminate(hi)
 
     norm = jnp.sqrt(jnp.sum(hi * eye, axis=0, keepdims=True))
@@ -501,28 +490,28 @@
         factor_ref[...] = factor
 
 
-def factors(info, kept, other, total):
+def factors(zero, one, total):
     return pl.pallas_call(
         functools.partial(factor_kernel, float(total)),
-        in_specs=[SM, VM, VM],
+        in_specs=[VM, VM],
         out_specs=[VM, VM],
         out_shape=[pltpu.VMEM((W, W), F32), jax.ShapeDtypeStruct((W, W), F32)],
         compiler_params=pltpu.CompilerParams(vmem_limit_bytes=VMEM_LIMIT),
         name="factors",
-    )(info, kept, other)
+    )(on_chip(zero), on_chip(one))
 
 
 def basis_kernel(s_ref, t_ref, out_ref):
     i = pl.program_id(0)
-    out_ref[...] = mm6(s_ref[pl.ds(i * 4, 4)].reshape(4 * BS, W), t_ref[...], 1, 1)
+    out_ref[...] = mm6(s_ref[pl.ds(i * 8, 8)].reshape(8 * BS, W), t_ref[...], 1, 1)
 
 
 def basis_of(second, inv):
     return pl.pallas_call(
         basis_kernel,
-        grid=(RB // 4,),
+        grid=(RB // 8,),
         in_specs=[VM, VM],
-        out_specs=pl.BlockSpec((4 * BS, W), lambda i: (i, 0)),
+        out_specs=pl.BlockSpec((8 * BS, W), lambda i: (i, 0)),
         out_shape=jax.ShapeDtypeStruct((RB * BS, W), F32),
         compiler_params=pltpu.CompilerParams(vmem_limit_bytes=VMEM_LIMIT),
         name="basis",
@@ -581,11 +570,14 @@
     theirs = move(sent, perm=pair_c)
     pair = pair_add(kept[0], kept[1], theirs[0], theirs[1])
     for shift in (1, 3, 5):
-        for by in (1, 3):
-            theirs = move(jnp.stack(pair), perm=[(i, i ^ (by << shift)) for i in range(count)])
-            pair = pair_add(*pair, theirs[0], theirs[1])
+        mine = jnp.stack(pair)
+        one, three, two = [move(mine, perm=[(i, i ^ (by << shift)) for i in range(count)]) for by in (1, 3, 2)]
+        pair = pair_add(*pair_add(*pair, one[0], one[1]), *pair_add(two[0], two[1], three[0], three[1]))
     kept = jnp.stack(pair)
-    inv, factor = factors(info, kept, move(kept, perm=pair_c), RB * BS * count)
+    other = move(kept, perm=pair_c)
+    first_core = core == 0
+    zero, one = jnp.where(first_core, kept, other), jnp.where(first_core, other, kept)
+    inv, factor = factors(zero, one, RB * BS * count)
     return basis_of(second, inv), factor
 
 

time: 125 us -> 116 us (0.928)
  waiting for transfers between devices: 31.5 us -> 12.8 us
  starting transfers between devices: 18.8 us -> 32.2 us
  Pallas kernels: 70.5 us -> 66.9 us
    ppermute x7 -> x10, waiting for transfers between devices: 28.5 us -> 10.6 us  [the longest x9 9.38 us: shards(): move(mine, perm=[(i, i ^ by << shift) for i in range(count)])]
    ppermute x7 -> x10, starting transfers between devices: 0.83 us -> 14.2 us  [the longest x9 14.1 us: shards(): move(mine, perm=[(i, i ^ by << shift) for i in range(count)])]
    pallas_call x1, Pallas kernels: 13.2 us -> 11.5 us  [convert(): pl.pallas_call(convert_kernel, in_specs=[SM, SM, ANY], out_specs=[VM, SM,...]
  transfers between devices with their start and end apart: 16 -> 19, of which waited for: 10 -> 12; matrix products, arithmetic and copies ran while one was open for 0% -> 0% of each run, Pallas kernels for 31% -> 32%
where the time goes in v3:
time: 116 us; the launch traced here: 114 us
  Pallas kernels  66.9 us (58%)
  starting transfers between devices  32.2 us (28%)
  waiting for transfers between devices  12.8 us (11%)
    pallas_call x4, Pallas kernels, run_phase(): pl.pallas_call(functools.partial(phase_kernel, which, group, places, acc...  25.4 us
    ppermute x8, starting transfers between devices, exchange(): move(x, perm=perm)  17.9 us
    ppermute x9, starting transfers between devices, shards(): move(mine, perm=[(i, i ^ by << shift) for i in range(count)])  14.1 us
    pallas_call x1, Pallas kernels, factors(): pl.pallas_call(functools.partial(factor_kernel, float(total)), in_specs=[...  11.8 us
    pallas_call x1, Pallas kernels, convert(): pl.pallas_call(convert_kernel, in_specs=[SM, SM, ANY], out_specs=[VM, SM,...  11.5 us
    ppermute x9, waiting for transfers between devices, shards(): move(mine, perm=[(i, i ^ by << shift) for i in range(count)])  9.38 us
    pallas_call x1, Pallas kernels, finish_one(): pl.pallas_call(finish_one_kernel, in_specs=[SM] * 4 + [VM] * 6, out_specs...  8.56 us
    pallas_call x1, Pallas kernels, finish_two(): pl.pallas_call(finish_two_kernel, in_specs=[SM] * 3 + [VM] * 5, out_specs...  5.57 us
  transfers between devices with their start and end apart: 19, of which 12 were waited for; matrix products, arithmetic and copies ran while one was open for 0% of the time, Pallas kernels for 32%

profile of v3, /device:TPU:0, one launch (start us, length us, event | category | flops | bytes accessed | tf_op | source)
XLA Modules:
  0.0 114.0 jit_solution(15363175044091353329)
XLA Ops:
  1.7 2.1 %pack.1 = (f32[16,128,128]{2,1,0:T(8,128)S(1)}, f32[8,128,128]{2,1,0:T(8,128)S(1)}, f32[8,128,128]{2,1,0:T(8,128)S(1)}, f32[8,128,128]{2,1,0:T(8,128)S(1)}, f32[8,128,128]{2,1,0:T(8,128)S(1)}) custom-call(s32[10]{0:T(128)S(1)} %stack.59.info_ref, s32[4,8]{1,0:T(4,128)S(1)} %dynamic-slice_reduce_fusion.lists_ref.mine_ref, f32[16,128,128]{2,1,0:T(8,128)} %bitcast.12), custom_call_target="tpu_custom_call" | custom-call | tf_op jit(solution)/shard_map/pack/pallas_call | solution.py:188
  3.8 2.1 %collective-permute-start = (f32[8,128,128]{2,1,0:T(8,128)S(1)}, f32[8,128,128]{2,1,0:T(8,128)S(1)}, u32[]{:S(2)}, u32[]{:S(2)}) collective-permute-start(f32[8,128,128]{2,1,0:T(8,128)S(1)} %get-tuple-element.23), channel_id=1, source_target_pairs={{0,2},{1,3},{2,0},{3,1},{4,6},{5,7},{6,4},{7,5},{8,10},{9,11},{10,... | collective-permute-start | bytes 1572872 | tf_op jit(solution)/shard_map/ppermute | solution.py:556
  5.9 7.2 %collective-permute-start.1 = (f32[8,128,128]{2,1,0:T(8,128)S(1)}, f32[8,128,128]{2,1,0:T(8,128)S(1)}, u32[]{:S(2)}, u32[]{:S(2)}) collective-permute-start(f32[8,128,128]{2,1,0:T(8,128)S(1)} %get-tuple-element.24), channel_id=1, source_target_pairs={{0,126},{1,127},{2,4},{3,5},{4,2},{5,3},{6,8},{7,9},{8,6},{9,7},{1... | collective-permute-start | bytes 1572872 | tf_op jit(solution)/shard_map/ppermute | solution.py:556
  13.1 11.5 %convert.1 = (bf16[320,384,128]{2,1,0:T(8,128)(2,1)S(1)}, s32[5,368]{1,0:T(8,128)}, s32[5]{0:T(128)}) custom-call(s32[16,20]{1,0:T(8,128)} %cols_ref.1, s32[10]{0:T(128)} %copy-done.5, f32[320,128,128]{2,1,0:T(8,128)} %bitcast.11), custom_call_target="tpu_custom_call" | custom-call | flops 2684354560 | bytes 20971520 | tf_op jit(solution)/shard_map/convert/pallas_call | solution.py:150
  24.6 8.3 %phase_0.2.acc_in = f32[16,128,128]{2,1,0:T(8,128)S(1)} custom-call(s32[5,368]{1,0:T(8,128)} %get-tuple-element.20.list_ref, s32[5]{0:T(128)} %get-tuple-element.21.cnt_ref, bf16[320,384,128]{2,1,0:T(8,128)(2,1)S(1)} %get-tuple-element.22.hs_ref, f32[16,128,128]{2,1,0:T(8,128)S(1)} %get-tuple-element.26.refs_0_.v_ref, ...), custom_call_target="tpu_custom_call" | custom-call | flops 2684354560 | bytes 4194304 | tf_op jit(solution)/shard_map/phase_0/pallas_call | solution.py:217
  33.0 8.6 %finish_one.1 = (f32[16,128,128]{2,1,0:T(8,128)S(1)}, f32[8,128,128]{2,1,0:T(8,128)S(1)}, f32[8,128,128]{2,1,0:T(8,128)S(1)}, f32[8,128,128]{2,1,0:T(8,128)S(1)}, f32[8,128,128]{2,1,0:T(8,128)S(1)}) custom-call(s32[5,368]{1,0:T(8,128)} %get-tuple-element.20.list_ref, s32[5]{0:T(128)} %get-tuple-element.21.cnt_ref, ...), custom_call_target="tpu_custom_call", output_to_operand_aliasing={{0}: (9, {})} | custom-call | flops 4026531840 | bytes 8388608 | tf_op jit(solution)/shard_map/finish_one/pallas_call | solution.py:244
  41.7 1.6 %collective-permute-start.6 = (f32[8,128,128]{2,1,0:T(8,128)S(1)}, f32[8,128,128]{2,1,0:T(8,128)S(1)}, u32[]{:S(2)}, u32[]{:S(2)}) collective-permute-start(f32[8,128,128]{2,1,0:T(8,128)S(1)} %get-tuple-element.31), channel_id=1, source_target_pairs={{0,2},{1,3},{2,0},{3,1},{4,6},{5,7},{6,4},{7,5},{8,10},{9,11},{10,... | collective-permute-start | bytes 1572872 | tf_op jit(solution)/shard_map/ppermute | solution.py:556
  43.3 5.4 %collective-permute-start.5 = (f32[8,128,128]{2,1,0:T(8,128)S(1)}, f32[8,128,128]{2,1,0:T(8,128)S(1)}, u32[]{:S(2)}, u32[]{:S(2)}) collective-permute-start(f32[8,128,128]{2,1,0:T(8,128)S(1)} %get-tuple-element.30), channel_id=1, source_target_pairs={{0,126},{1,127},{2,4},{3,5},{4,2},{5,3},{6,8},{7,9},{8,6},{9,7},{1... | collective-permute-start | bytes 1572872 | tf_op jit(solution)/shard_map/ppermute | solution.py:556
  48.7 1.5 %collective-permute-start.4 = (f32[8,128,128]{2,1,0:T(8,128)S(1)}, f32[8,128,128]{2,1,0:T(8,128)S(1)}, u32[]{:S(2)}, u32[]{:S(2)}) collective-permute-start(f32[8,128,128]{2,1,0:T(8,128)S(1)} %get-tuple-element.28), channel_id=1, source_target_pairs={{0,127},{1,2},{2,1},{3,4},{4,3},{5,6},{6,5},{7,8},{8,7},{9,10},{10... | collective-permute-start | bytes 1572872 | tf_op jit(solution)/shard_map/ppermute | solution.py:556
  50.2 8.3 %phase_0.3.refs_1_ = f32[16,128,128]{2,1,0:T(8,128)S(1)} custom-call(s32[5,368]{1,0:T(8,128)} %get-tuple-element.20.list_ref, s32[5]{0:T(128)} %get-tuple-element.21.cnt_ref, bf16[320,384,128]{2,1,0:T(8,128)(2,1)S(1)} %get-tuple-element.22.hs_ref, f32[16,128,128]{2,1,0:T(8,128)S(1)} %get-tuple-element.29.refs_0_.first_ref, ...), custom_call_target="tpu_custom_call" | custom-call | flops 2684354560 | bytes 4194304 | tf_op jit(solution)/shard_map/phase_0/pallas_call | solution.py:217
  58.6 4.7 %phase_1.1.refs_1_ = f32[16,128,128]{2,1,0:T(8,128)S(1)} custom-call(s32[5,368]{1,0:T(8,128)} %get-tuple-element.20.list_ref, s32[5]{0:T(128)} %get-tuple-element.21.cnt_ref, bf16[320,384,128]{2,1,0:T(8,128)(2,1)S(1)} %get-tuple-element.22.hs_ref, f32[8,128,128]{2,1,0:T(8,128)S(1)} %collective-permute-done.6.refs_0_, ...), custom_call_target="tpu_custom_call", output_to_operand_aliasing={{}: (4, {})} | custom-call | flops 1342177280 | bytes 4194304 | tf_op jit(solution)/shard_map/phase_1/pallas_call | solution.py:217
  63.5 4.0 %phase_2.1.acc_in = f32[16,128,128]{2,1,0:T(8,128)S(1)} custom-call(s32[5,368]{1,0:T(8,128)} %get-tuple-element.20.list_ref, s32[5]{0:T(128)} %get-tuple-element.21.cnt_ref, bf16[320,384,128]{2,1,0:T(8,128)(2,1)S(1)} %get-tuple-element.22.hs_ref, f32[8,128,128]{2,1,0:T(8,128)S(1)} %collective-permute-done.5.refs_0_, ...), custom_call_target="tpu_custom_call", output_to_operand_aliasing={{}: (4, {})} | custom-call | flops 1342177280 | bytes 4194304 | tf_op jit(solution)/shard_map/phase_2/pallas_call | solution.py:217
  68.3 5.6 %finish_two.1 = (f32[16,128,128]{2,1,0:T(8,128)S(1)}, f32[2,40,128]{2,1,0:T(8,128)S(1)}, f32[2,40,128]{2,1,0:T(8,128)S(1)}) custom-call(s32[5,368]{1,0:T(8,128)} %get-tuple-element.20.list_ref, s32[5]{0:T(128)} %get-tuple-element.21.cnt_ref, s32[10]{0:T(128)} %copy-done.5, ...), custom_call_target="tpu_custom_call", output_to_operand_aliasing={{0}: (7, {})} | custom-call | flops 1342177280 | bytes 8388608 | tf_op jit(solution)/shard_map/finish_two/pallas_call | solution.py:371
  74.0 1.2 %collective-permute-done.8 = f32[2,40,128]{2,1,0:T(8,128)S(1)} collective-permute-done((f32[2,40,128]{2,1,0:T(8,128)S(1)}, f32[2,40,128]{2,1,0:T(8,128)S(1)}, u32[]{:S(2)}, u32[]{:S(2)}) %collective-permute-start.8) | collective-permute-done | bytes 40992 | tf_op jit(solution)/shard_map/ppermute | solution.py:570
  75.7 3.7 %collective-permute-start.9 = (f32[2,40,128]{2,1,0:T(8,128)S(1)}, f32[2,40,128]{2,1,0:T(8,128)S(1)}, u32[]{:S(2)}, u32[]{:S(2)}) collective-permute-start(f32[2,40,128]{2,1,0:T(8,128)S(1)} %pad_maximum_fusion), channel_id=1, source_target_pairs={{0,2},{1,3},{2,0},{3,1},{4,6},{5,7},{6,4},{7,5},{8,10},{9,11},{10,... | collective-permute-start | bytes 122888 | tf_op jit(solution)/shard_map/ppermute | solution.py:574
  79.4 1.3 %collective-permute-done.11 = f32[2,40,128]{2,1,0:T(8,128)S(1)} collective-permute-done((f32[2,40,128]{2,1,0:T(8,128)S(1)}, f32[2,40,128]{2,1,0:T(8,128)S(1)}, u32[]{:S(2)}, u32[]{:S(2)}) %collective-permute-start.11) | collective-permute-done | bytes 40992 | tf_op jit(solution)/shard_map/ppermute | solution.py:574
  82.1 3.9 %collective-permute-start.12 = (f32[2,40,128]{2,1,0:T(8,128)S(1)}, f32[2,40,128]{2,1,0:T(8,128)S(1)}, u32[]{:S(2)}, u32[]{:S(2)}) collective-permute-start(f32[2,40,128]{2,1,0:T(8,128)S(1)} %pad_maximum_fusion.1), channel_id=1, source_target_pairs={{0,8},{1,9},{2,10},{3,11},{4,12},{5,13},{6,14},{7,15},{8,0},{9,1},... | collective-permute-start | bytes 122888 | tf_op jit(solution)/shard_map/ppermute | solution.py:574
  86.0 1.1 collective-permute-done.14
  88.5 4.9 %collective-permute-start.17 = (f32[2,40,128]{2,1,0:T(8,128)S(1)}, f32[2,40,128]{2,1,0:T(8,128)S(1)}, u32[]{:S(2)}, u32[]{:S(2)}) collective-permute-start(f32[2,40,128]{2,1,0:T(8,128)S(1)} %pad_maximum_fusion.2), channel_id=1, source_target_pairs={{0,96},{1,97},{2,98},{3,99},{4,100},{5,101},{6,102},{7,103},{8,104... | collective-permute-start | bytes 122888 | tf_op jit(solution)/shard_map/ppermute | solution.py:574
  94.3 1.2 %collective-permute-done.17 = f32[2,40,128]{2,1,0:T(8,128)S(1)} collective-permute-done((f32[2,40,128]{2,1,0:T(8,128)S(1)}, f32[2,40,128]{2,1,0:T(8,128)S(1)}, u32[]{:S(2)}, u32[]{:S(2)}) %collective-permute-start.17) | collective-permute-done | bytes 40992 | tf_op jit(solution)/shard_map/ppermute | solution.py:574
  95.5 3.3 %collective-permute-done.16 = f32[2,40,128]{2,1,0:T(8,128)S(1)} collective-permute-done((f32[2,40,128]{2,1,0:T(8,128)S(1)}, f32[2,40,128]{2,1,0:T(8,128)S(1)}, u32[]{:S(2)}, u32[]{:S(2)}) %collective-permute-start.16) | collective-permute-done | bytes 40992 | tf_op jit(solution)/shard_map/ppermute | solution.py:574
  99.0 1.2 %collective-permute-done.18 = f32[2,40,128]{2,1,0:T(8,128)S(1)} collective-permute-done((f32[2,40,128]{2,1,0:T(8,128)S(1)}, f32[2,40,128]{2,1,0:T(8,128)S(1)}, u32[]{:S(2)}, u32[]{:S(2)}) %collective-permute-start.18) | collective-permute-done | bytes 40992 | tf_op jit(solution)/shard_map/ppermute | solution.py:577
  100.2 11.8 %factors.1 = (f32[128,128]{1,0:T(8,128)S(1)}, f32[128,128]{1,0:T(8,128)}) custom-call(f32[2,40,128]{2,1,0:T(8,128)S(1)} %get-tuple-element.53.zero_ref, f32[2,40,128]{2,1,0:T(8,128)S(1)} %get-tuple-element.52.one_ref), custom_call_target="tpu_custom_call" | custom-call | tf_op jit(solution)/shard_map/factors/pallas_call | solution.py:494
  112.1 2.0 %basis.1 = f32[2048,128]{1,0:T(8,128)} custom-call(f32[16,128,128]{2,1,0:T(8,128)S(1)} %get-tuple-element.33.s_ref, f32[128,128]{1,0:T(8,128)S(1)} %get-tuple-element.36.t_ref), custom_call_target="tpu_custom_call" | custom-call | tf_op jit(solution)/shard_map/basis/pallas_call | solution.py:510
  (50 shorter events, 6.6 us)
Async XLA Ops:
  1.6 31.4 %copy-start.4 = (s32[4,8]{1,0:T(4,128)}, s32[4,8]{1,0:T(4,128)S(1)}, u32[]{:S(2)}) copy-start(s32[4,8]{1,0:T(4,128)S(1)} %dynamic-slice_reduce_fusion.lists_ref.mine_ref) | copy-start | bytes 388
  1.7 11.4 %copy-start.5 = (s32[10]{0:T(128)}, s32[10]{0:T(128)S(1)}, u32[]{:S(2)}) copy-start(s32[10]{0:T(128)S(1)} %stack.59.info_ref) | copy-start | bytes 124
  3.7 37.8 %copy-start.2 = (f32[16,128,128]{2,1,0:T(8,128)}, f32[16,128,128]{2,1,0:T(8,128)S(1)}, u32[]{:S(2)}) copy-start(f32[16,128,128]{2,1,0:T(8,128)S(1)} %get-tuple-element.26.refs_0_.v_ref) | copy-start | bytes 3145732
  3.7 20.9 %collective-permute-start.3 = (f32[8,128,128]{2,1,0:T(8,128)S(1)}, f32[8,128,128]{2,1,0:T(8,128)S(1)}, u32[]{:S(2)}, u32[]{:S(2)}) collective-permute-start(f32[8,128,128]{2,1,0:T(8,128)S(1)} %get-tuple-element.27), channel_id=1, source_target_pairs={{0,1},{1,0},{2,3},{3,2},{4,5},{5,4},{6,7},{7,6},{8,9},{9,8},{10,11... | collective-permute-start | bytes 1572872 | tf_op jit(solution)/shard_map/ppermute | solution.py:556
  3.8 29.1 %collective-permute-start = (f32[8,128,128]{2,1,0:T(8,128)S(1)}, f32[8,128,128]{2,1,0:T(8,128)S(1)}, u32[]{:S(2)}, u32[]{:S(2)}) collective-permute-start(f32[8,128,128]{2,1,0:T(8,128)S(1)} %get-tuple-element.23), channel_id=1, source_target_pairs={{0,2},{1,3},{2,0},{3,1},{4,6},{5,7},{6,4},{7,5},{8,10},{9,11},{10,... | collective-permute-start | bytes 1572872 | tf_op jit(solution)/shard_map/ppermute | solution.py:556
  5.9 27.1 %collective-permute-start.1 = (f32[8,128,128]{2,1,0:T(8,128)S(1)}, f32[8,128,128]{2,1,0:T(8,128)S(1)}, u32[]{:S(2)}, u32[]{:S(2)}) collective-permute-start(f32[8,128,128]{2,1,0:T(8,128)S(1)} %get-tuple-element.24), channel_id=1, source_target_pairs={{0,126},{1,127},{2,4},{3,5},{4,2},{5,3},{6,8},{7,9},{8,6},{9,7},{1... | collective-permute-start | bytes 1572872 | tf_op jit(solution)/shard_map/ppermute | solution.py:556
  13.1 19.9 %collective-permute-start.2 = (f32[8,128,128]{2,1,0:T(8,128)S(1)}, f32[8,128,128]{2,1,0:T(8,128)S(1)}, u32[]{:S(2)}, u32[]{:S(2)}) collective-permute-start(f32[8,128,128]{2,1,0:T(8,128)S(1)} %get-tuple-element.25), channel_id=1, source_target_pairs={{0,127},{1,2},{2,1},{3,4},{4,3},{5,6},{6,5},{7,8},{8,7},{9,10},{10... | collective-permute-start | bytes 1572872 | tf_op jit(solution)/shard_map/ppermute | solution.py:556
  41.6 8.6 %collective-permute-start.7 = (f32[8,128,128]{2,1,0:T(8,128)S(1)}, f32[8,128,128]{2,1,0:T(8,128)S(1)}, u32[]{:S(2)}, u32[]{:S(2)}) collective-permute-start(f32[8,128,128]{2,1,0:T(8,128)S(1)} %get-tuple-element.32), channel_id=1, source_target_pairs={{0,1},{1,0},{2,3},{3,2},{4,5},{5,4},{6,7},{7,6},{8,9},{9,8},{10,11... | collective-permute-start | bytes 1572872 | tf_op jit(solution)/shard_map/ppermute | solution.py:556
  41.7 16.9 %collective-permute-start.6 = (f32[8,128,128]{2,1,0:T(8,128)S(1)}, f32[8,128,128]{2,1,0:T(8,128)S(1)}, u32[]{:S(2)}, u32[]{:S(2)}) collective-permute-start(f32[8,128,128]{2,1,0:T(8,128)S(1)} %get-tuple-element.31), channel_id=1, source_target_pairs={{0,2},{1,3},{2,0},{3,1},{4,6},{5,7},{6,4},{7,5},{8,10},{9,11},{10,... | collective-permute-start | bytes 1572872 | tf_op jit(solution)/shard_map/ppermute | solution.py:556
  43.3 20.2 %collective-permute-start.5 = (f32[8,128,128]{2,1,0:T(8,128)S(1)}, f32[8,128,128]{2,1,0:T(8,128)S(1)}, u32[]{:S(2)}, u32[]{:S(2)}) collective-permute-start(f32[8,128,128]{2,1,0:T(8,128)S(1)} %get-tuple-element.30), channel_id=1, source_target_pairs={{0,126},{1,127},{2,4},{3,5},{4,2},{5,3},{6,8},{7,9},{8,6},{9,7},{1... | collective-permute-start | bytes 1572872 | tf_op jit(solution)/shard_map/ppermute | solution.py:556
  48.7 19.6 %collective-permute-start.4 = (f32[8,128,128]{2,1,0:T(8,128)S(1)}, f32[8,128,128]{2,1,0:T(8,128)S(1)}, u32[]{:S(2)}, u32[]{:S(2)}) collective-permute-start(f32[8,128,128]{2,1,0:T(8,128)S(1)} %get-tuple-element.28), channel_id=1, source_target_pairs={{0,127},{1,2},{2,1},{3,4},{4,3},{5,6},{6,5},{7,8},{8,7},{9,10},{10... | collective-permute-start | bytes 1572872 | tf_op jit(solution)/shard_map/ppermute | solution.py:556
  58.5 9.8 %copy-start.3 = (f32[16,128,128]{2,1,0:T(8,128)S(1)}, f32[16,128,128]{2,1,0:T(8,128)}, u32[]{:S(2)}) copy-start(f32[16,128,128]{2,1,0:T(8,128)} %copy-done.2) | copy-start | bytes 3145732
  58.5 55.5 %copy-start.1 = (s32[128,4,8]{0,2,1:T(8,128)S(1)}, s32[128,4,8]{0,2,1:T(8,128)}, u32[]{:S(2)}) copy-start(s32[128,4,8]{0,2,1:T(8,128)} %param.7) | copy-start | bytes 49156
  73.9 1.3 %collective-permute-start.8 = (f32[2,40,128]{2,1,0:T(8,128)S(1)}, f32[2,40,128]{2,1,0:T(8,128)S(1)}, u32[]{:S(2)}, u32[]{:S(2)}) collective-permute-start(f32[2,40,128]{2,1,0:T(8,128)S(1)} %get-tuple-element.35), channel_id=1, source_target_pairs={{0,1},{1,0},{2,3},{3,2},{4,5},{5,4},{6,7},{7,6},{8,9},{9,8},{10,11... | collective-permute-start | bytes 122888 | tf_op jit(solution)/shard_map/ppermute | solution.py:570
  75.2 5.5 %collective-permute-start.11 = (f32[2,40,128]{2,1,0:T(8,128)S(1)}, f32[2,40,128]{2,1,0:T(8,128)S(1)}, u32[]{:S(2)}, u32[]{:S(2)}) collective-permute-start(f32[2,40,128]{2,1,0:T(8,128)S(1)} %pad_maximum_fusion), channel_id=1, source_target_pairs={{0,6},{1,7},{2,4},{3,5},{4,2},{5,3},{6,0},{7,1},{8,14},{9,15},{10,... | collective-permute-start | bytes 122888 | tf_op jit(solution)/shard_map/ppermute | solution.py:574
  75.3 6.0 %collective-permute-start.10 = (f32[2,40,128]{2,1,0:T(8,128)S(1)}, f32[2,40,128]{2,1,0:T(8,128)S(1)}, u32[]{:S(2)}, u32[]{:S(2)}) collective-permute-start(f32[2,40,128]{2,1,0:T(8,128)S(1)} %pad_maximum_fusion), channel_id=1, source_target_pairs={{0,4},{1,5},{2,6},{3,7},{4,0},{5,1},{6,2},{7,3},{8,12},{9,13},{10,... | collective-permute-start | bytes 122888 | tf_op jit(solution)/shard_map/ppermute | solution.py:574
  75.7 6.1 %collective-permute-start.9 = (f32[2,40,128]{2,1,0:T(8,128)S(1)}, f32[2,40,128]{2,1,0:T(8,128)S(1)}, u32[]{:S(2)}, u32[]{:S(2)}) collective-permute-start(f32[2,40,128]{2,1,0:T(8,128)S(1)} %pad_maximum_fusion), channel_id=1, source_target_pairs={{0,2},{1,3},{2,0},{3,1},{4,6},{5,7},{6,4},{7,5},{8,10},{9,11},{10,... | collective-permute-start | bytes 122888 | tf_op jit(solution)/shard_map/ppermute | solution.py:574
  81.8 5.3 %collective-permute-start.14 = (f32[2,40,128]{2,1,0:T(8,128)S(1)}, f32[2,40,128]{2,1,0:T(8,128)S(1)}, u32[]{:S(2)}, u32[]{:S(2)}) collective-permute-start(f32[2,40,128]{2,1,0:T(8,128)S(1)} %pad_maximum_fusion.1), channel_id=1, source_target_pairs={{0,24},{1,25},{2,26},{3,27},{4,28},{5,29},{6,30},{7,31},{8,16},{9,... | collective-permute-start | bytes 122888 | tf_op jit(solution)/shard_map/ppermute | solution.py:574
  82.1 5.5 %collective-permute-start.13 = (f32[2,40,128]{2,1,0:T(8,128)S(1)}, f32[2,40,128]{2,1,0:T(8,128)S(1)}, u32[]{:S(2)}, u32[]{:S(2)}) collective-permute-start(f32[2,40,128]{2,1,0:T(8,128)S(1)} %pad_maximum_fusion.1), channel_id=1, source_target_pairs={{0,16},{1,17},{2,18},{3,19},{4,20},{5,21},{6,22},{7,23},{8,24},{9,... | collective-permute-start | bytes 122888 | tf_op jit(solution)/shard_map/ppermute | solution.py:574
  82.1 6.3 %collective-permute-start.12 = (f32[2,40,128]{2,1,0:T(8,128)S(1)}, f32[2,40,128]{2,1,0:T(8,128)S(1)}, u32[]{:S(2)}, u32[]{:S(2)}) collective-permute-start(f32[2,40,128]{2,1,0:T(8,128)S(1)} %pad_maximum_fusion.1), channel_id=1, source_target_pairs={{0,8},{1,9},{2,10},{3,11},{4,12},{5,13},{6,14},{7,15},{8,0},{9,1},... | collective-permute-start | bytes 122888 | tf_op jit(solution)/shard_map/ppermute | solution.py:574
  88.5 7.0 %collective-permute-start.17 = (f32[2,40,128]{2,1,0:T(8,128)S(1)}, f32[2,40,128]{2,1,0:T(8,128)S(1)}, u32[]{:S(2)}, u32[]{:S(2)}) collective-permute-start(f32[2,40,128]{2,1,0:T(8,128)S(1)} %pad_maximum_fusion.2), channel_id=1, source_target_pairs={{0,96},{1,97},{2,98},{3,99},{4,100},{5,101},{6,102},{7,103},{8,104... | collective-permute-start | bytes 122888 | tf_op jit(solution)/shard_map/ppermute | solution.py:574
  93.3 5.5 %collective-permute-start.16 = (f32[2,40,128]{2,1,0:T(8,128)S(1)}, f32[2,40,128]{2,1,0:T(8,128)S(1)}, u32[]{:S(2)}, u32[]{:S(2)}) collective-permute-start(f32[2,40,128]{2,1,0:T(8,128)S(1)} %pad_maximum_fusion.2), channel_id=1, source_target_pairs={{0,64},{1,65},{2,66},{3,67},{4,68},{5,69},{6,70},{7,71},{8,72},{9,... | collective-permute-start | bytes 122888 | tf_op jit(solution)/shard_map/ppermute | solution.py:574
  93.3 5.5 %collective-permute-start.15 = (f32[2,40,128]{2,1,0:T(8,128)S(1)}, f32[2,40,128]{2,1,0:T(8,128)S(1)}, u32[]{:S(2)}, u32[]{:S(2)}) collective-permute-start(f32[2,40,128]{2,1,0:T(8,128)S(1)} %pad_maximum_fusion.2), channel_id=1, source_target_pairs={{0,32},{1,33},{2,34},{3,35},{4,36},{5,37},{6,38},{7,39},{8,40},{9,... | collective-permute-start | bytes 122888 | tf_op jit(solution)/shard_map/ppermute | solution.py:574
  98.9 1.3 %collective-permute-start.18 = (f32[2,40,128]{2,1,0:T(8,128)S(1)}, f32[2,40,128]{2,1,0:T(8,128)S(1)}, u32[]{:S(2)}, u32[]{:S(2)}) collective-permute-start(f32[2,40,128]{2,1,0:T(8,128)S(1)} %pad_maximum_fusion.3), channel_id=1, source_target_pairs={{0,1},{1,0},{2,3},{3,2},{4,5},{5,4},{6,7},{7,6},{8,9},{9,8},{10,11... | collective-permute-start | bytes 122888 | tf_op jit(solution)/shard_map/ppermute | solution.py:577
  (1 other events, 0.7 us)

commit v4 on v3

--- a/solution.py
+++ b/solution.py
@@ -97,7 +97,7 @@
     lax.fori_loop(0, lax.div(count - begin + (2 * GROUP - 1), 2 * GROUP), small, 0)
 
 
-def convert_kernel(cols_ref, info_ref, h_ref, hs_ref, list_ref, cnt_ref, buf_ref, sem_ref):
+def convert_kernel(codes_ref, h_ref, hs_ref, list_ref, cnt_ref, buf_ref, sem_ref):
     def fetch(i, slot):
         return pltpu.make_async_copy(h_ref.at[pl.ds(i * FETCH, FETCH)], buf_ref.at[slot], sem_ref.at[slot])
 
@@ -114,11 +114,8 @@
             hs_ref[e, 0:BS, :] = hi
             hs_ref[e, BS : 2 * BS, :] = mid
             hs_ref[e, 2 * BS : 3 * BS, :] = lo
-            col = cols_ref[r, e - r * NNZB]
-            kind = jnp.where(col < RB, 0, 1 + lax.shift_right_logical(col - RB, 3))
-            v = col + info_ref[4 + kind]
-            code = r * 65536 + e * 64 + v
-            source = lax.shift_right_logical(v, 3)
+            code = codes_ref[r, e - r * NNZB]
+            source = lax.shift_right_logical(code, 3) & 7
             mine = [source < 3, source == 3, source == 4, source == 5]
             at = jnp.where(mine[0], counts[0], jnp.where(mine[1], counts[1], jnp.where(mine[2], counts[2], counts[3])))
             list_ref[jnp.maximum(source - 2, 0), at] = code
@@ -146,10 +143,10 @@
 TABLE = [pltpu.VMEM((VZERO + 1, BS, 2 * W), BF16), pltpu.VMEM((VZERO + 1, BS, W), BF16)]
 
 
-def convert(hblocks, local_cols, info):
+def convert(hblocks, codes):
     return pl.pallas_call(
         convert_kernel,
-        in_specs=[SM, SM, ANY],
+        in_specs=[SM, ANY],
         out_specs=[VM, SM, SM],
         out_shape=[
             pltpu.VMEM((NE, SPLIT * BS, BS), BF16),
@@ -160,7 +157,7 @@
         compiler_params=pltpu.CompilerParams(vmem_limit_bytes=VMEM_LIMIT),
         cost_estimate=pl.CostEstimate(flops=NE * 4 * BS**3, bytes_accessed=NE * BS * BS * 4, transcendentals=0),
         name="convert",
-    )(local_cols, info, hblocks.reshape(NE, BS, BS))
+    )(codes, hblocks.reshape(NE, BS, BS))
 
 
 def fill_packs(info_ref, lists_ref, blocks_ref, outs):
@@ -360,7 +357,7 @@
         lo = lo + e
     wide = jnp.broadcast_to(scale[0:1], (W, W))
     both = wide.T
-    core = info_ref[9]
+    core = info_ref[4]
     for i, part in enumerate((hi, lo)):
         zero, one = pack_symmetric((part * wide) * both)
         keep_ref[i] = jnp.where(core == 0, zero, one)
@@ -534,35 +531,37 @@
     pair_d = [(i, (i + (1 if i % 2 else -1)) % count) for i in range(count)]
 
     mine = lax.dynamic_index_in_dim(ghost_lists, me, 0, keepdims=False)
-    info = jnp.stack(
-        [
-            1 + core,
-            3 * odd,
-            3 - 3 * odd,
-            2 - core,
-            jnp.zeros_like(me),
-            jnp.where(odd == 1, AT_A, AT_B) - 16,
-            jnp.where(core == 1, AT_C, AT_D) - 24,
-            jnp.where(core == 1, AT_D, AT_C) - 32,
-            jnp.where(odd == 1, AT_B, AT_A) - 40,
-            core,
-        ]
-    ).astype(jnp.int32)
+    info = jnp.stack([1 + core, 3 * odd, 3 - 3 * odd, 2 - core, core]).astype(jnp.int32)
+    moved = [
+        jnp.where(odd == 1, AT_A, AT_B),
+        jnp.where(core == 1, AT_C, AT_D),
+        jnp.where(core == 1, AT_D, AT_C),
+        jnp.where(odd == 1, AT_B, AT_A),
+    ]
+    at = local_cols
+    for k in range(4):
+        begin = RB + k * GHOST
+        inside = (local_cols >= begin) & (local_cols < begin + GHOST)
+        at = jnp.where(inside, local_cols - begin + moved[k], at)
+    row = lax.broadcasted_iota(jnp.int32, (RB, NNZB), 0)
+    entry = row * NNZB + lax.broadcasted_iota(jnp.int32, (RB, NNZB), 1)
+    codes = (row * 65536 + entry * 64 + at).astype(jnp.int32)
 
     v = vectors.reshape(RB, BS, W)
     move = functools.partial(lax.ppermute, axis_name="rows")
 
-    def exchange(packs):
-        return [move(x, perm=perm) for x, perm in zip(packs, (pair_c, pair_a, pair_b, pair_d))]
-
     v, *packs = pack(info, mine, v)
-    c, a, b, d = exchange(packs)
-    hs, lists, cnt = convert(hblocks, local_cols, info)
+    c, a, b = [move(x, perm=perm) for x, perm in zip(packs, (pair_c, pair_a, pair_b))]
+    hs, lists, cnt = convert(hblocks, codes)
+    late, lists = lax.optimization_barrier((packs[3], lists))
+    d = move(late, perm=pair_d)
     acc = run_phase(0, 2 * GROUP, (OWN, AT_C), lists, cnt, hs, [v, c])
     first, *packs = finish_one(lists, cnt, info, mine, hs, [a, b, d], v, acc)
 
-    c, a, b, d = exchange(packs)
+    c, a, b = [move(x, perm=perm) for x, perm in zip(packs, (pair_c, pair_a, pair_b))]
     acc = run_phase(0, 2 * GROUP, (OWN, AT_C), lists, cnt, hs, [first, c])
+    late, acc = lax.optimization_barrier((packs[3], acc))
+    d = move(late, perm=pair_d)
     acc = run_phase(1, GROUP, (AT_A,), lists, cnt, hs, [a], acc)
     acc = run_phase(2, GROUP, (AT_B,), lists, cnt, hs, [b], acc)
     second, kept, sent = finish_two(lists, cnt, info, hs, d, first, v, acc)

time: 116 us -> 124 us (1.069)
  waiting for transfers between devices: 12.8 us -> 17 us
  local copies, waits for them, and re-layouts: 0.99 us -> 4.7 us
  other arithmetic: 0.17 us -> 1.54 us
    ppermute x8, waiting for transfers between devices: 1.04 us -> 5.05 us  [the longest x2 3.5 us: shards(): d = move(late, perm=pair_d)]
    unnamed x12 -> x20, local copies, waits for them, and re-layouts: 0.69 us -> 4.39 us
    add x0 -> x1, other arithmetic: none -> 1.37 us  [shards(): codes = (row * 65536 + entry * 64 + at).astype(jnp.int32)]
  transfers between devices with their start and end apart: 19 -> 19, of which waited for: 12 -> 13; matrix products, arithmetic and copies ran while one was open for 0% -> 1% of each run, Pallas kernels for 32% -> 29%
where the time goes in v4:
time: 124 us; the launch traced here: 122 us
  Pallas kernels  67 us (54%)
  starting transfers between devices  31.2 us (25%)
  waiting for transfers between devices  17 us (14%)
  local copies, waits for them, and re-layouts  4.7 us (4%)
  other arithmetic  1.54 us (1%)
    pallas_call x4, Pallas kernels, run_phase(): pl.pallas_call(functools.partial(phase_kernel, which, group, places, acc...  24.3 us
    ppermute x9, starting transfers between devices, shards(): move(mine, perm=[(i, i ^ by << shift) for i in range(count)])  14 us
    ppermute x6, starting transfers between devices, shards(): move(x, perm=perm)  12.2 us
    pallas_call x1, Pallas kernels, factors(): pl.pallas_call(functools.partial(factor_kernel, float(total)), in_specs=[...  11.8 us
    pallas_call x1, Pallas kernels, convert(): pl.pallas_call(convert_kernel, in_specs=[SM, ANY], out_specs=[VM, SM, SM]...  10.8 us
    ppermute x9, waiting for transfers between devices, shards(): move(mine, perm=[(i, i ^ by << shift) for i in range(count)])  9.54 us
    pallas_call x1, Pallas kernels, finish_one(): pl.pallas_call(finish_one_kernel, in_specs=[SM] * 4 + [VM] * 6, out_specs...  9.41 us
    pallas_call x1, Pallas kernels, finish_two(): pl.pallas_call(finish_two_kernel, in_specs=[SM] * 3 + [VM] * 5, out_specs...  5.57 us
  transfers between devices with their start and end apart: 19, of which 13 were waited for; matrix products, arithmetic and copies ran while one was open for 1% of the time, Pallas kernels for 29%

profile of v4, /device:TPU:0, one launch (start us, length us, event | category | flops | bytes accessed | tf_op | source)
XLA Modules:
  0.0 122.4 jit_solution(4301670340044214610)
XLA Ops:
  1.7 3.2 %pack.1 = (f32[16,128,128]{2,1,0:T(8,128)S(1)}, f32[8,128,128]{2,1,0:T(8,128)S(1)}, f32[8,128,128]{2,1,0:T(8,128)}, f32[8,128,128]{2,1,0:T(8,128)}, f32[8,128,128]{2,1,0:T(8,128)}) custom-call(s32[5]{0:T(128)S(1)} %stack.43.info_ref, s32[4,8]{1,0:T(4,128)S(1)} %dynamic-slice_reduce_fusion.lists_ref.mine_ref, f32[16,128,128]{2,1,0:T(8,128)} %bitcast.8), custom_call_target="tpu_custom_call" | custom-call | tf_op jit(solution)/shard_map/pack/pallas_call | solution.py:185
  4.9 2.1 %collective-permute-start = (f32[8,128,128]{2,1,0:T(8,128)}, f32[8,128,128]{2,1,0:T(8,128)S(1)}, u32[]{:S(2)}, u32[]{:S(2)}) collective-permute-start(f32[8,128,128]{2,1,0:T(8,128)} %get-tuple-element.29), channel_id=1, source_target_pairs={{0,2},{1,3},{2,0},{3,1},{4,6},{5,7},{6,4},{7,5},{8,10},{9,11},{10,... | collective-permute-start | bytes 1572872 | tf_op jit(solution)/shard_map/ppermute | solution.py:554
  7.0 7.2 %collective-permute-start.1 = (f32[8,128,128]{2,1,0:T(8,128)}, f32[8,128,128]{2,1,0:T(8,128)}, u32[]{:S(2)}, u32[]{:S(2)}) collective-permute-start(f32[8,128,128]{2,1,0:T(8,128)} %get-tuple-element.30), channel_id=1, source_target_pairs={{0,126},{1,127},{2,4},{3,5},{4,2},{5,3},{6,8},{7,9},{8,6},{9,7},{1... | collective-permute-start | bytes 1572872 | tf_op jit(solution)/shard_map/ppermute | solution.py:554
  14.2 1.4 %select_add_fusion.codes_ref = s32[16,20]{1,0:T(8,128)} fusion(s32[16,20]{1,0:T(8,128)} %param.6, s32[]{:T(128)S(6)} %select_n.64, s32[]{:T(128)S(6)} %select_n.63, s32[]{:T(128)S(6)} %select_n.62, s32[]{:T(128)S(6)} %select_n.61, s32[16]{0:T(128)S(1)} %get-tuple-element.62, s32[16]{0:T(128)S(1)} %get-tuple-element.63), kind=kLoop, calls=%fused_computation.35 | loop fusion | flops 8960 | bytes 2704 | tf_op jit(solution)/shard_map/add | solution.py:548
  15.5 10.8 %convert.1 = (bf16[320,384,128]{2,1,0:T(8,128)(2,1)S(1)}, s32[5,368]{1,0:T(8,128)}, s32[5]{0:T(128)}) custom-call(s32[16,20]{1,0:T(8,128)} %select_add_fusion.codes_ref, f32[320,128,128]{2,1,0:T(8,128)} %bitcast.7), custom_call_target="tpu_custom_call" | custom-call | flops 2684354560 | bytes 20971520 | tf_op jit(solution)/shard_map/convert/pallas_call | solution.py:147
  28.6 7.8 %phase_0.2.acc_in = f32[16,128,128]{2,1,0:T(8,128)S(1)} custom-call(s32[5,368]{1,0:T(8,128)} %get-tuple-element.26.list_ref, s32[5]{0:T(128)} %get-tuple-element.27.cnt_ref, bf16[320,384,128]{2,1,0:T(8,128)(2,1)S(1)} %get-tuple-element.28.hs_ref, f32[16,128,128]{2,1,0:T(8,128)S(1)} %get-tuple-element.32.refs_0_.v_ref, f32[8,128,128]{2,1,0:T(8,128)S(1)} %copy-done.7), custom_call_target="tpu_custom_call" | custom-call | flops 2684354560 | bytes 4194304 | tf_op jit(solution)/shard_map/phase_0/pallas_call | solution.py:214
  37.3 3.4 %collective-permute-done.2.d_ref = f32[8,128,128]{2,1,0:T(8,128)S(1)} collective-permute-done((f32[8,128,128]{2,1,0:T(8,128)}, f32[8,128,128]{2,1,0:T(8,128)S(1)}, u32[]{:S(2)}, u32[]{:S(2)}) %collective-permute-start.2) | collective-permute-done | bytes 524320 | tf_op jit(solution)/shard_map/ppermute | solution.py:557
  41.7 9.4 %finish_one.1 = (f32[16,128,128]{2,1,0:T(8,128)S(1)}, f32[8,128,128]{2,1,0:T(8,128)S(1)}, f32[8,128,128]{2,1,0:T(8,128)S(1)}, f32[8,128,128]{2,1,0:T(8,128)S(1)}, f32[8,128,128]{2,1,0:T(8,128)S(1)}) custom-call(s32[5,368]{1,0:T(8,128)} %get-tuple-element.26.list_ref, s32[5]{0:T(128)} %get-tuple-element.27.cnt_ref, ...), custom_call_target="tpu_custom_call", output_to_operand_aliasing={{0}: (9, {})} | custom-call | flops 4026531840 | bytes 8388608 | tf_op jit(solution)/shard_map/finish_one/pallas_call | solution.py:241
  51.2 2.9 %collective-permute-start.6 = (f32[8,128,128]{2,1,0:T(8,128)S(1)}, f32[8,128,128]{2,1,0:T(8,128)S(1)}, u32[]{:S(2)}, u32[]{:S(2)}) collective-permute-start(f32[8,128,128]{2,1,0:T(8,128)S(1)} %get-tuple-element.38), channel_id=1, source_target_pairs={{0,126},{1,127},{2,4},{3,5},{4,2},{5,3},{6,8},{7,9},{8,6},{9,7},{1... | collective-permute-start | bytes 1572872 | tf_op jit(solution)/shard_map/ppermute | solution.py:561
  54.1 7.8 %phase_0.3.refs_1_ = f32[16,128,128]{2,1,0:T(8,128)S(1)} custom-call(s32[5,368]{1,0:T(8,128)} %get-tuple-element.26.list_ref, s32[5]{0:T(128)} %get-tuple-element.27.cnt_ref, bf16[320,384,128]{2,1,0:T(8,128)(2,1)S(1)} %get-tuple-element.28.hs_ref, f32[16,128,128]{2,1,0:T(8,128)S(1)} %get-tuple-element.35.refs_0_.first_ref, ...), custom_call_target="tpu_custom_call" | custom-call | flops 2684354560 | bytes 4194304 | tf_op jit(solution)/shard_map/phase_0/pallas_call | solution.py:214
  61.9 4.3 %collective-permute-start.5 = (f32[8,128,128]{2,1,0:T(8,128)S(1)}, f32[8,128,128]{2,1,0:T(8,128)S(1)}, u32[]{:S(2)}, u32[]{:S(2)}) collective-permute-start(f32[8,128,128]{2,1,0:T(8,128)S(1)} %get-tuple-element.37), channel_id=1, source_target_pairs={{0,127},{1,2},{2,1},{3,4},{4,3},{5,6},{6,5},{7,8},{8,7},{9,10},{10... | collective-permute-start | bytes 1572872 | tf_op jit(solution)/shard_map/ppermute | solution.py:564
  66.2 1.5 %collective-permute-done.7.refs_0_ = f32[8,128,128]{2,1,0:T(8,128)S(1)} collective-permute-done((f32[8,128,128]{2,1,0:T(8,128)S(1)}, f32[8,128,128]{2,1,0:T(8,128)S(1)}, u32[]{:S(2)}, u32[]{:S(2)}) %collective-permute-start.7) | collective-permute-done | bytes 524320 | tf_op jit(solution)/shard_map/ppermute | solution.py:561
  67.8 4.7 %phase_1.1.refs_1_ = f32[16,128,128]{2,1,0:T(8,128)S(1)} custom-call(s32[5,368]{1,0:T(8,128)} %get-tuple-element.26.list_ref, s32[5]{0:T(128)} %get-tuple-element.27.cnt_ref, bf16[320,384,128]{2,1,0:T(8,128)(2,1)S(1)} %get-tuple-element.28.hs_ref, f32[8,128,128]{2,1,0:T(8,128)S(1)} %collective-permute-done.7.refs_0_, ...), custom_call_target="tpu_custom_call", output_to_operand_aliasing={{}: (4, {})} | custom-call | flops 1342177280 | bytes 4194304 | tf_op jit(solution)/shard_map/phase_1/pallas_call | solution.py:214
  72.5 4.0 %phase_2.1.acc_in = f32[16,128,128]{2,1,0:T(8,128)S(1)} custom-call(s32[5,368]{1,0:T(8,128)} %get-tuple-element.26.list_ref, s32[5]{0:T(128)} %get-tuple-element.27.cnt_ref, bf16[320,384,128]{2,1,0:T(8,128)(2,1)S(1)} %get-tuple-element.28.hs_ref, f32[8,128,128]{2,1,0:T(8,128)S(1)} %collective-permute-done.6.refs_0_, ...), custom_call_target="tpu_custom_call", output_to_operand_aliasing={{}: (4, {})} | custom-call | flops 1342177280 | bytes 4194304 | tf_op jit(solution)/shard_map/phase_2/pallas_call | solution.py:214
  76.6 5.6 %finish_two.1 = (f32[16,128,128]{2,1,0:T(8,128)S(1)}, f32[2,40,128]{2,1,0:T(8,128)S(1)}, f32[2,40,128]{2,1,0:T(8,128)S(1)}) custom-call(s32[5,368]{1,0:T(8,128)} %get-tuple-element.26.list_ref, s32[5]{0:T(128)} %get-tuple-element.27.cnt_ref, s32[5]{0:T(128)} %copy-done.9, ...), custom_call_target="tpu_custom_call", output_to_operand_aliasing={{0}: (7, {})} | custom-call | flops 1342177280 | bytes 8388608 | tf_op jit(solution)/shard_map/finish_two/pallas_call | solution.py:368
  82.3 1.2 collective-permute-done.8
  83.6 2.7 %collective-permute-start.10 = (f32[2,40,128]{2,1,0:T(8,128)S(1)}, f32[2,40,128]{2,1,0:T(8,128)S(1)}, u32[]{:S(2)}, u32[]{:S(2)}) collective-permute-start(f32[2,40,128]{2,1,0:T(8,128)S(1)} %pad_maximum_fusion), channel_id=1, source_target_pairs={{0,4},{1,5},{2,6},{3,7},{4,0},{5,1},{6,2},{7,3},{8,12},{9,13},{10,... | collective-permute-start | bytes 122888 | tf_op jit(solution)/shard_map/ppermute | solution.py:573
  86.3 1.4 %collective-permute-start.9 = (f32[2,40,128]{2,1,0:T(8,128)S(1)}, f32[2,40,128]{2,1,0:T(8,128)S(1)}, u32[]{:S(2)}, u32[]{:S(2)}) collective-permute-start(f32[2,40,128]{2,1,0:T(8,128)S(1)} %pad_maximum_fusion), channel_id=1, source_target_pairs={{0,2},{1,3},{2,0},{3,1},{4,6},{5,7},{6,4},{7,5},{8,10},{9,11},{10,... | collective-permute-start | bytes 122888 | tf_op jit(solution)/shard_map/ppermute | solution.py:573
  87.7 1.4 %collective-permute-done.11 = f32[2,40,128]{2,1,0:T(8,128)S(1)} collective-permute-done((f32[2,40,128]{2,1,0:T(8,128)S(1)}, f32[2,40,128]{2,1,0:T(8,128)S(1)}, u32[]{:S(2)}, u32[]{:S(2)}) %collective-permute-start.11) | collective-permute-done | bytes 40992 | tf_op jit(solution)/shard_map/ppermute | solution.py:573
  90.5 4.0 %collective-permute-start.12 = (f32[2,40,128]{2,1,0:T(8,128)S(1)}, f32[2,40,128]{2,1,0:T(8,128)S(1)}, u32[]{:S(2)}, u32[]{:S(2)}) collective-permute-start(f32[2,40,128]{2,1,0:T(8,128)S(1)} %pad_maximum_fusion.1), channel_id=1, source_target_pairs={{0,8},{1,9},{2,10},{3,11},{4,12},{5,13},{6,14},{7,15},{8,0},{9,1},... | collective-permute-start | bytes 122888 | tf_op jit(solution)/shard_map/ppermute | solution.py:573
  97.0 4.7 %collective-permute-start.17 = (f32[2,40,128]{2,1,0:T(8,128)S(1)}, f32[2,40,128]{2,1,0:T(8,128)S(1)}, u32[]{:S(2)}, u32[]{:S(2)}) collective-permute-start(f32[2,40,128]{2,1,0:T(8,128)S(1)} %pad_maximum_fusion.2), channel_id=1, source_target_pairs={{0,96},{1,97},{2,98},{3,99},{4,100},{5,101},{6,102},{7,103},{8,104... | collective-permute-start | bytes 122888 | tf_op jit(solution)/shard_map/ppermute | solution.py:573
  103.7 3.5 %collective-permute-done.16 = f32[2,40,128]{2,1,0:T(8,128)S(1)} collective-permute-done((f32[2,40,128]{2,1,0:T(8,128)S(1)}, f32[2,40,128]{2,1,0:T(8,128)S(1)}, u32[]{:S(2)}, u32[]{:S(2)}) %collective-permute-start.16) | collective-permute-done | bytes 40992 | tf_op jit(solution)/shard_map/ppermute | solution.py:573
  108.6 11.8 %factors.1 = (f32[128,128]{1,0:T(8,128)S(1)}, f32[128,128]{1,0:T(8,128)}) custom-call(f32[2,40,128]{2,1,0:T(8,128)S(1)} %get-tuple-element.61.zero_ref, f32[2,40,128]{2,1,0:T(8,128)S(1)} %get-tuple-element.60.one_ref), custom_call_target="tpu_custom_call" | custom-call | tf_op jit(solution)/shard_map/factors/pallas_call | solution.py:491
  120.4 2.0 %basis.1 = f32[2048,128]{1,0:T(8,128)} custom-call(f32[16,128,128]{2,1,0:T(8,128)S(1)} %get-tuple-element.41.s_ref, f32[128,128]{1,0:T(8,128)S(1)} %get-tuple-element.44.t_ref), custom_call_target="tpu_custom_call" | custom-call | tf_op jit(solution)/shard_map/basis/pallas_call | solution.py:507
  (60 shorter events, 12.8 us)
Async XLA Ops:
  1.6 39.1 %copy-start.8 = (s32[4,8]{1,0:T(4,128)}, s32[4,8]{1,0:T(4,128)S(1)}, u32[]{:S(2)}) copy-start(s32[4,8]{1,0:T(4,128)S(1)} %dynamic-slice_reduce_fusion.lists_ref.mine_ref) | copy-start | bytes 388
  1.7 39.0 %copy-start.9 = (s32[5]{0:T(128)}, s32[5]{0:T(128)S(1)}, u32[]{:S(2)}) copy-start(s32[5]{0:T(128)S(1)} %stack.43.info_ref) | copy-start | bytes 64
  4.9 46.2 %copy-start.2 = (f32[16,128,128]{2,1,0:T(8,128)}, f32[16,128,128]{2,1,0:T(8,128)S(1)}, u32[]{:S(2)}) copy-start(f32[16,128,128]{2,1,0:T(8,128)S(1)} %get-tuple-element.32.refs_0_.v_ref) | copy-start | bytes 3145732
  4.9 31.5 %collective-permute-start = (f32[8,128,128]{2,1,0:T(8,128)}, f32[8,128,128]{2,1,0:T(8,128)S(1)}, u32[]{:S(2)}, u32[]{:S(2)}) collective-permute-start(f32[8,128,128]{2,1,0:T(8,128)} %get-tuple-element.29), channel_id=1, source_target_pairs={{0,2},{1,3},{2,0},{3,1},{4,6},{5,7},{6,4},{7,5},{8,10},{9,11},{10,... | collective-permute-start | bytes 1572872 | tf_op jit(solution)/shard_map/ppermute | solution.py:554
  7.0 30.3 %collective-permute-start.1 = (f32[8,128,128]{2,1,0:T(8,128)}, f32[8,128,128]{2,1,0:T(8,128)}, u32[]{:S(2)}, u32[]{:S(2)}) collective-permute-start(f32[8,128,128]{2,1,0:T(8,128)} %get-tuple-element.30), channel_id=1, source_target_pairs={{0,126},{1,127},{2,4},{3,5},{4,2},{5,3},{6,8},{7,9},{8,6},{9,7},{1... | collective-permute-start | bytes 1572872 | tf_op jit(solution)/shard_map/ppermute | solution.py:554
  14.1 12.7 %collective-permute-start.3 = (f32[8,128,128]{2,1,0:T(8,128)S(1)}, f32[8,128,128]{2,1,0:T(8,128)S(1)}, u32[]{:S(2)}, u32[]{:S(2)}) collective-permute-start(f32[8,128,128]{2,1,0:T(8,128)S(1)} %get-tuple-element.33), channel_id=1, source_target_pairs={{0,1},{1,0},{2,3},{3,2},{4,5},{5,4},{6,7},{7,6},{8,9},{9,8},{10,11... | collective-permute-start | bytes 1572872 | tf_op jit(solution)/shard_map/ppermute | solution.py:554
  26.3 14.3 %collective-permute-start.2 = (f32[8,128,128]{2,1,0:T(8,128)}, f32[8,128,128]{2,1,0:T(8,128)S(1)}, u32[]{:S(2)}, u32[]{:S(2)}) collective-permute-start(f32[8,128,128]{2,1,0:T(8,128)} %get-tuple-element.31), channel_id=1, source_target_pairs={{0,127},{1,2},{2,1},{3,4},{4,3},{5,6},{6,5},{7,8},{8,7},{9,10},{10... | collective-permute-start | bytes 1572872 | tf_op jit(solution)/shard_map/ppermute | solution.py:557
  51.1 3.0 %collective-permute-start.4 = (f32[8,128,128]{2,1,0:T(8,128)S(1)}, f32[8,128,128]{2,1,0:T(8,128)S(1)}, u32[]{:S(2)}, u32[]{:S(2)}) collective-permute-start(f32[8,128,128]{2,1,0:T(8,128)S(1)} %get-tuple-element.36), channel_id=1, source_target_pairs={{0,1},{1,0},{2,3},{3,2},{4,5},{5,4},{6,7},{7,6},{8,9},{9,8},{10,11... | collective-permute-start | bytes 1572872 | tf_op jit(solution)/shard_map/ppermute | solution.py:561
  51.2 21.2 %collective-permute-start.6 = (f32[8,128,128]{2,1,0:T(8,128)S(1)}, f32[8,128,128]{2,1,0:T(8,128)S(1)}, u32[]{:S(2)}, u32[]{:S(2)}) collective-permute-start(f32[8,128,128]{2,1,0:T(8,128)S(1)} %get-tuple-element.38), channel_id=1, source_target_pairs={{0,126},{1,127},{2,4},{3,5},{4,2},{5,3},{6,8},{7,9},{8,6},{9,7},{1... | collective-permute-start | bytes 1572872 | tf_op jit(solution)/shard_map/ppermute | solution.py:561
  54.1 13.6 %collective-permute-start.7 = (f32[8,128,128]{2,1,0:T(8,128)S(1)}, f32[8,128,128]{2,1,0:T(8,128)S(1)}, u32[]{:S(2)}, u32[]{:S(2)}) collective-permute-start(f32[8,128,128]{2,1,0:T(8,128)S(1)} %get-tuple-element.39), channel_id=1, source_target_pairs={{0,2},{1,3},{2,0},{3,1},{4,6},{5,7},{6,4},{7,5},{8,10},{9,11},{10,... | collective-permute-start | bytes 1572872 | tf_op jit(solution)/shard_map/ppermute | solution.py:561
  61.9 14.7 %copy-start.3 = (f32[16,128,128]{2,1,0:T(8,128)S(1)}, f32[16,128,128]{2,1,0:T(8,128)}, u32[]{:S(2)}) copy-start(f32[16,128,128]{2,1,0:T(8,128)} %copy-done.2) | copy-start | bytes 3145732
  61.9 14.7 %collective-permute-start.5 = (f32[8,128,128]{2,1,0:T(8,128)S(1)}, f32[8,128,128]{2,1,0:T(8,128)S(1)}, u32[]{:S(2)}, u32[]{:S(2)}) collective-permute-start(f32[8,128,128]{2,1,0:T(8,128)S(1)} %get-tuple-element.37), channel_id=1, source_target_pairs={{0,127},{1,2},{2,1},{3,4},{4,3},{5,6},{6,5},{7,8},{8,7},{9,10},{10... | collective-permute-start | bytes 1572872 | tf_op jit(solution)/shard_map/ppermute | solution.py:564
  67.8 54.6 %copy-start.1 = (s32[128,4,8]{0,2,1:T(8,128)S(1)}, s32[128,4,8]{0,2,1:T(8,128)}, u32[]{:S(2)}) copy-start(s32[128,4,8]{0,2,1:T(8,128)} %param.7) | copy-start | bytes 49156
  82.2 1.3 %collective-permute-start.8 = (f32[2,40,128]{2,1,0:T(8,128)S(1)}, f32[2,40,128]{2,1,0:T(8,128)S(1)}, u32[]{:S(2)}, u32[]{:S(2)}) collective-permute-start(f32[2,40,128]{2,1,0:T(8,128)S(1)} %get-tuple-element.43), channel_id=1, source_target_pairs={{0,1},{1,0},{2,3},{3,2},{4,5},{5,4},{6,7},{7,6},{8,9},{9,8},{10,11... | collective-permute-start | bytes 122888 | tf_op jit(solution)/shard_map/ppermute | solution.py:569
  83.5 5.6 %collective-permute-start.11 = (f32[2,40,128]{2,1,0:T(8,128)S(1)}, f32[2,40,128]{2,1,0:T(8,128)S(1)}, u32[]{:S(2)}, u32[]{:S(2)}) collective-permute-start(f32[2,40,128]{2,1,0:T(8,128)S(1)} %pad_maximum_fusion), channel_id=1, source_target_pairs={{0,6},{1,7},{2,4},{3,5},{4,2},{5,3},{6,0},{7,1},{8,14},{9,15},{10,... | collective-permute-start | bytes 122888 | tf_op jit(solution)/shard_map/ppermute | solution.py:573
  83.6 5.9 %collective-permute-start.10 = (f32[2,40,128]{2,1,0:T(8,128)S(1)}, f32[2,40,128]{2,1,0:T(8,128)S(1)}, u32[]{:S(2)}, u32[]{:S(2)}) collective-permute-start(f32[2,40,128]{2,1,0:T(8,128)S(1)} %pad_maximum_fusion), channel_id=1, source_target_pairs={{0,4},{1,5},{2,6},{3,7},{4,0},{5,1},{6,2},{7,3},{8,12},{9,13},{10,... | collective-permute-start | bytes 122888 | tf_op jit(solution)/shard_map/ppermute | solution.py:573
  86.3 4.0 %collective-permute-start.9 = (f32[2,40,128]{2,1,0:T(8,128)S(1)}, f32[2,40,128]{2,1,0:T(8,128)S(1)}, u32[]{:S(2)}, u32[]{:S(2)}) collective-permute-start(f32[2,40,128]{2,1,0:T(8,128)S(1)} %pad_maximum_fusion), channel_id=1, source_target_pairs={{0,2},{1,3},{2,0},{3,1},{4,6},{5,7},{6,4},{7,5},{8,10},{9,11},{10,... | collective-permute-start | bytes 122888 | tf_op jit(solution)/shard_map/ppermute | solution.py:573
  90.3 5.3 %collective-permute-start.14 = (f32[2,40,128]{2,1,0:T(8,128)S(1)}, f32[2,40,128]{2,1,0:T(8,128)S(1)}, u32[]{:S(2)}, u32[]{:S(2)}) collective-permute-start(f32[2,40,128]{2,1,0:T(8,128)S(1)} %pad_maximum_fusion.1), channel_id=1, source_target_pairs={{0,24},{1,25},{2,26},{3,27},{4,28},{5,29},{6,30},{7,31},{8,16},{9,... | collective-permute-start | bytes 122888 | tf_op jit(solution)/shard_map/ppermute | solution.py:573
  90.4 5.6 %collective-permute-start.13 = (f32[2,40,128]{2,1,0:T(8,128)S(1)}, f32[2,40,128]{2,1,0:T(8,128)S(1)}, u32[]{:S(2)}, u32[]{:S(2)}) collective-permute-start(f32[2,40,128]{2,1,0:T(8,128)S(1)} %pad_maximum_fusion.1), channel_id=1, source_target_pairs={{0,16},{1,17},{2,18},{3,19},{4,20},{5,21},{6,22},{7,23},{8,24},{9,... | collective-permute-start | bytes 122888 | tf_op jit(solution)/shard_map/ppermute | solution.py:573
  90.5 6.4 %collective-permute-start.12 = (f32[2,40,128]{2,1,0:T(8,128)S(1)}, f32[2,40,128]{2,1,0:T(8,128)S(1)}, u32[]{:S(2)}, u32[]{:S(2)}) collective-permute-start(f32[2,40,128]{2,1,0:T(8,128)S(1)} %pad_maximum_fusion.1), channel_id=1, source_target_pairs={{0,8},{1,9},{2,10},{3,11},{4,12},{5,13},{6,14},{7,15},{8,0},{9,1},... | collective-permute-start | bytes 122888 | tf_op jit(solution)/shard_map/ppermute | solution.py:573
  97.0 6.7 %collective-permute-start.17 = (f32[2,40,128]{2,1,0:T(8,128)S(1)}, f32[2,40,128]{2,1,0:T(8,128)S(1)}, u32[]{:S(2)}, u32[]{:S(2)}) collective-permute-start(f32[2,40,128]{2,1,0:T(8,128)S(1)} %pad_maximum_fusion.2), channel_id=1, source_target_pairs={{0,96},{1,97},{2,98},{3,99},{4,100},{5,101},{6,102},{7,103},{8,104... | collective-permute-start | bytes 122888 | tf_op jit(solution)/shard_map/ppermute | solution.py:573
  101.7 5.5 %collective-permute-start.16 = (f32[2,40,128]{2,1,0:T(8,128)S(1)}, f32[2,40,128]{2,1,0:T(8,128)S(1)}, u32[]{:S(2)}, u32[]{:S(2)}) collective-permute-start(f32[2,40,128]{2,1,0:T(8,128)S(1)} %pad_maximum_fusion.2), channel_id=1, source_target_pairs={{0,64},{1,65},{2,66},{3,67},{4,68},{5,69},{6,70},{7,71},{8,72},{9,... | collective-permute-start | bytes 122888 | tf_op jit(solution)/shard_map/ppermute | solution.py:573
  101.7 5.5 %collective-permute-start.15 = (f32[2,40,128]{2,1,0:T(8,128)S(1)}, f32[2,40,128]{2,1,0:T(8,128)S(1)}, u32[]{:S(2)}, u32[]{:S(2)}) collective-permute-start(f32[2,40,128]{2,1,0:T(8,128)S(1)} %pad_maximum_fusion.2), channel_id=1, source_target_pairs={{0,32},{1,33},{2,34},{3,35},{4,36},{5,37},{6,38},{7,39},{8,40},{9,... | collective-permute-start | bytes 122888 | tf_op jit(solution)/shard_map/ppermute | solution.py:573
  107.3 1.3 %collective-permute-start.18 = (f32[2,40,128]{2,1,0:T(8,128)S(1)}, f32[2,40,128]{2,1,0:T(8,128)S(1)}, u32[]{:S(2)}, u32[]{:S(2)}) collective-permute-start(f32[2,40,128]{2,1,0:T(8,128)S(1)} %pad_maximum_fusion.3), channel_id=1, source_target_pairs={{0,1},{1,0},{2,3},{3,2},{4,5},{5,4},{6,7},{7,6},{8,9},{9,8},{10,11... | collective-permute-start | bytes 122888 | tf_op jit(solution)/shard_map/ppermute | solution.py:576
  (5 other events, 4.4 us)

commit v5 on v3

--- a/solution.py
+++ b/solution.py
@@ -164,9 +164,12 @@
 
 
 def fill_packs(info_ref, lists_ref, blocks_ref, outs):
-    for t in range(4):
-        for g in range(GHOST):
+    def one_of_each(g, carry):
+        for t in range(4):
             outs[t][g] = blocks_ref[lists_ref[info_ref[t], g]]
+        return carry
+
+    lax.fori_loop(0, GHOST, one_of_each, 0)
 
 
 PACKS = [pltpu.VMEM((GHOST, BS, W), F32)] * 4
@@ -199,8 +202,13 @@
 def add_list(which, group, places, bufs, list_ref, cnt_ref, hs_ref, v12_ref, v3_ref, acc_ref):
     load_zero(v12_ref, v3_ref)
     for place, buf in zip(places, bufs):
-        for i in range(buf.shape[0]):
-            load_table(v12_ref, v3_ref, place + i, buf[i])
+
+        def two(i, carry, place=place, buf=buf):
+            load_table(v12_ref, v3_ref, place + 2 * i, buf[2 * i])
+            load_table(v12_ref, v3_ref, place + 2 * i + 1, buf[2 * i + 1])
+            return carry
+
+        lax.fori_loop(0, buf.shape[0] // 2, two, 0)
     products(which, group, list_ref, cnt_ref, hs_ref, v12_ref, v3_ref, acc_ref)
 
 
@@ -208,7 +216,12 @@
     bufs = refs[: len(places)]
     acc_ref, v12_ref, v3_ref = refs[-3:]
     if fresh:
-        acc_ref[...] = jnp.zeros_like(acc_ref)
+
+        def clear(r, carry):
+            acc_ref[r] = jnp.zeros((BS, W), F32)
+            return carry
+
+        lax.fori_loop(0, RB, clear, 0)
     add_list(which, group, places, bufs, list_ref, cnt_ref, hs_ref, v12_ref, v3_ref, acc_ref)
 
 
@@ -233,10 +246,14 @@
     list_ref, cnt_ref, info_ref, mine_ref, hs_ref, a_ref, b_ref, d_ref, v_ref, acc_in, first_ref, *rest
 ):
     outs, tables = rest[:4], rest[4:]
-    for r in range(RB):
+
+    def block_row(r, carry):
         first_ref[r] = first_ref[r] - 0.5 * v_ref[r]
+        return carry
+
+    lax.fori_loop(0, RB, block_row, 0)
     places, bufs = (AT_A, AT_B, AT_D), (a_ref, b_ref, d_ref)
-    add_list(A_B_D, 2 * GROUP, places, bufs, list_ref, cnt_ref, hs_ref, *tables, first_ref)
+    add_list(A_B_D, GROUP, places, bufs, list_ref, cnt_ref, hs_ref, *tables, first_ref)
     fill_packs(info_ref, mine_ref, first_ref, outs)
 
 
@@ -288,9 +305,7 @@
     return out
 
 
-def gram_of_digits(cols, bits):
-    count = len(cols)
-    stacked = jnp.concatenate(cols, axis=1)
+def gram_of_digits(stacked, count, bits):
     full = lax.dot_general(stacked, stacked, (((0,), (0,)), ((), ())), preferred_element_type=F32)
     terms = []
     for w in range(2, 2 * count):
@@ -341,18 +356,26 @@
 
 def finish_two_kernel(
     list_ref, cnt_ref, info_ref, hs_ref, buf_ref, first_ref, v_ref, acc_in,
-    out_ref, keep_ref, send_ref, v12_ref, v3_ref,
+    out_ref, keep_ref, send_ref, v12_ref, v3_ref, digits_ref,
 ):
     add_list(3, GROUP, (AT_D,), (buf_ref,), list_ref, cnt_ref, hs_ref, v12_ref, v3_ref, out_ref)
-    biggest = jnp.zeros((BS, W), F32)
-    for r in range(RB):
+
+    def block_row(r, biggest):
         second = 2.0 * (out_ref[r] - 0.5 * first_ref[r]) - v_ref[r]
         out_ref[r] = second
-        biggest = jnp.maximum(biggest, jnp.abs(second))
+        return jnp.maximum(biggest, jnp.max(jnp.abs(second).reshape(BS // 8, 8, W), axis=0))
+
+    biggest = lax.fori_loop(0, RB, block_row, jnp.zeros((8, W), F32))
     biggest = jnp.max(biggest, axis=0, keepdims=True)
     scale, inverse = power_scale(jnp.broadcast_to(biggest, (8, W)))
-    scaled = out_ref[...].reshape(RB * BS, W) * inverse[0:1]
-    terms = gram_of_digits(digits(scaled, 7, 4), 7)
+
+    def block_digits(r, carry):
+        for i, d in enumerate(digits(out_ref[r] * inverse[0:1], 7, 4)):
+            digits_ref[pl.ds(pl.multiple_of(r * BS, BS), BS), i * W : (i + 1) * W] = d
+        return carry
+
+    lax.fori_loop(0, RB, block_digits, 0)
+    terms = gram_of_digits(digits_ref[...], 4, 7)
     hi = terms[0]
     lo = jnp.zeros_like(hi)
     for t in terms[1:]:
@@ -373,7 +396,7 @@
         in_specs=[SM] * 3 + [VM] * 5,
         out_specs=[VM] * 3,
         out_shape=[pltpu.VMEM((RB, BS, W), F32)] + [pltpu.VMEM((2, PACKED, W), F32)] * 2,
-        scratch_shapes=TABLE,
+        scratch_shapes=TABLE + [pltpu.VMEM((RB * BS, 4 * W), BF16)],
         input_output_aliases={7: 0},
         compiler_params=pltpu.CompilerParams(vmem_limit_bytes=VMEM_LIMIT),
         cost_estimate=pl.CostEstimate(flops=NE * 2 * BS**3, bytes_accessed=8 * 2**20, transcendentals=0),
@@ -425,6 +448,24 @@
     return jnp.concatenate(upper, axis=0), jnp.concatenate(lower_inv, axis=0)
 
 
+def eliminate_by_steps(G):
+    ri = lax.broadcasted_iota(jnp.int32, (W, W), 0)
+    ci = lax.broadcasted_iota(jnp.int32, (W, W), 1)
+
+    def step(j, state):
+        A, B = state
+        row = jnp.sum(jnp.where(ri == j, A, 0.0), axis=0, keepdims=True)
+        brow = jnp.sum(jnp.where(ri == j, B, 0.0), axis=0, keepdims=True)
+        col = jnp.sum(jnp.where(ci == j, A, 0.0), axis=1, keepdims=True)
+        pivot = jnp.sum(jnp.where(ci[0:1] == j, row, 0.0), axis=1, keepdims=True)
+        times = jnp.where(ri > j, col / pivot, 0.0)
+        return A - times * row, B - times * brow
+
+    A, B = lax.fori_loop(0, W, step, (G, (ri == ci).astype(F32)))
+    s = 1.0 / jnp.sqrt(jnp.sum(jnp.where(ri == ci, A, 0.0), axis=1, keepdims=True))
+    return jnp.where(ci >= ri, A * s, 0.0), jnp.where(ci <= ri, B * s, 0.0)
+
+
 def dot(a, b, ca, cb):
     return lax.dot_general(a, b, (((ca,), (cb,)), ((), ())), preferred_element_type=F32)
 
@@ -464,26 +505,30 @@
     tall, tall_inv = wide.T, wide_inv.T
     rest = (hi * wide_inv) * tall_inv
     small = (lo * wide_inv) * tall_inv
-    for t in gram_of_digits(digits(upper * wide_inv, 8, 4), 8):
+    for t in gram_of_digits(jnp.concatenate(digits(upper * wide_inv, 8, 4), axis=1), 4, 8):
         rest, e = two_sum(rest, -t)
         small = small + e
     rest = ((rest + small) * wide) * tall
 
     off = mm3(mm3(linv, rest), linv, 1, 1)
     defect = eye - mm6(linv, upper, 1, 1)
-    close = jnp.sum(off * off) < 1e-5
+    close = jnp.sum(off * off) < 1e-3
 
     @pl.when(close)
     def _():
         x = half_lower(off)
-        z = mm1(x, x - defect) + defect
-        x = half_lower(off - mm1(x, x, 1, 1))
-        inv_ref[...] = linv + mm3(z - x, linv)
+        for _ in range(3):
+            x = half_lower(off - mm1(x, x, 1, 1))
+        first_order = defect - x
+        z = first_order
+        for _ in range(3):
+            z = first_order - mm1(x, z)
+        inv_ref[...] = linv + mm3(z, linv)
         factor_ref[...] = upper + mm3(x, upper, 0, 0)
 
     @pl.when(jnp.logical_not(close))
     def _():
-        u2, l2 = eliminate(eye + off)
+        u2, l2 = eliminate_by_steps(eye + off)
         factor = mm6(u2, upper)
         inv = mm6(l2, linv)
         inv_ref[...] = inv + mm6(eye - mm6(inv, factor, 1, 1), inv)
@@ -558,11 +603,11 @@
     v, *packs = pack(info, mine, v)
     c, a, b, d = exchange(packs)
     hs, lists, cnt = convert(hblocks, local_cols, info)
-    acc = run_phase(0, 2 * GROUP, (OWN, AT_C), lists, cnt, hs, [v, c])
+    acc = run_phase(0, GROUP, (OWN, AT_C), lists, cnt, hs, [v, c])
     first, *packs = finish_one(lists, cnt, info, mine, hs, [a, b, d], v, acc)
 
     c, a, b, d = exchange(packs)
-    acc = run_phase(0, 2 * GROUP, (OWN, AT_C), lists, cnt, hs, [first, c])
+    acc = run_phase(0, GROUP, (OWN, AT_C), lists, cnt, hs, [first, c])
     acc = run_phase(1, GROUP, (AT_A,), lists, cnt, hs, [a], acc)
     acc = run_phase(2, GROUP, (AT_B,), lists, cnt, hs, [b], acc)
     second, kept, sent = finish_two(lists, cnt, info, hs, d, first, v, acc)

time: 116 us -> 114 us (0.983)
  Pallas kernels: 66.9 us -> 64.3 us
    pallas_call x1, Pallas kernels: 11.8 us -> 7.36 us  [factors(): pl.pallas_call(functools.partial(factor_kernel, float(total)), in_specs=[...]
    pallas_call x1, Pallas kernels: 8.56 us -> 10.3 us  [finish_one(): pl.pallas_call(finish_one_kernel, in_specs=[SM] * 4 + [VM] * 6, out_specs...]
where the time goes in v5:
time: 114 us; the launch traced here: 113 us
  Pallas kernels  64.3 us (56%)
  starting transfers between devices  32.8 us (29%)
  waiting for transfers between devices  13.5 us (12%)
    pallas_call x4, Pallas kernels, run_phase(): pl.pallas_call(functools.partial(phase_kernel, which, group, places, acc...  24.9 us
    ppermute x8, starting transfers between devices, exchange(): move(x, perm=perm)  17.9 us
    ppermute x9, starting transfers between devices, shards(): move(mine, perm=[(i, i ^ by << shift) for i in range(count)])  14.5 us
    pallas_call x1, Pallas kernels, convert(): pl.pallas_call(convert_kernel, in_specs=[SM, SM, ANY], out_specs=[VM, SM,...  11.5 us
    pallas_call x1, Pallas kernels, finish_one(): pl.pallas_call(finish_one_kernel, in_specs=[SM] * 4 + [VM] * 6, out_specs...  10.3 us
    ppermute x9, waiting for transfers between devices, shards(): move(mine, perm=[(i, i ^ by << shift) for i in range(count)])  9.38 us
    pallas_call x1, Pallas kernels, factors(): pl.pallas_call(functools.partial(factor_kernel, float(total)), in_specs=[...  7.36 us
    pallas_call x1, Pallas kernels, finish_two(): pl.pallas_call(finish_two_kernel, in_specs=[SM] * 3 + [VM] * 5, out_specs...  6.19 us
  transfers between devices with their start and end apart: 19, of which 12 were waited for; matrix products, arithmetic and copies ran while one was open for 0% of the time, Pallas kernels for 32%

profile of v5, /device:TPU:0, one launch (start us, length us, event | category | flops | bytes accessed | tf_op | source)
XLA Modules:
  0.0 112.7 jit_solution(3411047236703309776)
XLA Ops:
  1.7 2.1 %pack.1 = (f32[16,128,128]{2,1,0:T(8,128)S(1)}, f32[8,128,128]{2,1,0:T(8,128)S(1)}, f32[8,128,128]{2,1,0:T(8,128)S(1)}, f32[8,128,128]{2,1,0:T(8,128)S(1)}, f32[8,128,128]{2,1,0:T(8,128)S(1)}) custom-call(s32[10]{0:T(128)S(1)} %stack.59.info_ref, s32[4,8]{1,0:T(4,128)S(1)} %dynamic-slice_reduce_fusion.lists_ref.mine_ref, f32[16,128,128]{2,1,0:T(8,128)} %bitcast.12), custom_call_target="tpu_custom_call" | custom-call | tf_op jit(solution)/shard_map/pack/pallas_call | solution.py:191
  3.9 2.1 %collective-permute-start = (f32[8,128,128]{2,1,0:T(8,128)S(1)}, f32[8,128,128]{2,1,0:T(8,128)S(1)}, u32[]{:S(2)}, u32[]{:S(2)}) collective-permute-start(f32[8,128,128]{2,1,0:T(8,128)S(1)} %get-tuple-element.23), channel_id=1, source_target_pairs={{0,2},{1,3},{2,0},{3,1},{4,6},{5,7},{6,4},{7,5},{8,10},{9,11},{10,... | collective-permute-start | bytes 1572872 | tf_op jit(solution)/shard_map/ppermute | solution.py:601
  6.0 7.2 %collective-permute-start.1 = (f32[8,128,128]{2,1,0:T(8,128)S(1)}, f32[8,128,128]{2,1,0:T(8,128)S(1)}, u32[]{:S(2)}, u32[]{:S(2)}) collective-permute-start(f32[8,128,128]{2,1,0:T(8,128)S(1)} %get-tuple-element.24), channel_id=1, source_target_pairs={{0,126},{1,127},{2,4},{3,5},{4,2},{5,3},{6,8},{7,9},{8,6},{9,7},{1... | collective-permute-start | bytes 1572872 | tf_op jit(solution)/shard_map/ppermute | solution.py:601
  13.2 11.5 %convert.1 = (bf16[320,384,128]{2,1,0:T(8,128)(2,1)S(1)}, s32[5,368]{1,0:T(8,128)}, s32[5]{0:T(128)}) custom-call(s32[16,20]{1,0:T(8,128)} %cols_ref.1, s32[10]{0:T(128)} %copy-done.5, f32[320,128,128]{2,1,0:T(8,128)} %bitcast.11), custom_call_target="tpu_custom_call" | custom-call | flops 2684354560 | bytes 20971520 | tf_op jit(solution)/shard_map/convert/pallas_call | solution.py:150
  24.7 8.5 %phase_0.2.acc_in = f32[16,128,128]{2,1,0:T(8,128)S(1)} custom-call(s32[5,368]{1,0:T(8,128)} %get-tuple-element.20.list_ref, s32[5]{0:T(128)} %get-tuple-element.21.cnt_ref, bf16[320,384,128]{2,1,0:T(8,128)(2,1)S(1)} %get-tuple-element.22.hs_ref, f32[16,128,128]{2,1,0:T(8,128)S(1)} %get-tuple-element.26.refs_0_.v_ref, ...), custom_call_target="tpu_custom_call" | custom-call | flops 2684354560 | bytes 4194304 | tf_op jit(solution)/shard_map/phase_0/pallas_call | solution.py:230
  33.2 10.3 %finish_one.1 = (f32[16,128,128]{2,1,0:T(8,128)S(1)}, f32[8,128,128]{2,1,0:T(8,128)S(1)}, f32[8,128,128]{2,1,0:T(8,128)S(1)}, f32[8,128,128]{2,1,0:T(8,128)S(1)}, f32[8,128,128]{2,1,0:T(8,128)S(1)}) custom-call(s32[5,368]{1,0:T(8,128)} %get-tuple-element.20.list_ref, s32[5]{0:T(128)} %get-tuple-element.21.cnt_ref, ...), custom_call_target="tpu_custom_call", output_to_operand_aliasing={{0}: (9, {})} | custom-call | flops 4026531840 | bytes 8388608 | tf_op jit(solution)/shard_map/finish_one/pallas_call | solution.py:261
  43.6 1.6 %collective-permute-start.6 = (f32[8,128,128]{2,1,0:T(8,128)S(1)}, f32[8,128,128]{2,1,0:T(8,128)S(1)}, u32[]{:S(2)}, u32[]{:S(2)}) collective-permute-start(f32[8,128,128]{2,1,0:T(8,128)S(1)} %get-tuple-element.31), channel_id=1, source_target_pairs={{0,2},{1,3},{2,0},{3,1},{4,6},{5,7},{6,4},{7,5},{8,10},{9,11},{10,... | collective-permute-start | bytes 1572872 | tf_op jit(solution)/shard_map/ppermute | solution.py:601
  45.2 6.0 %collective-permute-start.5 = (f32[8,128,128]{2,1,0:T(8,128)S(1)}, f32[8,128,128]{2,1,0:T(8,128)S(1)}, u32[]{:S(2)}, u32[]{:S(2)}) collective-permute-start(f32[8,128,128]{2,1,0:T(8,128)S(1)} %get-tuple-element.30), channel_id=1, source_target_pairs={{0,126},{1,127},{2,4},{3,5},{4,2},{5,3},{6,8},{7,9},{8,6},{9,7},{1... | collective-permute-start | bytes 1572872 | tf_op jit(solution)/shard_map/ppermute | solution.py:601
  52.1 8.5 %phase_0.3.refs_1_ = f32[16,128,128]{2,1,0:T(8,128)S(1)} custom-call(s32[5,368]{1,0:T(8,128)} %get-tuple-element.20.list_ref, s32[5]{0:T(128)} %get-tuple-element.21.cnt_ref, bf16[320,384,128]{2,1,0:T(8,128)(2,1)S(1)} %get-tuple-element.22.hs_ref, f32[16,128,128]{2,1,0:T(8,128)S(1)} %get-tuple-element.29.refs_0_.first_ref, ...), custom_call_target="tpu_custom_call" | custom-call | flops 2684354560 | bytes 4194304 | tf_op jit(solution)/shard_map/phase_0/pallas_call | solution.py:230
  60.7 4.0 %phase_1.1.refs_1_ = f32[16,128,128]{2,1,0:T(8,128)S(1)} custom-call(s32[5,368]{1,0:T(8,128)} %get-tuple-element.20.list_ref, s32[5]{0:T(128)} %get-tuple-element.21.cnt_ref, bf16[320,384,128]{2,1,0:T(8,128)(2,1)S(1)} %get-tuple-element.22.hs_ref, f32[8,128,128]{2,1,0:T(8,128)S(1)} %collective-permute-done.6.refs_0_, ...), custom_call_target="tpu_custom_call", output_to_operand_aliasing={{}: (4, {})} | custom-call | flops 1342177280 | bytes 4194304 | tf_op jit(solution)/shard_map/phase_1/pallas_call | solution.py:230
  65.4 3.9 %phase_2.1.acc_in = f32[16,128,128]{2,1,0:T(8,128)S(1)} custom-call(s32[5,368]{1,0:T(8,128)} %get-tuple-element.20.list_ref, s32[5]{0:T(128)} %get-tuple-element.21.cnt_ref, bf16[320,384,128]{2,1,0:T(8,128)(2,1)S(1)} %get-tuple-element.22.hs_ref, f32[8,128,128]{2,1,0:T(8,128)S(1)} %collective-permute-done.5.refs_0_, ...), custom_call_target="tpu_custom_call", output_to_operand_aliasing={{}: (4, {})} | custom-call | flops 1342177280 | bytes 4194304 | tf_op jit(solution)/shard_map/phase_2/pallas_call | solution.py:230
  70.2 6.2 %finish_two.1 = (f32[16,128,128]{2,1,0:T(8,128)S(1)}, f32[2,40,128]{2,1,0:T(8,128)S(1)}, f32[2,40,128]{2,1,0:T(8,128)S(1)}) custom-call(s32[5,368]{1,0:T(8,128)} %get-tuple-element.20.list_ref, s32[5]{0:T(128)} %get-tuple-element.21.cnt_ref, s32[10]{0:T(128)} %copy-done.5, ...), custom_call_target="tpu_custom_call", output_to_operand_aliasing={{0}: (7, {})} | custom-call | flops 1342177280 | bytes 8388608 | tf_op jit(solution)/shard_map/finish_two/pallas_call | solution.py:394
  76.5 1.2 %collective-permute-done.8 = f32[2,40,128]{2,1,0:T(8,128)S(1)} collective-permute-done((f32[2,40,128]{2,1,0:T(8,128)S(1)}, f32[2,40,128]{2,1,0:T(8,128)S(1)}, u32[]{:S(2)}, u32[]{:S(2)}) %collective-permute-start.8) | collective-permute-done | bytes 40992 | tf_op jit(solution)/shard_map/ppermute | solution.py:615
  77.8 2.4 %collective-permute-start.10 = (f32[2,40,128]{2,1,0:T(8,128)S(1)}, f32[2,40,128]{2,1,0:T(8,128)S(1)}, u32[]{:S(2)}, u32[]{:S(2)}) collective-permute-start(f32[2,40,128]{2,1,0:T(8,128)S(1)} %pad_maximum_fusion), channel_id=1, source_target_pairs={{0,4},{1,5},{2,6},{3,7},{4,0},{5,1},{6,2},{7,3},{8,12},{9,13},{10,... | collective-permute-start | bytes 122888 | tf_op jit(solution)/shard_map/ppermute | solution.py:619
  80.2 1.7 %collective-permute-start.9 = (f32[2,40,128]{2,1,0:T(8,128)S(1)}, f32[2,40,128]{2,1,0:T(8,128)S(1)}, u32[]{:S(2)}, u32[]{:S(2)}) collective-permute-start(f32[2,40,128]{2,1,0:T(8,128)S(1)} %pad_maximum_fusion), channel_id=1, source_target_pairs={{0,2},{1,3},{2,0},{3,1},{4,6},{5,7},{6,4},{7,5},{8,10},{9,11},{10,... | collective-permute-start | bytes 122888 | tf_op jit(solution)/shard_map/ppermute | solution.py:619
  81.9 1.3 %collective-permute-done.11 = f32[2,40,128]{2,1,0:T(8,128)S(1)} collective-permute-done((f32[2,40,128]{2,1,0:T(8,128)S(1)}, f32[2,40,128]{2,1,0:T(8,128)S(1)}, u32[]{:S(2)}, u32[]{:S(2)}) %collective-permute-start.11) | collective-permute-done | bytes 40992 | tf_op jit(solution)/shard_map/ppermute | solution.py:619
  84.6 4.0 %collective-permute-start.12 = (f32[2,40,128]{2,1,0:T(8,128)S(1)}, f32[2,40,128]{2,1,0:T(8,128)S(1)}, u32[]{:S(2)}, u32[]{:S(2)}) collective-permute-start(f32[2,40,128]{2,1,0:T(8,128)S(1)} %pad_maximum_fusion.1), channel_id=1, source_target_pairs={{0,8},{1,9},{2,10},{3,11},{4,12},{5,13},{6,14},{7,15},{8,0},{9,1},... | collective-permute-start | bytes 122888 | tf_op jit(solution)/shard_map/ppermute | solution.py:619
  88.6 1.1 %collective-permute-done.14 = f32[2,40,128]{2,1,0:T(8,128)S(1)} collective-permute-done((f32[2,40,128]{2,1,0:T(8,128)S(1)}, f32[2,40,128]{2,1,0:T(8,128)S(1)}, u32[]{:S(2)}, u32[]{:S(2)}) %collective-permute-start.14) | collective-permute-done | bytes 40992 | tf_op jit(solution)/shard_map/ppermute | solution.py:619
  91.0 5.2 %collective-permute-start.17 = (f32[2,40,128]{2,1,0:T(8,128)S(1)}, f32[2,40,128]{2,1,0:T(8,128)S(1)}, u32[]{:S(2)}, u32[]{:S(2)}) collective-permute-start(f32[2,40,128]{2,1,0:T(8,128)S(1)} %pad_maximum_fusion.2), channel_id=1, source_target_pairs={{0,96},{1,97},{2,98},{3,99},{4,100},{5,101},{6,102},{7,103},{8,104... | collective-permute-start | bytes 122888 | tf_op jit(solution)/shard_map/ppermute | solution.py:619
  97.2 1.2 %collective-permute-done.17 = f32[2,40,128]{2,1,0:T(8,128)S(1)} collective-permute-done((f32[2,40,128]{2,1,0:T(8,128)S(1)}, f32[2,40,128]{2,1,0:T(8,128)S(1)}, u32[]{:S(2)}, u32[]{:S(2)}) %collective-permute-start.17) | collective-permute-done | bytes 40992 | tf_op jit(solution)/shard_map/ppermute | solution.py:619
  98.5 3.3 %collective-permute-done.16 = f32[2,40,128]{2,1,0:T(8,128)S(1)} collective-permute-done((f32[2,40,128]{2,1,0:T(8,128)S(1)}, f32[2,40,128]{2,1,0:T(8,128)S(1)}, u32[]{:S(2)}, u32[]{:S(2)}) %collective-permute-start.16) | collective-permute-done | bytes 40992 | tf_op jit(solution)/shard_map/ppermute | solution.py:619
  102.1 1.2 %collective-permute-done.18 = f32[2,40,128]{2,1,0:T(8,128)S(1)} collective-permute-done((f32[2,40,128]{2,1,0:T(8,128)S(1)}, f32[2,40,128]{2,1,0:T(8,128)S(1)}, u32[]{:S(2)}, u32[]{:S(2)}) %collective-permute-start.18) | collective-permute-done | bytes 40992 | tf_op jit(solution)/shard_map/ppermute | solution.py:622
  103.4 7.4 %factors.1 = (f32[128,128]{1,0:T(8,128)S(1)}, f32[128,128]{1,0:T(8,128)}) custom-call(f32[2,40,128]{2,1,0:T(8,128)S(1)} %get-tuple-element.53.zero_ref, f32[2,40,128]{2,1,0:T(8,128)S(1)} %get-tuple-element.52.one_ref), custom_call_target="tpu_custom_call" | custom-call | tf_op jit(solution)/shard_map/factors/pallas_call | solution.py:539
  110.7 2.0 %basis.1 = f32[2048,128]{1,0:T(8,128)} custom-call(f32[16,128,128]{2,1,0:T(8,128)S(1)} %get-tuple-element.33.s_ref, f32[128,128]{1,0:T(8,128)S(1)} %get-tuple-element.36.t_ref), custom_call_target="tpu_custom_call" | custom-call | tf_op jit(solution)/shard_map/basis/pallas_call | solution.py:555
  (50 shorter events, 7.9 us)
Async XLA Ops:
  1.6 31.7 %copy-start.4 = (s32[4,8]{1,0:T(4,128)}, s32[4,8]{1,0:T(4,128)S(1)}, u32[]{:S(2)}) copy-start(s32[4,8]{1,0:T(4,128)S(1)} %dynamic-slice_reduce_fusion.lists_ref.mine_ref) | copy-start | bytes 388
  1.7 11.5 %copy-start.5 = (s32[10]{0:T(128)}, s32[10]{0:T(128)S(1)}, u32[]{:S(2)}) copy-start(s32[10]{0:T(128)S(1)} %stack.59.info_ref) | copy-start | bytes 124
  3.8 39.7 %copy-start.2 = (f32[16,128,128]{2,1,0:T(8,128)}, f32[16,128,128]{2,1,0:T(8,128)S(1)}, u32[]{:S(2)}) copy-start(f32[16,128,128]{2,1,0:T(8,128)S(1)} %get-tuple-element.26.refs_0_.v_ref) | copy-start | bytes 3145732
  3.8 20.9 %collective-permute-start.3 = (f32[8,128,128]{2,1,0:T(8,128)S(1)}, f32[8,128,128]{2,1,0:T(8,128)S(1)}, u32[]{:S(2)}, u32[]{:S(2)}) collective-permute-start(f32[8,128,128]{2,1,0:T(8,128)S(1)} %get-tuple-element.27), channel_id=1, source_target_pairs={{0,1},{1,0},{2,3},{3,2},{4,5},{5,4},{6,7},{7,6},{8,9},{9,8},{10,11... | collective-permute-start | bytes 1572872 | tf_op jit(solution)/shard_map/ppermute | solution.py:601
  3.9 29.3 %collective-permute-start = (f32[8,128,128]{2,1,0:T(8,128)S(1)}, f32[8,128,128]{2,1,0:T(8,128)S(1)}, u32[]{:S(2)}, u32[]{:S(2)}) collective-permute-start(f32[8,128,128]{2,1,0:T(8,128)S(1)} %get-tuple-element.23), channel_id=1, source_target_pairs={{0,2},{1,3},{2,0},{3,1},{4,6},{5,7},{6,4},{7,5},{8,10},{9,11},{10,... | collective-permute-start | bytes 1572872 | tf_op jit(solution)/shard_map/ppermute | solution.py:601
  6.0 27.2 %collective-permute-start.1 = (f32[8,128,128]{2,1,0:T(8,128)S(1)}, f32[8,128,128]{2,1,0:T(8,128)S(1)}, u32[]{:S(2)}, u32[]{:S(2)}) collective-permute-start(f32[8,128,128]{2,1,0:T(8,128)S(1)} %get-tuple-element.24), channel_id=1, source_target_pairs={{0,126},{1,127},{2,4},{3,5},{4,2},{5,3},{6,8},{7,9},{8,6},{9,7},{1... | collective-permute-start | bytes 1572872 | tf_op jit(solution)/shard_map/ppermute | solution.py:601
  13.2 20.1 %collective-permute-start.2 = (f32[8,128,128]{2,1,0:T(8,128)S(1)}, f32[8,128,128]{2,1,0:T(8,128)S(1)}, u32[]{:S(2)}, u32[]{:S(2)}) collective-permute-start(f32[8,128,128]{2,1,0:T(8,128)S(1)} %get-tuple-element.25), channel_id=1, source_target_pairs={{0,127},{1,2},{2,1},{3,4},{4,3},{5,6},{6,5},{7,8},{8,7},{9,10},{10... | collective-permute-start | bytes 1572872 | tf_op jit(solution)/shard_map/ppermute | solution.py:601
  43.5 8.6 %collective-permute-start.7 = (f32[8,128,128]{2,1,0:T(8,128)S(1)}, f32[8,128,128]{2,1,0:T(8,128)S(1)}, u32[]{:S(2)}, u32[]{:S(2)}) collective-permute-start(f32[8,128,128]{2,1,0:T(8,128)S(1)} %get-tuple-element.32), channel_id=1, source_target_pairs={{0,1},{1,0},{2,3},{3,2},{4,5},{5,4},{6,7},{7,6},{8,9},{9,8},{10,11... | collective-permute-start | bytes 1572872 | tf_op jit(solution)/shard_map/ppermute | solution.py:601
  43.6 17.0 %collective-permute-start.6 = (f32[8,128,128]{2,1,0:T(8,128)S(1)}, f32[8,128,128]{2,1,0:T(8,128)S(1)}, u32[]{:S(2)}, u32[]{:S(2)}) collective-permute-start(f32[8,128,128]{2,1,0:T(8,128)S(1)} %get-tuple-element.31), channel_id=1, source_target_pairs={{0,2},{1,3},{2,0},{3,1},{4,6},{5,7},{6,4},{7,5},{8,10},{9,11},{10,... | collective-permute-start | bytes 1572872 | tf_op jit(solution)/shard_map/ppermute | solution.py:601
  45.2 20.2 %collective-permute-start.5 = (f32[8,128,128]{2,1,0:T(8,128)S(1)}, f32[8,128,128]{2,1,0:T(8,128)S(1)}, u32[]{:S(2)}, u32[]{:S(2)}) collective-permute-start(f32[8,128,128]{2,1,0:T(8,128)S(1)} %get-tuple-element.30), channel_id=1, source_target_pairs={{0,126},{1,127},{2,4},{3,5},{4,2},{5,3},{6,8},{7,9},{8,6},{9,7},{1... | collective-permute-start | bytes 1572872 | tf_op jit(solution)/shard_map/ppermute | solution.py:601
  51.2 19.0 %collective-permute-start.4 = (f32[8,128,128]{2,1,0:T(8,128)S(1)}, f32[8,128,128]{2,1,0:T(8,128)S(1)}, u32[]{:S(2)}, u32[]{:S(2)}) collective-permute-start(f32[8,128,128]{2,1,0:T(8,128)S(1)} %get-tuple-element.28), channel_id=1, source_target_pairs={{0,127},{1,2},{2,1},{3,4},{4,3},{5,6},{6,5},{7,8},{8,7},{9,10},{10... | collective-permute-start | bytes 1572872 | tf_op jit(solution)/shard_map/ppermute | solution.py:601
  60.6 9.6 %copy-start.3 = (f32[16,128,128]{2,1,0:T(8,128)S(1)}, f32[16,128,128]{2,1,0:T(8,128)}, u32[]{:S(2)}) copy-start(f32[16,128,128]{2,1,0:T(8,128)} %copy-done.2) | copy-start | bytes 3145732
  60.7 52.0 %copy-start.1 = (s32[128,4,8]{0,2,1:T(8,128)S(1)}, s32[128,4,8]{0,2,1:T(8,128)}, u32[]{:S(2)}) copy-start(s32[128,4,8]{0,2,1:T(8,128)} %param.7) | copy-start | bytes 49156
  76.4 1.3 %collective-permute-start.8 = (f32[2,40,128]{2,1,0:T(8,128)S(1)}, f32[2,40,128]{2,1,0:T(8,128)S(1)}, u32[]{:S(2)}, u32[]{:S(2)}) collective-permute-start(f32[2,40,128]{2,1,0:T(8,128)S(1)} %get-tuple-element.35), channel_id=1, source_target_pairs={{0,1},{1,0},{2,3},{3,2},{4,5},{5,4},{6,7},{7,6},{8,9},{9,8},{10,11... | collective-permute-start | bytes 122888 | tf_op jit(solution)/shard_map/ppermute | solution.py:615
  77.7 5.5 %collective-permute-start.11 = (f32[2,40,128]{2,1,0:T(8,128)S(1)}, f32[2,40,128]{2,1,0:T(8,128)S(1)}, u32[]{:S(2)}, u32[]{:S(2)}) collective-permute-start(f32[2,40,128]{2,1,0:T(8,128)S(1)} %pad_maximum_fusion), channel_id=1, source_target_pairs={{0,6},{1,7},{2,4},{3,5},{4,2},{5,3},{6,0},{7,1},{8,14},{9,15},{10,... | collective-permute-start | bytes 122888 | tf_op jit(solution)/shard_map/ppermute | solution.py:619
  77.8 6.0 %collective-permute-start.10 = (f32[2,40,128]{2,1,0:T(8,128)S(1)}, f32[2,40,128]{2,1,0:T(8,128)S(1)}, u32[]{:S(2)}, u32[]{:S(2)}) collective-permute-start(f32[2,40,128]{2,1,0:T(8,128)S(1)} %pad_maximum_fusion), channel_id=1, source_target_pairs={{0,4},{1,5},{2,6},{3,7},{4,0},{5,1},{6,2},{7,3},{8,12},{9,13},{10,... | collective-permute-start | bytes 122888 | tf_op jit(solution)/shard_map/ppermute | solution.py:619
  80.2 4.1 %collective-permute-start.9 = (f32[2,40,128]{2,1,0:T(8,128)S(1)}, f32[2,40,128]{2,1,0:T(8,128)S(1)}, u32[]{:S(2)}, u32[]{:S(2)}) collective-permute-start(f32[2,40,128]{2,1,0:T(8,128)S(1)} %pad_maximum_fusion), channel_id=1, source_target_pairs={{0,2},{1,3},{2,0},{3,1},{4,6},{5,7},{6,4},{7,5},{8,10},{9,11},{10,... | collective-permute-start | bytes 122888 | tf_op jit(solution)/shard_map/ppermute | solution.py:619
  84.4 5.3 %collective-permute-start.14 = (f32[2,40,128]{2,1,0:T(8,128)S(1)}, f32[2,40,128]{2,1,0:T(8,128)S(1)}, u32[]{:S(2)}, u32[]{:S(2)}) collective-permute-start(f32[2,40,128]{2,1,0:T(8,128)S(1)} %pad_maximum_fusion.1), channel_id=1, source_target_pairs={{0,24},{1,25},{2,26},{3,27},{4,28},{5,29},{6,30},{7,31},{8,16},{9,... | collective-permute-start | bytes 122888 | tf_op jit(solution)/shard_map/ppermute | solution.py:619
  84.5 5.6 %collective-permute-start.13 = (f32[2,40,128]{2,1,0:T(8,128)S(1)}, f32[2,40,128]{2,1,0:T(8,128)S(1)}, u32[]{:S(2)}, u32[]{:S(2)}) collective-permute-start(f32[2,40,128]{2,1,0:T(8,128)S(1)} %pad_maximum_fusion.1), channel_id=1, source_target_pairs={{0,16},{1,17},{2,18},{3,19},{4,20},{5,21},{6,22},{7,23},{8,24},{9,... | collective-permute-start | bytes 122888 | tf_op jit(solution)/shard_map/ppermute | solution.py:619
  84.6 6.4 %collective-permute-start.12 = (f32[2,40,128]{2,1,0:T(8,128)S(1)}, f32[2,40,128]{2,1,0:T(8,128)S(1)}, u32[]{:S(2)}, u32[]{:S(2)}) collective-permute-start(f32[2,40,128]{2,1,0:T(8,128)S(1)} %pad_maximum_fusion.1), channel_id=1, source_target_pairs={{0,8},{1,9},{2,10},{3,11},{4,12},{5,13},{6,14},{7,15},{8,0},{9,1},... | collective-permute-start | bytes 122888 | tf_op jit(solution)/shard_map/ppermute | solution.py:619
  91.0 7.4 %collective-permute-start.17 = (f32[2,40,128]{2,1,0:T(8,128)S(1)}, f32[2,40,128]{2,1,0:T(8,128)S(1)}, u32[]{:S(2)}, u32[]{:S(2)}) collective-permute-start(f32[2,40,128]{2,1,0:T(8,128)S(1)} %pad_maximum_fusion.2), channel_id=1, source_target_pairs={{0,96},{1,97},{2,98},{3,99},{4,100},{5,101},{6,102},{7,103},{8,104... | collective-permute-start | bytes 122888 | tf_op jit(solution)/shard_map/ppermute | solution.py:619
  96.3 5.5 %collective-permute-start.16 = (f32[2,40,128]{2,1,0:T(8,128)S(1)}, f32[2,40,128]{2,1,0:T(8,128)S(1)}, u32[]{:S(2)}, u32[]{:S(2)}) collective-permute-start(f32[2,40,128]{2,1,0:T(8,128)S(1)} %pad_maximum_fusion.2), channel_id=1, source_target_pairs={{0,64},{1,65},{2,66},{3,67},{4,68},{5,69},{6,70},{7,71},{8,72},{9,... | collective-permute-start | bytes 122888 | tf_op jit(solution)/shard_map/ppermute | solution.py:619
  96.3 5.5 %collective-permute-start.15 = (f32[2,40,128]{2,1,0:T(8,128)S(1)}, f32[2,40,128]{2,1,0:T(8,128)S(1)}, u32[]{:S(2)}, u32[]{:S(2)}) collective-permute-start(f32[2,40,128]{2,1,0:T(8,128)S(1)} %pad_maximum_fusion.2), channel_id=1, source_target_pairs={{0,32},{1,33},{2,34},{3,35},{4,36},{5,37},{6,38},{7,39},{8,40},{9,... | collective-permute-start | bytes 122888 | tf_op jit(solution)/shard_map/ppermute | solution.py:619
  101.9 1.5 %collective-permute-start.18 = (f32[2,40,128]{2,1,0:T(8,128)S(1)}, f32[2,40,128]{2,1,0:T(8,128)S(1)}, u32[]{:S(2)}, u32[]{:S(2)}) collective-permute-start(f32[2,40,128]{2,1,0:T(8,128)S(1)} %pad_maximum_fusion.3), channel_id=1, source_target_pairs={{0,1},{1,0},{2,3},{3,2},{4,5},{5,4},{6,7},{7,6},{8,9},{9,8},{10,11... | collective-permute-start | bytes 122888 | tf_op jit(solution)/shard_map/ppermute | solution.py:622
  (1 other events, 0.7 us)

commit v6 on v3

--- a/solution.py
+++ b/solution.py
@@ -425,6 +425,24 @@
     return jnp.concatenate(upper, axis=0), jnp.concatenate(lower_inv, axis=0)
 
 
+def eliminate_by_steps(G):
+    ri = lax.broadcasted_iota(jnp.int32, (W, W), 0)
+    ci = lax.broadcasted_iota(jnp.int32, (W, W), 1)
+
+    def step(j, state):
+        A, B = state
+        row = jnp.sum(jnp.where(ri == j, A, 0.0), axis=0, keepdims=True)
+        brow = jnp.sum(jnp.where(ri == j, B, 0.0), axis=0, keepdims=True)
+        col = jnp.sum(jnp.where(ci == j, A, 0.0), axis=1, keepdims=True)
+        pivot = jnp.sum(jnp.where(ci[0:1] == j, row, 0.0), axis=1, keepdims=True)
+        times = jnp.where(ri > j, col / pivot, 0.0)
+        return A - times * row, B - times * brow
+
+    A, B = lax.fori_loop(0, W, step, (G, (ri == ci).astype(F32)))
+    s = 1.0 / jnp.sqrt(jnp.sum(jnp.where(ri == ci, A, 0.0), axis=1, keepdims=True))
+    return jnp.where(ci >= ri, A * s, 0.0), jnp.where(ci <= ri, B * s, 0.0)
+
+
 def dot(a, b, ca, cb):
     return lax.dot_general(a, b, (((ca,), (cb,)), ((), ())), preferred_element_type=F32)
 
@@ -471,19 +489,23 @@
 
     off = mm3(mm3(linv, rest), linv, 1, 1)
     defect = eye - mm6(linv, upper, 1, 1)
-    close = jnp.sum(off * off) < 1e-5
+    close = jnp.sum(off * off) < 1e-3
 
     @pl.when(close)
     def _():
         x = half_lower(off)
-        z = mm1(x, x - defect) + defect
-        x = half_lower(off - mm1(x, x, 1, 1))
-        inv_ref[...] = linv + mm3(z - x, linv)
+        for _ in range(3):
+            x = half_lower(off - mm1(x, x, 1, 1))
+        first_order = defect - x
+        z = first_order
+        for _ in range(3):
+            z = first_order - mm1(x, z)
+        inv_ref[...] = linv + mm3(z, linv)
         factor_ref[...] = upper + mm3(x, upper, 0, 0)
 
     @pl.when(jnp.logical_not(close))
     def _():
-        u2, l2 = eliminate(eye + off)
+        u2, l2 = eliminate_by_steps(eye + off)
         factor = mm6(u2, upper)
         inv = mm6(l2, linv)
         inv_ref[...] = inv + mm6(eye - mm6(inv, factor, 1, 1), inv)

time: 116 us -> 111 us (0.957)
  Pallas kernels: 66.9 us -> 63.1 us
    pallas_call x1, Pallas kernels: 11.8 us -> 7.36 us  [factors(): pl.pallas_call(functools.partial(factor_kernel, float(total)), in_specs=[...]
  transfers between devices with their start and end apart: 19 -> 19, of which waited for: 12 -> 12; matrix products, arithmetic and copies ran while one was open for 0% -> 0% of each run, Pallas kernels for 32% -> 34%
where the time goes in v6:
time: 111 us; the launch traced here: 110 us
  Pallas kernels  63.1 us (57%)
  starting transfers between devices  31.5 us (28%)
  waiting for transfers between devices  12.8 us (12%)
    pallas_call x4, Pallas kernels, run_phase(): pl.pallas_call(functools.partial(phase_kernel, which, group, places, acc...  25.4 us
    ppermute x8, starting transfers between devices, exchange(): move(x, perm=perm)  17.9 us
    ppermute x9, starting transfers between devices, shards(): move(mine, perm=[(i, i ^ by << shift) for i in range(count)])  13.4 us
    pallas_call x1, Pallas kernels, convert(): pl.pallas_call(convert_kernel, in_specs=[SM, SM, ANY], out_specs=[VM, SM,...  11.5 us
    ppermute x9, waiting for transfers between devices, shards(): move(mine, perm=[(i, i ^ by << shift) for i in range(count)])  9.38 us
    pallas_call x1, Pallas kernels, finish_one(): pl.pallas_call(finish_one_kernel, in_specs=[SM] * 4 + [VM] * 6, out_specs...  8.56 us
    pallas_call x1, Pallas kernels, factors(): pl.pallas_call(functools.partial(factor_kernel, float(total)), in_specs=[...  7.36 us
    pallas_call x1, Pallas kernels, finish_two(): pl.pallas_call(finish_two_kernel, in_specs=[SM] * 3 + [VM] * 5, out_specs...  6.28 us
  transfers between devices with their start and end apart: 19, of which 12 were waited for; matrix products, arithmetic and copies ran while one was open for 0% of the time, Pallas kernels for 34%

profile of v6, /device:TPU:0, one launch (start us, length us, event | category | flops | bytes accessed | tf_op | source)
XLA Modules:
  0.0 109.6 jit_solution(9325447547375574716)
XLA Ops:
  1.7 2.1 %pack.1 = (f32[16,128,128]{2,1,0:T(8,128)S(1)}, f32[8,128,128]{2,1,0:T(8,128)S(1)}, f32[8,128,128]{2,1,0:T(8,128)S(1)}, f32[8,128,128]{2,1,0:T(8,128)S(1)}, f32[8,128,128]{2,1,0:T(8,128)S(1)}) custom-call(s32[10]{0:T(128)S(1)} %stack.59.info_ref, s32[4,8]{1,0:T(4,128)S(1)} %dynamic-slice_reduce_fusion.lists_ref.mine_ref, f32[16,128,128]{2,1,0:T(8,128)} %bitcast.12), custom_call_target="tpu_custom_call" | custom-call | tf_op jit(solution)/shard_map/pack/pallas_call | solution.py:188
  3.8 2.1 %collective-permute-start = (f32[8,128,128]{2,1,0:T(8,128)S(1)}, f32[8,128,128]{2,1,0:T(8,128)S(1)}, u32[]{:S(2)}, u32[]{:S(2)}) collective-permute-start(f32[8,128,128]{2,1,0:T(8,128)S(1)} %get-tuple-element.23), channel_id=1, source_target_pairs={{0,2},{1,3},{2,0},{3,1},{4,6},{5,7},{6,4},{7,5},{8,10},{9,11},{10,... | collective-permute-start | bytes 1572872 | tf_op jit(solution)/shard_map/ppermute | solution.py:578
  5.9 7.2 %collective-permute-start.1 = (f32[8,128,128]{2,1,0:T(8,128)S(1)}, f32[8,128,128]{2,1,0:T(8,128)S(1)}, u32[]{:S(2)}, u32[]{:S(2)}) collective-permute-start(f32[8,128,128]{2,1,0:T(8,128)S(1)} %get-tuple-element.24), channel_id=1, source_target_pairs={{0,126},{1,127},{2,4},{3,5},{4,2},{5,3},{6,8},{7,9},{8,6},{9,7},{1... | collective-permute-start | bytes 1572872 | tf_op jit(solution)/shard_map/ppermute | solution.py:578
  13.1 11.5 %convert.1 = (bf16[320,384,128]{2,1,0:T(8,128)(2,1)S(1)}, s32[5,368]{1,0:T(8,128)}, s32[5]{0:T(128)}) custom-call(s32[16,20]{1,0:T(8,128)} %cols_ref.1, s32[10]{0:T(128)} %copy-done.5, f32[320,128,128]{2,1,0:T(8,128)} %bitcast.11), custom_call_target="tpu_custom_call" | custom-call | flops 2684354560 | bytes 20971520 | tf_op jit(solution)/shard_map/convert/pallas_call | solution.py:150
  24.6 8.3 %phase_0.2.acc_in = f32[16,128,128]{2,1,0:T(8,128)S(1)} custom-call(s32[5,368]{1,0:T(8,128)} %get-tuple-element.20.list_ref, s32[5]{0:T(128)} %get-tuple-element.21.cnt_ref, bf16[320,384,128]{2,1,0:T(8,128)(2,1)S(1)} %get-tuple-element.22.hs_ref, f32[16,128,128]{2,1,0:T(8,128)S(1)} %get-tuple-element.26.refs_0_.v_ref, ...), custom_call_target="tpu_custom_call" | custom-call | flops 2684354560 | bytes 4194304 | tf_op jit(solution)/shard_map/phase_0/pallas_call | solution.py:217
  33.0 8.6 %finish_one.1 = (f32[16,128,128]{2,1,0:T(8,128)S(1)}, f32[8,128,128]{2,1,0:T(8,128)S(1)}, f32[8,128,128]{2,1,0:T(8,128)S(1)}, f32[8,128,128]{2,1,0:T(8,128)S(1)}, f32[8,128,128]{2,1,0:T(8,128)S(1)}) custom-call(s32[5,368]{1,0:T(8,128)} %get-tuple-element.20.list_ref, s32[5]{0:T(128)} %get-tuple-element.21.cnt_ref, ...), custom_call_target="tpu_custom_call", output_to_operand_aliasing={{0}: (9, {})} | custom-call | flops 4026531840 | bytes 8388608 | tf_op jit(solution)/shard_map/finish_one/pallas_call | solution.py:244
  41.7 1.6 %collective-permute-start.6 = (f32[8,128,128]{2,1,0:T(8,128)S(1)}, f32[8,128,128]{2,1,0:T(8,128)S(1)}, u32[]{:S(2)}, u32[]{:S(2)}) collective-permute-start(f32[8,128,128]{2,1,0:T(8,128)S(1)} %get-tuple-element.31), channel_id=1, source_target_pairs={{0,2},{1,3},{2,0},{3,1},{4,6},{5,7},{6,4},{7,5},{8,10},{9,11},{10,... | collective-permute-start | bytes 1572872 | tf_op jit(solution)/shard_map/ppermute | solution.py:578
  43.3 6.1 %collective-permute-start.5 = (f32[8,128,128]{2,1,0:T(8,128)S(1)}, f32[8,128,128]{2,1,0:T(8,128)S(1)}, u32[]{:S(2)}, u32[]{:S(2)}) collective-permute-start(f32[8,128,128]{2,1,0:T(8,128)S(1)} %get-tuple-element.30), channel_id=1, source_target_pairs={{0,126},{1,127},{2,4},{3,5},{4,2},{5,3},{6,8},{7,9},{8,6},{9,7},{1... | collective-permute-start | bytes 1572872 | tf_op jit(solution)/shard_map/ppermute | solution.py:578
  50.2 8.3 %phase_0.3.refs_1_ = f32[16,128,128]{2,1,0:T(8,128)S(1)} custom-call(s32[5,368]{1,0:T(8,128)} %get-tuple-element.20.list_ref, s32[5]{0:T(128)} %get-tuple-element.21.cnt_ref, bf16[320,384,128]{2,1,0:T(8,128)(2,1)S(1)} %get-tuple-element.22.hs_ref, f32[16,128,128]{2,1,0:T(8,128)S(1)} %get-tuple-element.29.refs_0_.first_ref, ...), custom_call_target="tpu_custom_call" | custom-call | flops 2684354560 | bytes 4194304 | tf_op jit(solution)/shard_map/phase_0/pallas_call | solution.py:217
  58.6 4.0 %phase_1.1.refs_1_ = f32[16,128,128]{2,1,0:T(8,128)S(1)} custom-call(s32[5,368]{1,0:T(8,128)} %get-tuple-element.20.list_ref, s32[5]{0:T(128)} %get-tuple-element.21.cnt_ref, bf16[320,384,128]{2,1,0:T(8,128)(2,1)S(1)} %get-tuple-element.22.hs_ref, f32[8,128,128]{2,1,0:T(8,128)S(1)} %collective-permute-done.6.refs_0_, ...), custom_call_target="tpu_custom_call", output_to_operand_aliasing={{}: (4, {})} | custom-call | flops 1342177280 | bytes 4194304 | tf_op jit(solution)/shard_map/phase_1/pallas_call | solution.py:217
  63.5 4.7 %phase_2.1.acc_in = f32[16,128,128]{2,1,0:T(8,128)S(1)} custom-call(s32[5,368]{1,0:T(8,128)} %get-tuple-element.20.list_ref, s32[5]{0:T(128)} %get-tuple-element.21.cnt_ref, bf16[320,384,128]{2,1,0:T(8,128)(2,1)S(1)} %get-tuple-element.22.hs_ref, f32[8,128,128]{2,1,0:T(8,128)S(1)} %collective-permute-done.5.refs_0_, ...), custom_call_target="tpu_custom_call", output_to_operand_aliasing={{}: (4, {})} | custom-call | flops 1342177280 | bytes 4194304 | tf_op jit(solution)/shard_map/phase_2/pallas_call | solution.py:217
  68.3 6.3 %finish_two.1 = (f32[16,128,128]{2,1,0:T(8,128)S(1)}, f32[2,40,128]{2,1,0:T(8,128)S(1)}, f32[2,40,128]{2,1,0:T(8,128)S(1)}) custom-call(s32[5,368]{1,0:T(8,128)} %get-tuple-element.20.list_ref, s32[5]{0:T(128)} %get-tuple-element.21.cnt_ref, s32[10]{0:T(128)} %copy-done.5, ...), custom_call_target="tpu_custom_call", output_to_operand_aliasing={{0}: (7, {})} | custom-call | flops 1342177280 | bytes 8388608 | tf_op jit(solution)/shard_map/finish_two/pallas_call | solution.py:371
  74.7 1.2 %collective-permute-done.8 = f32[2,40,128]{2,1,0:T(8,128)S(1)} collective-permute-done((f32[2,40,128]{2,1,0:T(8,128)S(1)}, f32[2,40,128]{2,1,0:T(8,128)S(1)}, u32[]{:S(2)}, u32[]{:S(2)}) %collective-permute-start.8) | collective-permute-done | bytes 40992 | tf_op jit(solution)/shard_map/ppermute | solution.py:592
  76.0 1.8 %collective-permute-start.10 = (f32[2,40,128]{2,1,0:T(8,128)S(1)}, f32[2,40,128]{2,1,0:T(8,128)S(1)}, u32[]{:S(2)}, u32[]{:S(2)}) collective-permute-start(f32[2,40,128]{2,1,0:T(8,128)S(1)} %pad_maximum_fusion), channel_id=1, source_target_pairs={{0,4},{1,5},{2,6},{3,7},{4,0},{5,1},{6,2},{7,3},{8,12},{9,13},{10,... | collective-permute-start | bytes 122888 | tf_op jit(solution)/shard_map/ppermute | solution.py:596
  77.8 2.3 %collective-permute-start.9 = (f32[2,40,128]{2,1,0:T(8,128)S(1)}, f32[2,40,128]{2,1,0:T(8,128)S(1)}, u32[]{:S(2)}, u32[]{:S(2)}) collective-permute-start(f32[2,40,128]{2,1,0:T(8,128)S(1)} %pad_maximum_fusion), channel_id=1, source_target_pairs={{0,2},{1,3},{2,0},{3,1},{4,6},{5,7},{6,4},{7,5},{8,10},{9,11},{10,... | collective-permute-start | bytes 122888 | tf_op jit(solution)/shard_map/ppermute | solution.py:596
  80.1 1.3 %collective-permute-done.11 = f32[2,40,128]{2,1,0:T(8,128)S(1)} collective-permute-done((f32[2,40,128]{2,1,0:T(8,128)S(1)}, f32[2,40,128]{2,1,0:T(8,128)S(1)}, u32[]{:S(2)}, u32[]{:S(2)}) %collective-permute-start.11) | collective-permute-done | bytes 40992 | tf_op jit(solution)/shard_map/ppermute | solution.py:596
  82.7 4.0 %collective-permute-start.12 = (f32[2,40,128]{2,1,0:T(8,128)S(1)}, f32[2,40,128]{2,1,0:T(8,128)S(1)}, u32[]{:S(2)}, u32[]{:S(2)}) collective-permute-start(f32[2,40,128]{2,1,0:T(8,128)S(1)} %pad_maximum_fusion.1), channel_id=1, source_target_pairs={{0,8},{1,9},{2,10},{3,11},{4,12},{5,13},{6,14},{7,15},{8,0},{9,1},... | collective-permute-start | bytes 122888 | tf_op jit(solution)/shard_map/ppermute | solution.py:596
  86.7 1.1 %collective-permute-done.14 = f32[2,40,128]{2,1,0:T(8,128)S(1)} collective-permute-done((f32[2,40,128]{2,1,0:T(8,128)S(1)}, f32[2,40,128]{2,1,0:T(8,128)S(1)}, u32[]{:S(2)}, u32[]{:S(2)}) %collective-permute-start.14) | collective-permute-done | bytes 40992 | tf_op jit(solution)/shard_map/ppermute | solution.py:596
  89.2 4.1 %collective-permute-start.17 = (f32[2,40,128]{2,1,0:T(8,128)S(1)}, f32[2,40,128]{2,1,0:T(8,128)S(1)}, u32[]{:S(2)}, u32[]{:S(2)}) collective-permute-start(f32[2,40,128]{2,1,0:T(8,128)S(1)} %pad_maximum_fusion.2), channel_id=1, source_target_pairs={{0,96},{1,97},{2,98},{3,99},{4,100},{5,101},{6,102},{7,103},{8,104... | collective-permute-start | bytes 122888 | tf_op jit(solution)/shard_map/ppermute | solution.py:596
  94.3 1.2 %collective-permute-done.17 = f32[2,40,128]{2,1,0:T(8,128)S(1)} collective-permute-done((f32[2,40,128]{2,1,0:T(8,128)S(1)}, f32[2,40,128]{2,1,0:T(8,128)S(1)}, u32[]{:S(2)}, u32[]{:S(2)}) %collective-permute-start.17) | collective-permute-done | bytes 40992 | tf_op jit(solution)/shard_map/ppermute | solution.py:596
  95.5 3.3 %collective-permute-done.16 = f32[2,40,128]{2,1,0:T(8,128)S(1)} collective-permute-done((f32[2,40,128]{2,1,0:T(8,128)S(1)}, f32[2,40,128]{2,1,0:T(8,128)S(1)}, u32[]{:S(2)}, u32[]{:S(2)}) %collective-permute-start.16) | collective-permute-done | bytes 40992 | tf_op jit(solution)/shard_map/ppermute | solution.py:596
  99.0 1.2 %collective-permute-done.18 = f32[2,40,128]{2,1,0:T(8,128)S(1)} collective-permute-done((f32[2,40,128]{2,1,0:T(8,128)S(1)}, f32[2,40,128]{2,1,0:T(8,128)S(1)}, u32[]{:S(2)}, u32[]{:S(2)}) %collective-permute-start.18) | collective-permute-done | bytes 40992 | tf_op jit(solution)/shard_map/ppermute | solution.py:599
  100.2 7.4 %factors.1 = (f32[128,128]{1,0:T(8,128)S(1)}, f32[128,128]{1,0:T(8,128)}) custom-call(f32[2,40,128]{2,1,0:T(8,128)S(1)} %get-tuple-element.53.zero_ref, f32[2,40,128]{2,1,0:T(8,128)S(1)} %get-tuple-element.52.one_ref), custom_call_target="tpu_custom_call" | custom-call | tf_op jit(solution)/shard_map/factors/pallas_call | solution.py:516
  107.6 2.0 %basis.1 = f32[2048,128]{1,0:T(8,128)} custom-call(f32[16,128,128]{2,1,0:T(8,128)S(1)} %get-tuple-element.33.s_ref, f32[128,128]{1,0:T(8,128)S(1)} %get-tuple-element.36.t_ref), custom_call_target="tpu_custom_call" | custom-call | tf_op jit(solution)/shard_map/basis/pallas_call | solution.py:532
  (50 shorter events, 6.9 us)
Async XLA Ops:
  1.6 31.4 %copy-start.4 = (s32[4,8]{1,0:T(4,128)}, s32[4,8]{1,0:T(4,128)S(1)}, u32[]{:S(2)}) copy-start(s32[4,8]{1,0:T(4,128)S(1)} %dynamic-slice_reduce_fusion.lists_ref.mine_ref) | copy-start | bytes 388
  1.7 11.4 %copy-start.5 = (s32[10]{0:T(128)}, s32[10]{0:T(128)S(1)}, u32[]{:S(2)}) copy-start(s32[10]{0:T(128)S(1)} %stack.59.info_ref) | copy-start | bytes 124
  3.7 37.8 %copy-start.2 = (f32[16,128,128]{2,1,0:T(8,128)}, f32[16,128,128]{2,1,0:T(8,128)S(1)}, u32[]{:S(2)}) copy-start(f32[16,128,128]{2,1,0:T(8,128)S(1)} %get-tuple-element.26.refs_0_.v_ref) | copy-start | bytes 3145732
  3.7 20.9 %collective-permute-start.3 = (f32[8,128,128]{2,1,0:T(8,128)S(1)}, f32[8,128,128]{2,1,0:T(8,128)S(1)}, u32[]{:S(2)}, u32[]{:S(2)}) collective-permute-start(f32[8,128,128]{2,1,0:T(8,128)S(1)} %get-tuple-element.27), channel_id=1, source_target_pairs={{0,1},{1,0},{2,3},{3,2},{4,5},{5,4},{6,7},{7,6},{8,9},{9,8},{10,11... | collective-permute-start | bytes 1572872 | tf_op jit(solution)/shard_map/ppermute | solution.py:578
  3.8 29.1 %collective-permute-start = (f32[8,128,128]{2,1,0:T(8,128)S(1)}, f32[8,128,128]{2,1,0:T(8,128)S(1)}, u32[]{:S(2)}, u32[]{:S(2)}) collective-permute-start(f32[8,128,128]{2,1,0:T(8,128)S(1)} %get-tuple-element.23), channel_id=1, source_target_pairs={{0,2},{1,3},{2,0},{3,1},{4,6},{5,7},{6,4},{7,5},{8,10},{9,11},{10,... | collective-permute-start | bytes 1572872 | tf_op jit(solution)/shard_map/ppermute | solution.py:578
  5.9 27.1 %collective-permute-start.1 = (f32[8,128,128]{2,1,0:T(8,128)S(1)}, f32[8,128,128]{2,1,0:T(8,128)S(1)}, u32[]{:S(2)}, u32[]{:S(2)}) collective-permute-start(f32[8,128,128]{2,1,0:T(8,128)S(1)} %get-tuple-element.24), channel_id=1, source_target_pairs={{0,126},{1,127},{2,4},{3,5},{4,2},{5,3},{6,8},{7,9},{8,6},{9,7},{1... | collective-permute-start | bytes 1572872 | tf_op jit(solution)/shard_map/ppermute | solution.py:578
  13.1 19.9 %collective-permute-start.2 = (f32[8,128,128]{2,1,0:T(8,128)S(1)}, f32[8,128,128]{2,1,0:T(8,128)S(1)}, u32[]{:S(2)}, u32[]{:S(2)}) collective-permute-start(f32[8,128,128]{2,1,0:T(8,128)S(1)} %get-tuple-element.25), channel_id=1, source_target_pairs={{0,127},{1,2},{2,1},{3,4},{4,3},{5,6},{6,5},{7,8},{8,7},{9,10},{10... | collective-permute-start | bytes 1572872 | tf_op jit(solution)/shard_map/ppermute | solution.py:578
  41.6 8.6 %collective-permute-start.7 = (f32[8,128,128]{2,1,0:T(8,128)S(1)}, f32[8,128,128]{2,1,0:T(8,128)S(1)}, u32[]{:S(2)}, u32[]{:S(2)}) collective-permute-start(f32[8,128,128]{2,1,0:T(8,128)S(1)} %get-tuple-element.32), channel_id=1, source_target_pairs={{0,1},{1,0},{2,3},{3,2},{4,5},{5,4},{6,7},{7,6},{8,9},{9,8},{10,11... | collective-permute-start | bytes 1572872 | tf_op jit(solution)/shard_map/ppermute | solution.py:578
  41.7 16.9 %collective-permute-start.6 = (f32[8,128,128]{2,1,0:T(8,128)S(1)}, f32[8,128,128]{2,1,0:T(8,128)S(1)}, u32[]{:S(2)}, u32[]{:S(2)}) collective-permute-start(f32[8,128,128]{2,1,0:T(8,128)S(1)} %get-tuple-element.31), channel_id=1, source_target_pairs={{0,2},{1,3},{2,0},{3,1},{4,6},{5,7},{6,4},{7,5},{8,10},{9,11},{10,... | collective-permute-start | bytes 1572872 | tf_op jit(solution)/shard_map/ppermute | solution.py:578
  43.3 20.2 %collective-permute-start.5 = (f32[8,128,128]{2,1,0:T(8,128)S(1)}, f32[8,128,128]{2,1,0:T(8,128)S(1)}, u32[]{:S(2)}, u32[]{:S(2)}) collective-permute-start(f32[8,128,128]{2,1,0:T(8,128)S(1)} %get-tuple-element.30), channel_id=1, source_target_pairs={{0,126},{1,127},{2,4},{3,5},{4,2},{5,3},{6,8},{7,9},{8,6},{9,7},{1... | collective-permute-start | bytes 1572872 | tf_op jit(solution)/shard_map/ppermute | solution.py:578
  49.4 18.9 %collective-permute-start.4 = (f32[8,128,128]{2,1,0:T(8,128)S(1)}, f32[8,128,128]{2,1,0:T(8,128)S(1)}, u32[]{:S(2)}, u32[]{:S(2)}) collective-permute-start(f32[8,128,128]{2,1,0:T(8,128)S(1)} %get-tuple-element.28), channel_id=1, source_target_pairs={{0,127},{1,2},{2,1},{3,4},{4,3},{5,6},{6,5},{7,8},{8,7},{9,10},{10... | collective-permute-start | bytes 1572872 | tf_op jit(solution)/shard_map/ppermute | solution.py:578
  58.5 9.8 %copy-start.3 = (f32[16,128,128]{2,1,0:T(8,128)S(1)}, f32[16,128,128]{2,1,0:T(8,128)}, u32[]{:S(2)}) copy-start(f32[16,128,128]{2,1,0:T(8,128)} %copy-done.2) | copy-start | bytes 3145732
  58.5 51.0 %copy-start.1 = (s32[128,4,8]{0,2,1:T(8,128)S(1)}, s32[128,4,8]{0,2,1:T(8,128)}, u32[]{:S(2)}) copy-start(s32[128,4,8]{0,2,1:T(8,128)} %param.7) | copy-start | bytes 49156
  74.6 1.3 %collective-permute-start.8 = (f32[2,40,128]{2,1,0:T(8,128)S(1)}, f32[2,40,128]{2,1,0:T(8,128)S(1)}, u32[]{:S(2)}, u32[]{:S(2)}) collective-permute-start(f32[2,40,128]{2,1,0:T(8,128)S(1)} %get-tuple-element.35), channel_id=1, source_target_pairs={{0,1},{1,0},{2,3},{3,2},{4,5},{5,4},{6,7},{7,6},{8,9},{9,8},{10,11... | collective-permute-start | bytes 122888 | tf_op jit(solution)/shard_map/ppermute | solution.py:592
  75.9 5.5 %collective-permute-start.11 = (f32[2,40,128]{2,1,0:T(8,128)S(1)}, f32[2,40,128]{2,1,0:T(8,128)S(1)}, u32[]{:S(2)}, u32[]{:S(2)}) collective-permute-start(f32[2,40,128]{2,1,0:T(8,128)S(1)} %pad_maximum_fusion), channel_id=1, source_target_pairs={{0,6},{1,7},{2,4},{3,5},{4,2},{5,3},{6,0},{7,1},{8,14},{9,15},{10,... | collective-permute-start | bytes 122888 | tf_op jit(solution)/shard_map/ppermute | solution.py:596
  76.0 6.0 %collective-permute-start.10 = (f32[2,40,128]{2,1,0:T(8,128)S(1)}, f32[2,40,128]{2,1,0:T(8,128)S(1)}, u32[]{:S(2)}, u32[]{:S(2)}) collective-permute-start(f32[2,40,128]{2,1,0:T(8,128)S(1)} %pad_maximum_fusion), channel_id=1, source_target_pairs={{0,4},{1,5},{2,6},{3,7},{4,0},{5,1},{6,2},{7,3},{8,12},{9,13},{10,... | collective-permute-start | bytes 122888 | tf_op jit(solution)/shard_map/ppermute | solution.py:596
  77.8 4.7 %collective-permute-start.9 = (f32[2,40,128]{2,1,0:T(8,128)S(1)}, f32[2,40,128]{2,1,0:T(8,128)S(1)}, u32[]{:S(2)}, u32[]{:S(2)}) collective-permute-start(f32[2,40,128]{2,1,0:T(8,128)S(1)} %pad_maximum_fusion), channel_id=1, source_target_pairs={{0,2},{1,3},{2,0},{3,1},{4,6},{5,7},{6,4},{7,5},{8,10},{9,11},{10,... | collective-permute-start | bytes 122888 | tf_op jit(solution)/shard_map/ppermute | solution.py:596
  82.5 5.3 %collective-permute-start.14 = (f32[2,40,128]{2,1,0:T(8,128)S(1)}, f32[2,40,128]{2,1,0:T(8,128)S(1)}, u32[]{:S(2)}, u32[]{:S(2)}) collective-permute-start(f32[2,40,128]{2,1,0:T(8,128)S(1)} %pad_maximum_fusion.1), channel_id=1, source_target_pairs={{0,24},{1,25},{2,26},{3,27},{4,28},{5,29},{6,30},{7,31},{8,16},{9,... | collective-permute-start | bytes 122888 | tf_op jit(solution)/shard_map/ppermute | solution.py:596
  82.6 5.6 %collective-permute-start.13 = (f32[2,40,128]{2,1,0:T(8,128)S(1)}, f32[2,40,128]{2,1,0:T(8,128)S(1)}, u32[]{:S(2)}, u32[]{:S(2)}) collective-permute-start(f32[2,40,128]{2,1,0:T(8,128)S(1)} %pad_maximum_fusion.1), channel_id=1, source_target_pairs={{0,16},{1,17},{2,18},{3,19},{4,20},{5,21},{6,22},{7,23},{8,24},{9,... | collective-permute-start | bytes 122888 | tf_op jit(solution)/shard_map/ppermute | solution.py:596
  82.7 6.4 %collective-permute-start.12 = (f32[2,40,128]{2,1,0:T(8,128)S(1)}, f32[2,40,128]{2,1,0:T(8,128)S(1)}, u32[]{:S(2)}, u32[]{:S(2)}) collective-permute-start(f32[2,40,128]{2,1,0:T(8,128)S(1)} %pad_maximum_fusion.1), channel_id=1, source_target_pairs={{0,8},{1,9},{2,10},{3,11},{4,12},{5,13},{6,14},{7,15},{8,0},{9,1},... | collective-permute-start | bytes 122888 | tf_op jit(solution)/shard_map/ppermute | solution.py:596
  89.2 6.3 %collective-permute-start.17 = (f32[2,40,128]{2,1,0:T(8,128)S(1)}, f32[2,40,128]{2,1,0:T(8,128)S(1)}, u32[]{:S(2)}, u32[]{:S(2)}) collective-permute-start(f32[2,40,128]{2,1,0:T(8,128)S(1)} %pad_maximum_fusion.2), channel_id=1, source_target_pairs={{0,96},{1,97},{2,98},{3,99},{4,100},{5,101},{6,102},{7,103},{8,104... | collective-permute-start | bytes 122888 | tf_op jit(solution)/shard_map/ppermute | solution.py:596
  93.3 5.5 %collective-permute-start.16 = (f32[2,40,128]{2,1,0:T(8,128)S(1)}, f32[2,40,128]{2,1,0:T(8,128)S(1)}, u32[]{:S(2)}, u32[]{:S(2)}) collective-permute-start(f32[2,40,128]{2,1,0:T(8,128)S(1)} %pad_maximum_fusion.2), channel_id=1, source_target_pairs={{0,64},{1,65},{2,66},{3,67},{4,68},{5,69},{6,70},{7,71},{8,72},{9,... | collective-permute-start | bytes 122888 | tf_op jit(solution)/shard_map/ppermute | solution.py:596
  93.3 5.5 %collective-permute-start.15 = (f32[2,40,128]{2,1,0:T(8,128)S(1)}, f32[2,40,128]{2,1,0:T(8,128)S(1)}, u32[]{:S(2)}, u32[]{:S(2)}) collective-permute-start(f32[2,40,128]{2,1,0:T(8,128)S(1)} %pad_maximum_fusion.2), channel_id=1, source_target_pairs={{0,32},{1,33},{2,34},{3,35},{4,36},{5,37},{6,38},{7,39},{8,40},{9,... | collective-permute-start | bytes 122888 | tf_op jit(solution)/shard_map/ppermute | solution.py:596
  98.9 1.3 %collective-permute-start.18 = (f32[2,40,128]{2,1,0:T(8,128)S(1)}, f32[2,40,128]{2,1,0:T(8,128)S(1)}, u32[]{:S(2)}, u32[]{:S(2)}) collective-permute-start(f32[2,40,128]{2,1,0:T(8,128)S(1)} %pad_maximum_fusion.3), channel_id=1, source_target_pairs={{0,1},{1,0},{2,3},{3,2},{4,5},{5,4},{6,7},{7,6},{8,9},{9,8},{10,11... | collective-permute-start | bytes 122888 | tf_op jit(solution)/shard_map/ppermute | solution.py:599
  (1 other events, 0.7 us)
